TPU v7x, 256 devices: a whole 4x4x8 slice. The times are simulated.
256 devices in a mesh: chord: 16 (over z_hi, x), span: 16 (over y, z_lo, core).
Axes of the slice: x: 4, y: 4, z: 8 (z_hi: 4, z_lo: 2; z = z_hi * 2 + z_lo), core: 2. Of those that a mesh axis runs over, the one named last changes fastest.
Arguments:
- adjoint: float32 [6, 32, 128, 256], P(None, 'chord', 'span'), may hold values from -6 to 6
- source: float32 [6, 32, 128, 256], P(None, 'chord', 'span'), may hold values from -24 to 24
- diag_block: bfloat16 [6, 6, 32, 128, 256], P(None, None, 'chord', 'span'), as said below
- couplings: bfloat16 [6, 6, 6, 32, 128, 256], P(None, None, None, 'chord', 'span'), may hold values from -1.1953125 to 1.1953125
- line_inverse: bfloat16 [6, 6, 2, 32, 128, 256], P(None, None, None, 'chord', 'span')
- partner: int32 [32], P('chord'), may hold values from -1 to 31, as said below
- codes: int32 [32, 128], P('chord', 'span'), may hold values from 0 to 1
Outputs:
- adjoint_out: float32 [6, 32, 128, 256], P(None, 'chord', 'span')
- residual: float32 [6, 32, 128, 256], P(None, 'chord', 'span')
Inputs may be any that keep to these rules, and one draw needn't show every extreme that they name: partner[i] is either -1 or 31 - i; partner[i] >= 0 exactly when partner[31 - i] >= 0; partner[0] >= 0. The diagonal entries of diag_block lie in 3 to 9.
All inputs are finite; a program needn't handle non-finite values.
Results may differ from a plain program's by a relative error of at most 0.0006.
Values may be sent and summed in bfloat16 or wider, within the bound.
No kernel may reach another device: no remote copies, remote signals or barrier semaphores. Data moves between devices by JAX's collectives and lax.ppermute only.
A program may use at most 64 MiB of HBM per device.

v0:
```python
import jax
import jax.numpy as jnp
from jax import lax
from jax.sharding import PartitionSpec as P

SWEEPS = 6


def padded(x, sides, width):
    for axis, dim in sides:
        count, length = (lax.axis_size(axis), x.shape[dim])
        up = [(i, (i + 1) % count) for i in range(count - 1)]
        down = [(j, i) for i, j in up]
        last = lax.slice_in_dim(x, length - width, length, axis=dim)
        initial = lax.slice_in_dim(x, 0, width, axis=dim)
        before = lax.ppermute(last, axis, up)
        after = lax.ppermute(initial, axis, down)
        x = jnp.concatenate([before, x, after], axis=dim)
    return x


def block_product(blocks, field):
    return jnp.einsum(
        "abcsn,acsn->bcsn", blocks.astype(jnp.float32), field, precision=lax.Precision.HIGHEST
    )


def shift_down(values, dimension):
    padding = [(0, 0)] * values.ndim
    padding[dimension] = (1, 0)
    return jnp.pad(
        lax.slice_in_dim(values, 0, values.shape[dimension] - 1, axis=dimension), padding
    )


def shift_up(values, dimension):
    padding = [(0, 0)] * values.ndim
    padding[dimension] = (0, 1)
    return jnp.pad(lax.slice_in_dim(values, 1, values.shape[dimension], axis=dimension), padding)


def wall_keep(partner, codes):
    wall_cell = (partner < 0)[:, None]
    component = jnp.arange(6)[:, None, None]
    velocity = (component >= 1) & (component <= 3)
    dropped = wall_cell[None] & ((component == 5) | velocity & (codes[None] == 0))
    return jnp.where(dropped, 0.0, 1.0).astype(jnp.float32)


def line_update(line_inverse, residual):
    count_state, count_chord, count_span, count_line = residual.shape
    pairs = residual.reshape(count_state, count_chord, count_span, count_line // 2, 2)
    spread = jnp.broadcast_to(
        jnp.moveaxis(pairs, 4, 1)[..., None],
        (count_state, 2, count_chord, count_span, count_line // 2, 2),
    )
    spread = spread.reshape(count_state, 2, count_chord, count_span, count_line)
    return jnp.einsum(
        "abqcsn,bqcsn->acsn",
        line_inverse.astype(jnp.float32),
        spread,
        precision=lax.Precision.HIGHEST,
    )


def per_device(adjoint, source, diag_block, couplings, line_inverse, partner, codes):
    keeping = wall_keep(partner, codes)
    has_partner = partner >= 0
    residual = source
    for repeat in range(SWEEPS):
        applied = block_product(diag_block, adjoint)
        chord_minus = block_product(couplings[0], adjoint)
        chord_plus = block_product(couplings[1], adjoint)
        chord_edges = jnp.concatenate([chord_minus[:, :1], chord_plus[:, -1:]], axis=1)
        chord_padded = padded(chord_edges, (("chord", 1),), 1)
        applied = applied + jnp.concatenate([chord_padded[:, :1], chord_plus[:, :-1]], axis=1)
        applied = applied + jnp.concatenate([chord_minus[:, 1:], chord_padded[:, 3:]], axis=1)
        span_minus = block_product(couplings[2], adjoint)
        span_plus = block_product(couplings[3], adjoint)
        span_edges = jnp.concatenate([span_minus[:, :, :1], span_plus[:, :, -1:]], axis=2)
        span_padded = padded(span_edges, (("span", 2),), 1)
        applied = applied + jnp.concatenate([span_padded[:, :, :1], span_plus[:, :, :-1]], axis=2)
        applied = applied + jnp.concatenate([span_minus[:, :, 1:], span_padded[:, :, 3:]], axis=2)
        normal_minus = block_product(couplings[4], adjoint)
        applied = (
            applied
            + shift_down(block_product(couplings[5], adjoint), 3)
            + shift_up(normal_minus, 3)
        )
        cut_rows = jnp.transpose(normal_minus[:, :, :, 0], (1, 0, 2))
        whole_rows = lax.all_gather(cut_rows, "chord", axis=0, tiled=True)
        arrived = whole_rows[jnp.where(has_partner, partner, 0)]
        arrived = jnp.where(has_partner[:, None, None], arrived, 0.0)
        applied = applied.at[:, :, :, 0].add(jnp.transpose(arrived, (1, 0, 2)))
        residual = source - applied
        residual = residual.at[:, :, :, 0].multiply(keeping)
        adjoint = adjoint + line_update(line_inverse, residual)
    return (adjoint, residual)


def solution(mesh):
    placed = (
        P(None, "chord", "span", None),
        P(None, "chord", "span", None),
        P(None, None, "chord", "span", None),
        P(None, None, None, "chord", "span", None),
        P(None, None, None, "chord", "span", None),
        P("chord"),
        P("chord", "span"),
    )
    return jax.shard_map(
        per_device,
        mesh=mesh,
        in_specs=placed,
        out_specs=(P(None, "chord", "span", None), P(None, "chord", "span", None)),
        check_vma=False,
    )
```

profile of v0, /device:TPU:130, one launch (start us, length us, event | category | flops | bytes accessed | tf_op | source)
XLA Modules:
  0.0 424.4 jit_solution(4417882331074765823)
XLA Ops:
  0.6 2.0 fusion.36
  4.0 3.4 collective-permute-start
  7.5 2.8 collective-permute-start.2
  10.3 2.4 collective-permute-start.1
  12.9 43.4 %all_gather.18 = f32[32,6,8]{2,1,0:T(8,128)S(1)} all-gather(f32[2,6,8]{2,1,0:T(8,128)S(1)} %copy.239), channel_id=1, replica_groups=mesh['chord'=16,'span'=16] {'chord'}, dimensions={0}, use_global_device_ids=true | all-gather | bytes 6528 | tf_op jit(solution)/shard_map/all_gather | solution.py:91
  58.5 2.8 broadcast_in_dim.104
  61.3 2.5 copy.644
  69.7 3.6 collective-permute-start.6
  73.9 3.6 collective-permute-start.5
  77.5 45.6 %all_gather.19 = f32[32,6,8]{2,1,0:T(8,128)} all-gather(f32[2,6,8]{2,1,0:T(8,128)S(1)} %copy.248), channel_id=1, replica_groups=mesh['chord'=16,'span'=16] {'chord'}, dimensions={0}, use_global_device_ids=true | all-gather | bytes 6528 | tf_op jit(solution)/shard_map/all_gather | solution.py:91
  133.1 2.8 broadcast_in_dim.105
  135.9 2.3 copy.646
  144.0 3.6 collective-permute-start.10
  148.3 3.6 collective-permute-start.9
  151.9 46.4 %all_gather.20 = f32[32,6,8]{2,1,0:T(8,128)} all-gather(f32[2,6,8]{2,1,0:T(8,128)S(1)} %copy.257), channel_id=1, replica_groups=mesh['chord'=16,'span'=16] {'chord'}, dimensions={0}, use_global_device_ids=true | all-gather | bytes 6528 | tf_op jit(solution)/shard_map/all_gather | solution.py:91
  208.3 2.8 broadcast_in_dim.106
  211.1 2.3 copy.648
  219.2 3.8 collective-permute-start.14
  223.7 3.6 collective-permute-start.13
  227.3 45.3 %all_gather.21 = f32[32,6,8]{2,1,0:T(8,128)} all-gather(f32[2,6,8]{2,1,0:T(8,128)S(1)} %copy.266), channel_id=1, replica_groups=mesh['chord'=16,'span'=16] {'chord'}, dimensions={0}, use_global_device_ids=true | all-gather | bytes 6528 | tf_op jit(solution)/shard_map/all_gather | solution.py:91
  282.7 2.8 broadcast_in_dim.107
  285.5 2.3 copy.650
  293.6 3.6 collective-permute-start.18
  297.9 3.6 collective-permute-start.17
  301.5 45.8 %all_gather.22 = f32[32,6,8]{2,1,0:T(8,128)} all-gather(f32[2,6,8]{2,1,0:T(8,128)S(1)} %copy.275), channel_id=1, replica_groups=mesh['chord'=16,'span'=16] {'chord'}, dimensions={0}, use_global_device_ids=true | all-gather | bytes 6528 | tf_op jit(solution)/shard_map/all_gather | solution.py:91
  357.4 2.8 broadcast_in_dim.108
  360.2 2.3 copy.652
  366.6 3.0 collective-permute-start.22
  369.6 3.6 collective-permute-start.21
  373.3 42.9 %all_gather.23 = f32[32,6,8]{2,1,0:T(8,128)S(1)} all-gather(f32[2,6,8]{2,1,0:T(8,128)S(1)} %copy.284), channel_id=1, replica_groups=mesh['chord'=16,'span'=16] {'chord'}, dimensions={0}, use_global_device_ids=true | all-gather | bytes 6528 | tf_op jit(solution)/shard_map/all_gather | solution.py:91
  418.5 2.8 broadcast_in_dim.109
  421.3 2.3 copy.654
  (243 shorter events, 75.7 us)
Async XLA Ops:
  2.7 54.9 %copy-start.3 = (f32[6,2,8,256]{3,2,1,0:T(8,128)S(1)}, f32[6,2,8,256]{3,2,1,0:T(8,128)}, u32[]{:S(2)}) copy-start(f32[6,2,8,256]{3,2,1,0:T(8,128)} %param.32) | copy-start | bytes 294916
  2.7 54.6 %collective-permute-start.3 = (f32[6,2,1,256]{3,1,2,0:T(2,128)S(1)}, f32[6,2,1,256]{3,1,2,0:T(2,128)S(1)}, u32[]{:S(2)}, u32[]{:S(2)}) collective-permute-start(f32[6,2,1,256]{3,1,2,0:T(2,128)S(1)} %copy.237), channel_id=1, source_target_pairs={{1,0},{2,1},{3,2},{4,3},{5,4},{6,5},{7,6},{8,7},{9,8},{10,9},{11,1... | collective-permute-start | bytes 36872 | tf_op jit(solution)/shard_map/ppermute | solution.py:17
  4.0 53.3 %collective-permute-start = (f32[6,1,8,256]{3,2,1,0:T(8,128)S(1)}, f32[6,1,8,256]{3,2,1,0:T(8,128)S(1)}, u32[]{:S(2)}, u32[]{:S(2)}) collective-permute-start(f32[6,1,8,256]{3,2,1,0:T(8,128)S(1)} %get-tuple-element.218), channel_id=1, source_target_pairs={{0,16},{16,32},{32,48},{48,64},{64,80},{80,96},{96,112},{112,128},... | collective-permute-start | bytes 147464 | tf_op jit(solution)/shard_map/ppermute | solution.py:16
  7.5 49.8 %collective-permute-start.2 = (f32[6,2,1,256]{3,1,2,0:T(2,128)S(1)}, f32[6,2,1,256]{3,1,2,0:T(2,128)S(1)}, u32[]{:S(2)}, u32[]{:S(2)}) collective-permute-start(f32[6,2,1,256]{3,1,2,0:T(2,128)S(1)} %slice.670), channel_id=1, source_target_pairs={{0,1},{1,2},{2,3},{3,4},{4,5},{5,6},{6,7},{7,8},{8,9},{9,10},{10,1... | collective-permute-start | bytes 36872 | tf_op jit(solution)/shard_map/ppermute | solution.py:16
  10.3 47.1 %collective-permute-start.1 = (f32[6,1,8,256]{3,2,1,0:T(8,128)S(1)}, f32[6,1,8,256]{3,2,1,0:T(8,128)S(1)}, u32[]{:S(2)}, u32[]{:S(2)}) collective-permute-start(f32[6,1,8,256]{3,2,1,0:T(8,128)S(1)} %get-tuple-element.217), channel_id=1, source_target_pairs={{16,0},{32,16},{48,32},{64,48},{80,64},{96,80},{112,96},{128,112},... | collective-permute-start | bytes 147464 | tf_op jit(solution)/shard_map/ppermute | solution.py:17
  12.8 111.8 %copy-start.10 = (pred[2]{0:T(512)(128)(4,1)}, pred[2]{0:T(512)(128)(4,1)S(1)}, u32[]{:S(2)}) copy-start(pred[2]{0:T(512)(128)(4,1)S(1)} %get-tuple-element.221) | copy-start | bytes 10
  12.8 110.3 %copy-start.15 = (s32[1024]{0:T(1024)}, s32[1024]{0:T(1024)S(1)}, u32[]{:S(2)}) copy-start(s32[1024]{0:T(1024)S(1)} %pad_clamp_fusion) | copy-start | bytes 12292
  65.8 59.8 %collective-permute-start.7 = (f32[6,2,1,256]{3,1,2,0:T(2,128)}, f32[6,2,1,256]{3,1,2,0:T(2,128)}, u32[]{:S(2)}, u32[]{:S(2)}) collective-permute-start(f32[6,2,1,256]{3,1,2,0:T(2,128)} %copy.246), channel_id=1, source_target_pairs={{1,0},{2,1},{3,2},{4,3},{5,4},{6,5},{7,6},{8,7},{9,8},{10,9},{11,1... | collective-permute-start | bytes 36872 | tf_op jit(solution)/shard_map/ppermute | solution.py:17
  67.1 60.0 %collective-permute-start.4 = (f32[6,1,8,256]{3,2,1,0:T(8,128)}, f32[6,1,8,256]{3,2,1,0:T(8,128)}, u32[]{:S(2)}, u32[]{:S(2)}) collective-permute-start(f32[6,1,8,256]{3,2,1,0:T(8,128)} %get-tuple-element.214), channel_id=1, source_target_pairs={{0,16},{16,32},{32,48},{48,64},{64,80},{80,96},{96,112},{112,128},... | collective-permute-start | bytes 147464 | tf_op jit(solution)/shard_map/ppermute | solution.py:16
  69.7 56.7 %collective-permute-start.6 = (f32[6,2,1,256]{3,1,2,0:T(2,128)}, f32[6,2,1,256]{3,1,2,0:T(2,128)}, u32[]{:S(2)}, u32[]{:S(2)}) collective-permute-start(f32[6,2,1,256]{3,1,2,0:T(2,128)} %slice.683), channel_id=1, source_target_pairs={{0,1},{1,2},{2,3},{3,4},{4,5},{5,6},{6,7},{7,8},{8,9},{9,10},{10,1... | collective-permute-start | bytes 36872 | tf_op jit(solution)/shard_map/ppermute | solution.py:16
  73.9 53.2 %collective-permute-start.5 = (f32[6,1,8,256]{3,2,1,0:T(8,128)}, f32[6,1,8,256]{3,2,1,0:T(8,128)}, u32[]{:S(2)}, u32[]{:S(2)}) collective-permute-start(f32[6,1,8,256]{3,2,1,0:T(8,128)} %get-tuple-element.213), channel_id=1, source_target_pairs={{16,0},{32,16},{48,32},{64,48},{80,64},{96,80},{112,96},{128,112},... | collective-permute-start | bytes 147464 | tf_op jit(solution)/shard_map/ppermute | solution.py:17
  138.4 61.5 %copy-start.11 = (pred[2]{0:T(512)(128)(4,1)S(1)}, pred[2]{0:T(512)(128)(4,1)}, u32[]{:S(2)}) copy-start(pred[2]{0:T(512)(128)(4,1)} %copy-done.10) | copy-start | bytes 10
  140.2 60.7 %collective-permute-start.11 = (f32[6,2,1,256]{3,1,2,0:T(2,128)}, f32[6,2,1,256]{3,1,2,0:T(2,128)}, u32[]{:S(2)}, u32[]{:S(2)}) collective-permute-start(f32[6,2,1,256]{3,1,2,0:T(2,128)} %copy.255), channel_id=1, source_target_pairs={{1,0},{2,1},{3,2},{4,3},{5,4},{6,5},{7,6},{8,7},{9,8},{10,9},{11,1... | collective-permute-start | bytes 36872 | tf_op jit(solution)/shard_map/ppermute | solution.py:17
  141.4 60.9 %collective-permute-start.8 = (f32[6,1,8,256]{3,2,1,0:T(8,128)}, f32[6,1,8,256]{3,2,1,0:T(8,128)}, u32[]{:S(2)}, u32[]{:S(2)}) collective-permute-start(f32[6,1,8,256]{3,2,1,0:T(8,128)} %get-tuple-element.210), channel_id=1, source_target_pairs={{0,16},{16,32},{32,48},{48,64},{64,80},{80,96},{96,112},{112,128},... | collective-permute-start | bytes 147464 | tf_op jit(solution)/shard_map/ppermute | solution.py:16
  144.0 57.5 %collective-permute-start.10 = (f32[6,2,1,256]{3,1,2,0:T(2,128)}, f32[6,2,1,256]{3,1,2,0:T(2,128)}, u32[]{:S(2)}, u32[]{:S(2)}) collective-permute-start(f32[6,2,1,256]{3,1,2,0:T(2,128)} %slice.696), channel_id=1, source_target_pairs={{0,1},{1,2},{2,3},{3,4},{4,5},{5,6},{6,7},{7,8},{8,9},{9,10},{10,1... | collective-permute-start | bytes 36872 | tf_op jit(solution)/shard_map/ppermute | solution.py:16
  148.3 54.0 %collective-permute-start.9 = (f32[6,1,8,256]{3,2,1,0:T(8,128)}, f32[6,1,8,256]{3,2,1,0:T(8,128)}, u32[]{:S(2)}, u32[]{:S(2)}) collective-permute-start(f32[6,1,8,256]{3,2,1,0:T(8,128)} %get-tuple-element.209), channel_id=1, source_target_pairs={{16,0},{32,16},{48,32},{64,48},{80,64},{96,80},{112,96},{128,112},... | collective-permute-start | bytes 147464 | tf_op jit(solution)/shard_map/ppermute | solution.py:17
  213.6 60.7 %copy-start.12 = (pred[2]{0:T(512)(128)(4,1)S(1)}, pred[2]{0:T(512)(128)(4,1)}, u32[]{:S(2)}) copy-start(pred[2]{0:T(512)(128)(4,1)} %copy-done.10) | copy-start | bytes 10
  215.4 59.9 %collective-permute-start.15 = (f32[6,2,1,256]{3,1,2,0:T(2,128)}, f32[6,2,1,256]{3,1,2,0:T(2,128)}, u32[]{:S(2)}, u32[]{:S(2)}) collective-permute-start(f32[6,2,1,256]{3,1,2,0:T(2,128)} %copy.264), channel_id=1, source_target_pairs={{1,0},{2,1},{3,2},{4,3},{5,4},{6,5},{7,6},{8,7},{9,8},{10,9},{11,1... | collective-permute-start | bytes 36872 | tf_op jit(solution)/shard_map/ppermute | solution.py:17
  216.7 60.0 %collective-permute-start.12 = (f32[6,1,8,256]{3,2,1,0:T(8,128)}, f32[6,1,8,256]{3,2,1,0:T(8,128)}, u32[]{:S(2)}, u32[]{:S(2)}) collective-permute-start(f32[6,1,8,256]{3,2,1,0:T(8,128)} %get-tuple-element.206), channel_id=1, source_target_pairs={{0,16},{16,32},{32,48},{48,64},{64,80},{80,96},{96,112},{112,128},... | collective-permute-start | bytes 147464 | tf_op jit(solution)/shard_map/ppermute | solution.py:16
  219.2 56.7 %collective-permute-start.14 = (f32[6,2,1,256]{3,1,2,0:T(2,128)}, f32[6,2,1,256]{3,1,2,0:T(2,128)}, u32[]{:S(2)}, u32[]{:S(2)}) collective-permute-start(f32[6,2,1,256]{3,1,2,0:T(2,128)} %slice.709), channel_id=1, source_target_pairs={{0,1},{1,2},{2,3},{3,4},{4,5},{5,6},{6,7},{7,8},{8,9},{9,10},{10,1... | collective-permute-start | bytes 36872 | tf_op jit(solution)/shard_map/ppermute | solution.py:16
  223.7 53.0 %collective-permute-start.13 = (f32[6,1,8,256]{3,2,1,0:T(8,128)}, f32[6,1,8,256]{3,2,1,0:T(8,128)}, u32[]{:S(2)}, u32[]{:S(2)}) collective-permute-start(f32[6,1,8,256]{3,2,1,0:T(8,128)} %get-tuple-element.205), channel_id=1, source_target_pairs={{16,0},{32,16},{48,32},{64,48},{80,64},{96,80},{112,96},{128,112},... | collective-permute-start | bytes 147464 | tf_op jit(solution)/shard_map/ppermute | solution.py:17
  288.0 61.0 %copy-start.13 = (pred[2]{0:T(512)(128)(4,1)S(1)}, pred[2]{0:T(512)(128)(4,1)}, u32[]{:S(2)}) copy-start(pred[2]{0:T(512)(128)(4,1)} %copy-done.10) | copy-start | bytes 10
  289.8 60.2 %collective-permute-start.19 = (f32[6,2,1,256]{3,1,2,0:T(2,128)}, f32[6,2,1,256]{3,1,2,0:T(2,128)}, u32[]{:S(2)}, u32[]{:S(2)}) collective-permute-start(f32[6,2,1,256]{3,1,2,0:T(2,128)} %copy.273), channel_id=1, source_target_pairs={{1,0},{2,1},{3,2},{4,3},{5,4},{6,5},{7,6},{8,7},{9,8},{10,9},{11,1... | collective-permute-start | bytes 36872 | tf_op jit(solution)/shard_map/ppermute | solution.py:17
  291.1 60.3 %collective-permute-start.16 = (f32[6,1,8,256]{3,2,1,0:T(8,128)}, f32[6,1,8,256]{3,2,1,0:T(8,128)}, u32[]{:S(2)}, u32[]{:S(2)}) collective-permute-start(f32[6,1,8,256]{3,2,1,0:T(8,128)} %get-tuple-element.202), channel_id=1, source_target_pairs={{0,16},{16,32},{32,48},{48,64},{64,80},{80,96},{96,112},{112,128},... | collective-permute-start | bytes 147464 | tf_op jit(solution)/shard_map/ppermute | solution.py:16
  293.6 57.0 %collective-permute-start.18 = (f32[6,2,1,256]{3,1,2,0:T(2,128)}, f32[6,2,1,256]{3,1,2,0:T(2,128)}, u32[]{:S(2)}, u32[]{:S(2)}) collective-permute-start(f32[6,2,1,256]{3,1,2,0:T(2,128)} %slice.722), channel_id=1, source_target_pairs={{0,1},{1,2},{2,3},{3,4},{4,5},{5,6},{6,7},{7,8},{8,9},{9,10},{10,1... | collective-permute-start | bytes 36872 | tf_op jit(solution)/shard_map/ppermute | solution.py:16
  297.9 53.5 %collective-permute-start.17 = (f32[6,1,8,256]{3,2,1,0:T(8,128)}, f32[6,1,8,256]{3,2,1,0:T(8,128)}, u32[]{:S(2)}, u32[]{:S(2)}) collective-permute-start(f32[6,1,8,256]{3,2,1,0:T(8,128)} %get-tuple-element.201), channel_id=1, source_target_pairs={{16,0},{32,16},{48,32},{64,48},{80,64},{96,80},{112,96},{128,112},... | collective-permute-start | bytes 147464 | tf_op jit(solution)/shard_map/ppermute | solution.py:17
  363.1 54.5 %copy-start.7 = (pred[6]{0:T(512)(128)(4,1)S(1)}, pred[6]{0:T(512)(128)(4,1)}, u32[]{:S(2)}) copy-start(pred[6]{0:T(512)(128)(4,1)} %copy-done.6) | copy-start | bytes 22
  363.1 54.5 %copy-start.9 = (pred[6]{0:T(512)(128)(4,1)S(1)}, pred[6]{0:T(512)(128)(4,1)}, u32[]{:S(2)}) copy-start(pred[6]{0:T(512)(128)(4,1)} %copy-done.8) | copy-start | bytes 22
  363.3 54.0 %collective-permute-start.23 = (f32[6,2,1,256]{3,1,2,0:T(2,128)S(1)}, f32[6,2,1,256]{3,1,2,0:T(2,128)S(1)}, u32[]{:S(2)}, u32[]{:S(2)}) collective-permute-start(f32[6,2,1,256]{3,1,2,0:T(2,128)S(1)} %copy.282), channel_id=1, source_target_pairs={{1,0},{2,1},{3,2},{4,3},{5,4},{6,5},{7,6},{8,7},{9,8},{10,9},{11,1... | collective-permute-start | bytes 36872 | tf_op jit(solution)/shard_map/ppermute | solution.py:17
  364.6 52.8 %collective-permute-start.20 = (f32[6,1,8,256]{3,2,1,0:T(8,128)S(1)}, f32[6,1,8,256]{3,2,1,0:T(8,128)S(1)}, u32[]{:S(2)}, u32[]{:S(2)}) collective-permute-start(f32[6,1,8,256]{3,2,1,0:T(8,128)S(1)} %get-tuple-element.198), channel_id=1, source_target_pairs={{0,16},{16,32},{32,48},{48,64},{64,80},{80,96},{96,112},{112,128},... | collective-permute-start | bytes 147464 | tf_op jit(solution)/shard_map/ppermute | solution.py:16
  366.6 50.7 %collective-permute-start.22 = (f32[6,2,1,256]{3,1,2,0:T(2,128)S(1)}, f32[6,2,1,256]{3,1,2,0:T(2,128)S(1)}, u32[]{:S(2)}, u32[]{:S(2)}) collective-permute-start(f32[6,2,1,256]{3,1,2,0:T(2,128)S(1)} %slice.735), channel_id=1, source_target_pairs={{0,1},{1,2},{2,3},{3,4},{4,5},{5,6},{6,7},{7,8},{8,9},{9,10},{10,1... | collective-permute-start | bytes 36872 | tf_op jit(solution)/shard_map/ppermute | solution.py:16
  369.6 47.7 %collective-permute-start.21 = (f32[6,1,8,256]{3,2,1,0:T(8,128)S(1)}, f32[6,1,8,256]{3,2,1,0:T(8,128)S(1)}, u32[]{:S(2)}, u32[]{:S(2)}) collective-permute-start(f32[6,1,8,256]{3,2,1,0:T(8,128)S(1)} %get-tuple-element.197), channel_id=1, source_target_pairs={{16,0},{32,16},{48,32},{64,48},{80,64},{96,80},{112,96},{128,112},... | collective-permute-start | bytes 147464 | tf_op jit(solution)/shard_map/ppermute | solution.py:17
  (10 other events, 92.3 us)
where the time goes:
time: 426 us; the launch traced here: 424 us
  blocking collectives  269 us (63%)
  local copies, waits for them, and re-layouts  74.3 us (17%)
  starting transfers between devices  61.7 us (14%)
  other arithmetic  16.8 us (4%)
    all_gather x6, blocking collectives, per_device(): whole_rows = lax.all_gather(cut_rows, 'chord', axis=0, tiled=True)  269 us
    ppermute x12, starting transfers between devices, padded(): before = lax.ppermute(last, axis, up)  33.4 us
    ppermute x12, starting transfers between devices, padded(): after = lax.ppermute(initial, axis, down)  28.3 us
    broadcast_in_dim x6, local copies, waits for them, and re-layouts, line_update(): jnp.broadcast_to(jnp.moveaxis(pairs, 4, 1)[..., None], (count_state, 2, c...  16.7 us
    unnamed x42, local copies, waits for them, and re-layouts  14.1 us
  transfers between devices with their start and end apart: 24, of which 0 were waited for; matrix products, arithmetic and copies ran while one was open for 5% of the time, Pallas kernels for 0%

commit v1 on v0

v1 whole, which is shorter than its diff:
```python
import jax
import jax.numpy as jnp
from jax import lax
from jax.experimental import pallas as pl
from jax.experimental.pallas import tpu as pltpu
from jax.sharding import PartitionSpec as P

SWEEPS = 6
F32 = jnp.float32
VMEM_LIMIT = 24 * 2**20


def product(blocks, lead, field):
    out = [None] * 6
    for a in range(6):
        for b in range(6):
            term = blocks[(*lead, a, b)].astype(F32) * field[a]
            out[b] = term if a == 0 else out[b] + term
    return out


def product_rows(blocks, lead, field, low):
    out = [None] * 6
    for a in range(6):
        for b in range(6):
            term = blocks[(*lead, a, b)].astype(F32)[low : low + 8] * field[a][low : low + 8]
            out[b] = term if a == 0 else out[b] + term
    return out


def iotas(shape):
    return lax.broadcasted_iota(jnp.int32, shape, 0), lax.broadcasted_iota(jnp.int32, shape, 1)


def edges(source, couplings, field, even_chord, even_span, out):
    part_ref, chord_even_ref, chord_odd_ref, span_even_ref, span_odd_ref, cut_ref = out
    up = product_rows(couplings, (1,), field, 8)
    down = product_rows(couplings, (0,), field, 0)
    for b in range(6):
        chord_odd_ref[b] = jnp.where(even_chord, down[b], up[b])
        chord_even_ref[b] = jnp.where(even_chord, up[b], down[b])
    plus = product(couplings, (3,), field)
    minus = product(couplings, (2,), field)
    for b in range(6):
        for c in range(2):
            top, bottom = (minus[b][8 * c : 8 * c + 1], plus[b][8 * c + 7 : 8 * c + 8])
            at = 2 * b + c
            span_odd_ref[at : at + 1] = jnp.where(even_span, top, bottom)
            span_even_ref[at : at + 1] = jnp.where(even_span, bottom, top)
    normal = product(couplings, (4,), field)
    row, lane = iotas((16, 256))
    row = row % 8
    cut = jnp.zeros((8, 128), F32)
    cut_lane = iotas((8, 128))[1]
    for b in range(6):
        for c in range(2):
            column = normal[b][8 * c : 8 * c + 8, 0:1]
            cut = jnp.where(cut_lane == 2 * b + c, column, cut)
    cut_ref[...] = cut
    for b in range(6):
        inside = jnp.where(row == 0, 0.0, pltpu.roll(plus[b], 1, 0))
        inside = inside + jnp.where(row == 7, 0.0, pltpu.roll(minus[b], 15, 0))
        inside = inside + jnp.where(lane == 255, 0.0, pltpu.roll(normal[b], 255, 1))
        part_ref[b] = source[b] - inside


def first_kernel(source, couplings, adjoint, *out):
    even_chord = lax.axis_index("chord") % 2 == 0
    even_span = lax.axis_index("span") % 2 == 0
    field = [adjoint[a] for a in range(6)]
    edges(source, couplings, field, even_chord, even_span, out)


def inside_kernel(part, diag_block, couplings, adjoint, out):
    field = [adjoint[a] for a in range(6)]
    own = product(diag_block, (), field)
    up = product_rows(couplings, (1,), field, 0)
    down = product_rows(couplings, (0,), field, 8)
    normal = product(couplings, (5,), field)
    lane = iotas((16, 256))[1]
    for b in range(6):
        inside = own[b] + jnp.where(lane == 0, 0.0, pltpu.roll(normal[b], 1, 1))
        inside = inside + jnp.concatenate([down[b], up[b]], axis=0)
        out[b] = part[b] - inside


def finish(part, got, masks, line_inverse, adjoint, even_chord, even_span):
    chord_even, chord_odd, span_even, span_odd, cut = got
    row, lane = iotas((16, 256))
    row = row % 8
    top = jnp.where(even_span, span_odd[...], span_even[...])
    bottom = jnp.where(even_span, span_even[...], span_odd[...])
    arrived = cut[...]
    odd_lane = lane % 2 == 1
    residual, even_part, odd_part = [], [], []
    for b in range(6):
        ev, od = chord_even[b], chord_odd[b]
        outside = jnp.concatenate([jnp.where(even_chord, od, ev), jnp.where(even_chord, ev, od)], axis=0)
        tops = jnp.concatenate(
            [jnp.broadcast_to(top[2 * b + c : 2 * b + c + 1], (8, 256)) for c in range(2)], axis=0
        )
        bottoms = jnp.concatenate(
            [jnp.broadcast_to(bottom[2 * b + c : 2 * b + c + 1], (8, 256)) for c in range(2)], axis=0
        )
        outside = outside + jnp.where(row == 0, tops, jnp.where(row == 7, bottoms, 0.0))
        columns = jnp.concatenate([arrived[:, 2 * b + 1 : 2 * b + 2], arrived[:, 2 * b : 2 * b + 1]], axis=0)
        outside = outside + jnp.where((lane == 0) & (masks[2][:, 0:1] > 0), columns, 0.0)
        value = part[b] - outside
        if 1 <= b <= 3:
            value = value * jnp.where(lane == 0, masks[0][:, 0:1], 1.0)
        if b == 5:
            value = value * jnp.where(lane == 0, masks[1][:, 0:1], 1.0)
        residual.append(value)
        even_part.append(jnp.where(odd_lane, pltpu.roll(value, 1, 1), value))
        odd_part.append(jnp.where(odd_lane, value, pltpu.roll(value, 255, 1)))
    after = []
    for a in range(6):
        total = adjoint[a]
        for b in range(6):
            total = total + line_inverse[a, b, 0].astype(F32) * even_part[b]
            total = total + line_inverse[a, b, 1].astype(F32) * odd_part[b]
        after.append(total)
    return residual, after


def middle_kernel(
    part, chord_even, chord_odd, span_even, span_odd, cut, masks, line_inverse, adjoint, source, couplings, after_ref, *out
):
    even_chord = lax.axis_index("chord") % 2 == 0
    even_span = lax.axis_index("span") % 2 == 0
    got = (chord_even, chord_odd, span_even, span_odd, cut)
    _, after = finish(part, got, masks, line_inverse, adjoint, even_chord, even_span)
    for a in range(6):
        after_ref[a] = after[a]
    edges(source, couplings, after, even_chord, even_span, out)


def last_kernel(
    part, chord_even, chord_odd, span_even, span_odd, cut, masks, line_inverse, adjoint, after_ref, residual_ref
):
    even_chord = lax.axis_index("chord") % 2 == 0
    even_span = lax.axis_index("span") % 2 == 0
    got = (chord_even, chord_odd, span_even, span_odd, cut)
    residual, after = finish(part, got, masks, line_inverse, adjoint, even_chord, even_span)
    for a in range(6):
        after_ref[a] = after[a]
        residual_ref[a] = residual[a]


def call(kernel, name, operands, shapes, flops, in_vmem=True):
    vmem = pl.BlockSpec(memory_space=pltpu.VMEM)
    made = [pltpu.VMEM(s, F32) if in_vmem else jax.ShapeDtypeStruct(s, F32) for s in shapes]
    held = [pltpu.with_memory_space_constraint(x, pltpu.VMEM) for x in operands]
    return pl.pallas_call(
        kernel,
        name=name,
        out_shape=made,
        in_specs=[vmem] * len(held),
        out_specs=[vmem] * len(shapes),
        compiler_params=pltpu.CompilerParams(vmem_limit_bytes=VMEM_LIMIT),
        cost_estimate=pl.CostEstimate(flops=flops, bytes_accessed=0, transcendentals=0),
    )(*held)


FIELD = (6, 16, 256)
SENT = [FIELD, (6, 8, 256), (6, 8, 256), (16, 256), (16, 256), (8, 128)]


def wall_masks(partner, codes):
    wall = jnp.repeat(partner < 0, 8)
    stuck = wall & (codes.reshape(16) == 0)
    rows = jnp.stack([jnp.where(stuck, 0.0, 1.0), jnp.where(wall, 0.0, 1.0), jnp.where(wall, 0.0, 1.0)])
    return jnp.broadcast_to(rows[:, :, None], (3, 16, 128)).astype(F32)


def pairs(count, start):
    found = []
    for i in range(start, count - 1, 2):
        found += [(i, i + 1), (i + 1, i)]
    return found


def exchange(sent):
    chord_even, chord_odd, span_even, span_odd, cut = sent
    chords, spans = lax.axis_size("chord"), lax.axis_size("span")
    cut = lax.ppermute(cut, "chord", [(i, chords - 1 - i) for i in range(chords)])
    chord_odd = lax.ppermute(chord_odd, "chord", pairs(chords, 1))
    span_odd = lax.ppermute(span_odd, "span", pairs(spans, 1))
    chord_even = lax.ppermute(chord_even, "chord", pairs(chords, 0))
    span_even = lax.ppermute(span_even, "span", pairs(spans, 0))
    return chord_even, chord_odd, span_even, span_odd, cut


def per_device(adjoint, source, diag_block, couplings, line_inverse, partner, codes):
    adjoint = adjoint.reshape(FIELD)
    source = source.reshape(FIELD)
    diag_block = diag_block.reshape(6, 6, 16, 256)
    couplings = couplings.reshape(6, 6, 6, 16, 256)
    line_inverse = line_inverse.reshape(6, 6, 2, 16, 256)
    masks = wall_masks(partner, codes)
    part, *sent = call(first_kernel, "first_edges", (source, couplings, adjoint), SENT, 5_000_000)
    for sweep in range(SWEEPS):
        got = exchange(sent)
        [part] = call(inside_kernel, "inside", (part, diag_block, couplings, adjoint), [FIELD], 4_000_000)
        arguments = (part, *got, masks, line_inverse, adjoint)
        if sweep < SWEEPS - 1:
            adjoint, part, *sent = call(
                middle_kernel, "sweep", (*arguments, source, couplings), [FIELD, *SENT], 8_000_000
            )
        else:
            adjoint, residual = call(last_kernel, "last", arguments, [FIELD, FIELD], 3_000_000, False)
    return adjoint.reshape(6, 2, 8, 256), residual.reshape(6, 2, 8, 256)


def solution(mesh):
    placed = (
        P(None, "chord", "span", None),
        P(None, "chord", "span", None),
        P(None, None, "chord", "span", None),
        P(None, None, None, "chord", "span", None),
        P(None, None, None, "chord", "span", None),
        P("chord"),
        P("chord", "span"),
    )
    return jax.shard_map(
        per_device,
        mesh=mesh,
        in_specs=placed,
        out_specs=(P(None, "chord", "span", None), P(None, "chord", "span", None)),
        check_vma=False,
    )
```

time: 426 us -> 108 us (0.25)
  the two profiles are of different devices: /device:TPU:130 before, /device:TPU:184 now
where the time goes in v1:
time: 108 us
  starting transfers between devices  68.6 us (64%)
  waiting for transfers between devices  27.4 us (25%)
  local copies, waits for them, and re-layouts  5.45 us (5%)
  Pallas kernels  5.25 us (5%)
    ppermute x6, starting transfers between devices, exchange(): chord_odd = lax.ppermute(chord_odd, 'chord', pairs(chords, 1))  32.3 us
    ppermute x6, waiting for transfers between devices, exchange(): lax.ppermute(cut, 'chord', [(i, chords - 1 - i) for i in range(chords)])  26 us
    ppermute x6, starting transfers between devices, exchange(): span_odd = lax.ppermute(span_odd, 'span', pairs(spans, 1))  19.4 us
    ppermute x6, starting transfers between devices, exchange(): lax.ppermute(cut, 'chord', [(i, chords - 1 - i) for i in range(chords)])  15.6 us
    pallas_call x13, Pallas kernels, call(): pl.pallas_call(kernel, name=name, out_shape=made, in_specs=[vmem] * len(h...  5.25 us
    unnamed x22, local copies, waits for them, and re-layouts  5.14 us
  transfers between devices with their start and end apart: 30, of which 6 were waited for; matrix products, arithmetic and copies ran while one was open for 0% of the time, Pallas kernels for 1%

profile of v1, /device:TPU:184, one launch (start us, length us, event | category | flops | bytes accessed | tf_op | source)
XLA Modules:
  0.0 107.8 jit_solution(10470843437403785701)
XLA Ops:
  0.7 1.5 %copy-done = bf16[6,6,6,2,8,256]{5,4,3,2,1,0:T(8,128)(2,1)S(1)} copy-done((bf16[6,6,6,2,8,256]{5,4,3,2,1,0:T(8,128)(2,1)S(1)}, bf16[6,6,6,2,8,256]{5,4,3,2,1,0:T(8,128)(2,1)}, u32[]{:S(2)}) %copy-start) | copy-done | bytes 1769496
  2.1 0.9 copy-done.5
  3.0 0.9 copy-done.7
  4.2 2.8 %collective-permute-start.4 = (f32[8,128]{1,0:T(8,128)S(1)}, f32[8,128]{1,0:T(8,128)S(1)}, u32[]{:S(2)}, u32[]{:S(2)}) collective-permute-start(f32[8,128]{1,0:T(8,128)S(1)} %get-tuple-element.50), channel_id=1, source_target_pairs={{0,240},{16,224},{32,208},{48,192},{64,176},{80,160},{96,144},{112... | collective-permute-start | bytes 12296 | tf_op jit(solution)/shard_map/ppermute | solution.py:186
  7.1 2.1 %collective-permute-start.3 = (f32[16,256]{1,0:T(8,128)S(1)}, f32[16,256]{1,0:T(8,128)S(1)}, u32[]{:S(2)}, u32[]{:S(2)}) collective-permute-start(f32[16,256]{1,0:T(8,128)S(1)} %get-tuple-element.49), channel_id=1, source_target_pairs={{1,2},{2,1},{3,4},{4,3},{5,6},{6,5},{7,8},{8,7},{9,10},{10,9},{11,... | collective-permute-start | bytes 49160 | tf_op jit(solution)/shard_map/ppermute | solution.py:188
  9.5 7.0 %collective-permute-start.1 = (f32[6,8,256]{2,1,0:T(8,128)S(1)}, f32[6,8,256]{2,1,0:T(8,128)S(1)}, u32[]{:S(2)}, u32[]{:S(2)}) collective-permute-start(f32[6,8,256]{2,1,0:T(8,128)S(1)} %get-tuple-element.47), channel_id=1, source_target_pairs={{16,32},{32,16},{48,64},{64,48},{80,96},{96,80},{112,128},{128,112... | collective-permute-start | bytes 147464 | tf_op jit(solution)/shard_map/ppermute | solution.py:187
  16.8 1.0 copy-done.3
  17.8 0.9 copy-done.8
  18.9 1.3 %collective-permute-done.1.chord_odd = f32[6,8,256]{2,1,0:T(8,128)S(1)} collective-permute-done((f32[6,8,256]{2,1,0:T(8,128)S(1)}, f32[6,8,256]{2,1,0:T(8,128)S(1)}, u32[]{:S(2)}, u32[]{:S(2)}) %collective-permute-start.1) | collective-permute-done | bytes 49184 | tf_op jit(solution)/shard_map/ppermute | solution.py:187
  20.3 0.6 sweep.5
  21.0 6.5 %collective-permute-start.6 = (f32[6,8,256]{2,1,0:T(8,128)S(1)}, f32[6,8,256]{2,1,0:T(8,128)S(1)}, u32[]{:S(2)}, u32[]{:S(2)}) collective-permute-start(f32[6,8,256]{2,1,0:T(8,128)S(1)} %get-tuple-element.54), channel_id=1, source_target_pairs={{16,32},{32,16},{48,64},{64,48},{80,96},{96,80},{112,128},{128,112... | collective-permute-start | bytes 147464 | tf_op jit(solution)/shard_map/ppermute | solution.py:187
  27.6 3.6 %collective-permute-start.8 = (f32[16,256]{1,0:T(8,128)S(1)}, f32[16,256]{1,0:T(8,128)S(1)}, u32[]{:S(2)}, u32[]{:S(2)}) collective-permute-start(f32[16,256]{1,0:T(8,128)S(1)} %get-tuple-element.56), channel_id=1, source_target_pairs={{1,2},{2,1},{3,4},{4,3},{5,6},{6,5},{7,8},{8,7},{9,10},{10,9},{11,... | collective-permute-start | bytes 49160 | tf_op jit(solution)/shard_map/ppermute | solution.py:188
  31.3 1.6 %collective-permute-start.9 = (f32[8,128]{1,0:T(8,128)S(1)}, f32[8,128]{1,0:T(8,128)S(1)}, u32[]{:S(2)}, u32[]{:S(2)}) collective-permute-start(f32[8,128]{1,0:T(8,128)S(1)} %get-tuple-element.57), channel_id=1, source_target_pairs={{0,240},{16,224},{32,208},{48,192},{64,176},{80,160},{96,144},{112... | collective-permute-start | bytes 12296 | tf_op jit(solution)/shard_map/ppermute | solution.py:186
  33.1 6.1 %collective-permute-done.9.cut = f32[8,128]{1,0:T(8,128)S(1)} collective-permute-done((f32[8,128]{1,0:T(8,128)S(1)}, f32[8,128]{1,0:T(8,128)S(1)}, u32[]{:S(2)}, u32[]{:S(2)}) %collective-permute-start.9) | collective-permute-done | bytes 4128 | tf_op jit(solution)/shard_map/ppermute | solution.py:186
  39.9 3.5 %collective-permute-start.11 = (f32[6,8,256]{2,1,0:T(8,128)S(1)}, f32[6,8,256]{2,1,0:T(8,128)S(1)}, u32[]{:S(2)}, u32[]{:S(2)}) collective-permute-start(f32[6,8,256]{2,1,0:T(8,128)S(1)} %get-tuple-element.61), channel_id=1, source_target_pairs={{16,32},{32,16},{48,64},{64,48},{80,96},{96,80},{112,128},{128,112... | collective-permute-start | bytes 147464 | tf_op jit(solution)/shard_map/ppermute | solution.py:187
  43.5 2.8 %collective-permute-start.13 = (f32[16,256]{1,0:T(8,128)S(1)}, f32[16,256]{1,0:T(8,128)S(1)}, u32[]{:S(2)}, u32[]{:S(2)}) collective-permute-start(f32[16,256]{1,0:T(8,128)S(1)} %get-tuple-element.63), channel_id=1, source_target_pairs={{1,2},{2,1},{3,4},{4,3},{5,6},{6,5},{7,8},{8,7},{9,10},{10,9},{11,... | collective-permute-start | bytes 49160 | tf_op jit(solution)/shard_map/ppermute | solution.py:188
  46.3 4.6 %collective-permute-start.14 = (f32[8,128]{1,0:T(8,128)S(1)}, f32[8,128]{1,0:T(8,128)S(1)}, u32[]{:S(2)}, u32[]{:S(2)}) collective-permute-start(f32[8,128]{1,0:T(8,128)S(1)} %get-tuple-element.64), channel_id=1, source_target_pairs={{0,240},{16,224},{32,208},{48,192},{64,176},{80,160},{96,144},{112... | collective-permute-start | bytes 12296 | tf_op jit(solution)/shard_map/ppermute | solution.py:186
  51.1 3.1 %collective-permute-done.14.cut = f32[8,128]{1,0:T(8,128)S(1)} collective-permute-done((f32[8,128]{1,0:T(8,128)S(1)}, f32[8,128]{1,0:T(8,128)S(1)}, u32[]{:S(2)}, u32[]{:S(2)}) %collective-permute-start.14) | collective-permute-done | bytes 4128 | tf_op jit(solution)/shard_map/ppermute | solution.py:186
  54.9 6.4 %collective-permute-start.16 = (f32[6,8,256]{2,1,0:T(8,128)S(1)}, f32[6,8,256]{2,1,0:T(8,128)S(1)}, u32[]{:S(2)}, u32[]{:S(2)}) collective-permute-start(f32[6,8,256]{2,1,0:T(8,128)S(1)} %get-tuple-element.68), channel_id=1, source_target_pairs={{16,32},{32,16},{48,64},{64,48},{80,96},{96,80},{112,128},{128,112... | collective-permute-start | bytes 147464 | tf_op jit(solution)/shard_map/ppermute | solution.py:187
  61.5 3.8 %collective-permute-start.18 = (f32[16,256]{1,0:T(8,128)S(1)}, f32[16,256]{1,0:T(8,128)S(1)}, u32[]{:S(2)}, u32[]{:S(2)}) collective-permute-start(f32[16,256]{1,0:T(8,128)S(1)} %get-tuple-element.70), channel_id=1, source_target_pairs={{1,2},{2,1},{3,4},{4,3},{5,6},{6,5},{7,8},{8,7},{9,10},{10,9},{11,... | collective-permute-start | bytes 49160 | tf_op jit(solution)/shard_map/ppermute | solution.py:188
  65.2 1.1 %collective-permute-start.19 = (f32[8,128]{1,0:T(8,128)S(1)}, f32[8,128]{1,0:T(8,128)S(1)}, u32[]{:S(2)}, u32[]{:S(2)}) collective-permute-start(f32[8,128]{1,0:T(8,128)S(1)} %get-tuple-element.71), channel_id=1, source_target_pairs={{0,240},{16,224},{32,208},{48,192},{64,176},{80,160},{96,144},{112... | collective-permute-start | bytes 12296 | tf_op jit(solution)/shard_map/ppermute | solution.py:186
  66.5 6.6 %collective-permute-done.19.cut = f32[8,128]{1,0:T(8,128)S(1)} collective-permute-done((f32[8,128]{1,0:T(8,128)S(1)}, f32[8,128]{1,0:T(8,128)S(1)}, u32[]{:S(2)}, u32[]{:S(2)}) %collective-permute-start.19) | collective-permute-done | bytes 4128 | tf_op jit(solution)/shard_map/ppermute | solution.py:186
  73.9 2.9 %collective-permute-start.21 = (f32[6,8,256]{2,1,0:T(8,128)S(1)}, f32[6,8,256]{2,1,0:T(8,128)S(1)}, u32[]{:S(2)}, u32[]{:S(2)}) collective-permute-start(f32[6,8,256]{2,1,0:T(8,128)S(1)} %get-tuple-element.75), channel_id=1, source_target_pairs={{16,32},{32,16},{48,64},{64,48},{80,96},{96,80},{112,128},{128,112... | collective-permute-start | bytes 147464 | tf_op jit(solution)/shard_map/ppermute | solution.py:187
  76.9 3.6 %collective-permute-start.23 = (f32[16,256]{1,0:T(8,128)S(1)}, f32[16,256]{1,0:T(8,128)S(1)}, u32[]{:S(2)}, u32[]{:S(2)}) collective-permute-start(f32[16,256]{1,0:T(8,128)S(1)} %get-tuple-element.77), channel_id=1, source_target_pairs={{1,2},{2,1},{3,4},{4,3},{5,6},{6,5},{7,8},{8,7},{9,10},{10,9},{11,... | collective-permute-start | bytes 49160 | tf_op jit(solution)/shard_map/ppermute | solution.py:188
  80.5 4.3 %collective-permute-start.24 = (f32[8,128]{1,0:T(8,128)S(1)}, f32[8,128]{1,0:T(8,128)S(1)}, u32[]{:S(2)}, u32[]{:S(2)}) collective-permute-start(f32[8,128]{1,0:T(8,128)S(1)} %get-tuple-element.78), channel_id=1, source_target_pairs={{0,240},{16,224},{32,208},{48,192},{64,176},{80,160},{96,144},{112... | collective-permute-start | bytes 12296 | tf_op jit(solution)/shard_map/ppermute | solution.py:186
  85.0 3.6 %collective-permute-done.24.cut = f32[8,128]{1,0:T(8,128)S(1)} collective-permute-done((f32[8,128]{1,0:T(8,128)S(1)}, f32[8,128]{1,0:T(8,128)S(1)}, u32[]{:S(2)}, u32[]{:S(2)}) %collective-permute-start.24) | collective-permute-done | bytes 4128 | tf_op jit(solution)/shard_map/ppermute | solution.py:186
  88.6 0.6 sweep.9
  89.3 5.9 %collective-permute-start.26 = (f32[6,8,256]{2,1,0:T(8,128)S(1)}, f32[6,8,256]{2,1,0:T(8,128)S(1)}, u32[]{:S(2)}, u32[]{:S(2)}) collective-permute-start(f32[6,8,256]{2,1,0:T(8,128)S(1)} %get-tuple-element.82), channel_id=1, source_target_pairs={{16,32},{32,16},{48,64},{64,48},{80,96},{96,80},{112,128},{128,112... | collective-permute-start | bytes 147464 | tf_op jit(solution)/shard_map/ppermute | solution.py:187
  95.3 3.5 %collective-permute-start.28 = (f32[16,256]{1,0:T(8,128)S(1)}, f32[16,256]{1,0:T(8,128)S(1)}, u32[]{:S(2)}, u32[]{:S(2)}) collective-permute-start(f32[16,256]{1,0:T(8,128)S(1)} %get-tuple-element.84), channel_id=1, source_target_pairs={{1,2},{2,1},{3,4},{4,3},{5,6},{6,5},{7,8},{8,7},{9,10},{10,9},{11,... | collective-permute-start | bytes 49160 | tf_op jit(solution)/shard_map/ppermute | solution.py:188
  98.9 1.1 %collective-permute-start.29 = (f32[8,128]{1,0:T(8,128)S(1)}, f32[8,128]{1,0:T(8,128)S(1)}, u32[]{:S(2)}, u32[]{:S(2)}) collective-permute-start(f32[8,128]{1,0:T(8,128)S(1)} %get-tuple-element.85), channel_id=1, source_target_pairs={{0,240},{16,224},{32,208},{48,192},{64,176},{80,160},{96,144},{112... | collective-permute-start | bytes 12296 | tf_op jit(solution)/shard_map/ppermute | solution.py:186
  100.2 6.6 %collective-permute-done.29.cut = f32[8,128]{1,0:T(8,128)S(1)} collective-permute-done((f32[8,128]{1,0:T(8,128)S(1)}, f32[8,128]{1,0:T(8,128)S(1)}, u32[]{:S(2)}, u32[]{:S(2)}) %collective-permute-start.29) | collective-permute-done | bytes 4128 | tf_op jit(solution)/shard_map/ppermute | solution.py:186
  106.8 0.9 last.1
  (71 shorter events, 4.9 us)
Async XLA Ops:
  0.6 16.0 %copy-start.9 = (s32[2,8]{1,0:T(2,128)S(1)}, s32[2,8]{1,0:T(2,128)}, u32[]{:S(2)}) copy-start(s32[2,8]{1,0:T(2,128)} %param.13) | copy-start | bytes 196
  3.9 16.4 %copy-start.2 = (bf16[6,6,2,2,8,256]{5,4,3,2,1,0:T(8,128)(2,1)S(1)}, bf16[6,6,2,2,8,256]{5,4,3,2,1,0:T(8,128)(2,1)}, u32[]{:S(2)}) copy-start(bf16[6,6,2,2,8,256]{5,4,3,2,1,0:T(8,128)(2,1)} %param.11) | copy-start | bytes 1769476
  4.2 14.7 %collective-permute-start.4 = (f32[8,128]{1,0:T(8,128)S(1)}, f32[8,128]{1,0:T(8,128)S(1)}, u32[]{:S(2)}, u32[]{:S(2)}) collective-permute-start(f32[8,128]{1,0:T(8,128)S(1)} %get-tuple-element.50), channel_id=1, source_target_pairs={{0,240},{16,224},{32,208},{48,192},{64,176},{80,160},{96,144},{112... | collective-permute-start | bytes 12296 | tf_op jit(solution)/shard_map/ppermute | solution.py:186
  7.0 11.8 %collective-permute-start.2 = (f32[16,256]{1,0:T(8,128)S(1)}, f32[16,256]{1,0:T(8,128)S(1)}, u32[]{:S(2)}, u32[]{:S(2)}) collective-permute-start(f32[16,256]{1,0:T(8,128)S(1)} %get-tuple-element.48), channel_id=1, source_target_pairs={{0,1},{1,0},{2,3},{3,2},{4,5},{5,4},{6,7},{7,6},{8,9},{9,8},{10,11... | collective-permute-start | bytes 49160 | tf_op jit(solution)/shard_map/ppermute | solution.py:190
  7.1 11.8 %collective-permute-start.3 = (f32[16,256]{1,0:T(8,128)S(1)}, f32[16,256]{1,0:T(8,128)S(1)}, u32[]{:S(2)}, u32[]{:S(2)}) collective-permute-start(f32[16,256]{1,0:T(8,128)S(1)} %get-tuple-element.49), channel_id=1, source_target_pairs={{1,2},{2,1},{3,4},{4,3},{5,6},{6,5},{7,8},{8,7},{9,10},{10,9},{11,... | collective-permute-start | bytes 49160 | tf_op jit(solution)/shard_map/ppermute | solution.py:188
  9.2 9.7 %collective-permute-start = (f32[6,8,256]{2,1,0:T(8,128)S(1)}, f32[6,8,256]{2,1,0:T(8,128)S(1)}, u32[]{:S(2)}, u32[]{:S(2)}) collective-permute-start(f32[6,8,256]{2,1,0:T(8,128)S(1)} %get-tuple-element.46), channel_id=1, source_target_pairs={{0,16},{16,0},{32,48},{48,32},{64,80},{80,64},{96,112},{112,96},{1... | collective-permute-start | bytes 147464 | tf_op jit(solution)/shard_map/ppermute | solution.py:189
  9.5 10.7 %collective-permute-start.1 = (f32[6,8,256]{2,1,0:T(8,128)S(1)}, f32[6,8,256]{2,1,0:T(8,128)S(1)}, u32[]{:S(2)}, u32[]{:S(2)}) collective-permute-start(f32[6,8,256]{2,1,0:T(8,128)S(1)} %get-tuple-element.47), channel_id=1, source_target_pairs={{16,32},{32,16},{48,64},{64,48},{80,96},{96,80},{112,128},{128,112... | collective-permute-start | bytes 147464 | tf_op jit(solution)/shard_map/ppermute | solution.py:187
  20.9 18.3 %collective-permute-start.5 = (f32[6,8,256]{2,1,0:T(8,128)S(1)}, f32[6,8,256]{2,1,0:T(8,128)S(1)}, u32[]{:S(2)}, u32[]{:S(2)}) collective-permute-start(f32[6,8,256]{2,1,0:T(8,128)S(1)} %get-tuple-element.53), channel_id=1, source_target_pairs={{0,16},{16,0},{32,48},{48,32},{64,80},{80,64},{96,112},{112,96},{1... | collective-permute-start | bytes 147464 | tf_op jit(solution)/shard_map/ppermute | solution.py:189
  21.0 18.2 %collective-permute-start.6 = (f32[6,8,256]{2,1,0:T(8,128)S(1)}, f32[6,8,256]{2,1,0:T(8,128)S(1)}, u32[]{:S(2)}, u32[]{:S(2)}) collective-permute-start(f32[6,8,256]{2,1,0:T(8,128)S(1)} %get-tuple-element.54), channel_id=1, source_target_pairs={{16,32},{32,16},{48,64},{64,48},{80,96},{96,80},{112,128},{128,112... | collective-permute-start | bytes 147464 | tf_op jit(solution)/shard_map/ppermute | solution.py:187
  27.5 11.6 %collective-permute-start.7 = (f32[16,256]{1,0:T(8,128)S(1)}, f32[16,256]{1,0:T(8,128)S(1)}, u32[]{:S(2)}, u32[]{:S(2)}) collective-permute-start(f32[16,256]{1,0:T(8,128)S(1)} %get-tuple-element.55), channel_id=1, source_target_pairs={{0,1},{1,0},{2,3},{3,2},{4,5},{5,4},{6,7},{7,6},{8,9},{9,8},{10,11... | collective-permute-start | bytes 49160 | tf_op jit(solution)/shard_map/ppermute | solution.py:190
  27.6 11.5 %collective-permute-start.8 = (f32[16,256]{1,0:T(8,128)S(1)}, f32[16,256]{1,0:T(8,128)S(1)}, u32[]{:S(2)}, u32[]{:S(2)}) collective-permute-start(f32[16,256]{1,0:T(8,128)S(1)} %get-tuple-element.56), channel_id=1, source_target_pairs={{1,2},{2,1},{3,4},{4,3},{5,6},{6,5},{7,8},{8,7},{9,10},{10,9},{11,... | collective-permute-start | bytes 49160 | tf_op jit(solution)/shard_map/ppermute | solution.py:188
  31.3 7.9 %collective-permute-start.9 = (f32[8,128]{1,0:T(8,128)S(1)}, f32[8,128]{1,0:T(8,128)S(1)}, u32[]{:S(2)}, u32[]{:S(2)}) collective-permute-start(f32[8,128]{1,0:T(8,128)S(1)} %get-tuple-element.57), channel_id=1, source_target_pairs={{0,240},{16,224},{32,208},{48,192},{64,176},{80,160},{96,144},{112... | collective-permute-start | bytes 12296 | tf_op jit(solution)/shard_map/ppermute | solution.py:186
  39.8 14.4 %collective-permute-start.10 = (f32[6,8,256]{2,1,0:T(8,128)S(1)}, f32[6,8,256]{2,1,0:T(8,128)S(1)}, u32[]{:S(2)}, u32[]{:S(2)}) collective-permute-start(f32[6,8,256]{2,1,0:T(8,128)S(1)} %get-tuple-element.60), channel_id=1, source_target_pairs={{0,16},{16,0},{32,48},{48,32},{64,80},{80,64},{96,112},{112,96},{1... | collective-permute-start | bytes 147464 | tf_op jit(solution)/shard_map/ppermute | solution.py:189
  39.9 14.3 %collective-permute-start.11 = (f32[6,8,256]{2,1,0:T(8,128)S(1)}, f32[6,8,256]{2,1,0:T(8,128)S(1)}, u32[]{:S(2)}, u32[]{:S(2)}) collective-permute-start(f32[6,8,256]{2,1,0:T(8,128)S(1)} %get-tuple-element.61), channel_id=1, source_target_pairs={{16,32},{32,16},{48,64},{64,48},{80,96},{96,80},{112,128},{128,112... | collective-permute-start | bytes 147464 | tf_op jit(solution)/shard_map/ppermute | solution.py:187
  43.4 10.9 %collective-permute-start.12 = (f32[16,256]{1,0:T(8,128)S(1)}, f32[16,256]{1,0:T(8,128)S(1)}, u32[]{:S(2)}, u32[]{:S(2)}) collective-permute-start(f32[16,256]{1,0:T(8,128)S(1)} %get-tuple-element.62), channel_id=1, source_target_pairs={{0,1},{1,0},{2,3},{3,2},{4,5},{5,4},{6,7},{7,6},{8,9},{9,8},{10,11... | collective-permute-start | bytes 49160 | tf_op jit(solution)/shard_map/ppermute | solution.py:190
  43.5 10.8 %collective-permute-start.13 = (f32[16,256]{1,0:T(8,128)S(1)}, f32[16,256]{1,0:T(8,128)S(1)}, u32[]{:S(2)}, u32[]{:S(2)}) collective-permute-start(f32[16,256]{1,0:T(8,128)S(1)} %get-tuple-element.63), channel_id=1, source_target_pairs={{1,2},{2,1},{3,4},{4,3},{5,6},{6,5},{7,8},{8,7},{9,10},{10,9},{11,... | collective-permute-start | bytes 49160 | tf_op jit(solution)/shard_map/ppermute | solution.py:188
  46.3 7.9 %collective-permute-start.14 = (f32[8,128]{1,0:T(8,128)S(1)}, f32[8,128]{1,0:T(8,128)S(1)}, u32[]{:S(2)}, u32[]{:S(2)}) collective-permute-start(f32[8,128]{1,0:T(8,128)S(1)} %get-tuple-element.64), channel_id=1, source_target_pairs={{0,240},{16,224},{32,208},{48,192},{64,176},{80,160},{96,144},{112... | collective-permute-start | bytes 12296 | tf_op jit(solution)/shard_map/ppermute | solution.py:186
  54.8 18.3 %collective-permute-start.15 = (f32[6,8,256]{2,1,0:T(8,128)S(1)}, f32[6,8,256]{2,1,0:T(8,128)S(1)}, u32[]{:S(2)}, u32[]{:S(2)}) collective-permute-start(f32[6,8,256]{2,1,0:T(8,128)S(1)} %get-tuple-element.67), channel_id=1, source_target_pairs={{0,16},{16,0},{32,48},{48,32},{64,80},{80,64},{96,112},{112,96},{1... | collective-permute-start | bytes 147464 | tf_op jit(solution)/shard_map/ppermute | solution.py:189
  54.9 18.2 %collective-permute-start.16 = (f32[6,8,256]{2,1,0:T(8,128)S(1)}, f32[6,8,256]{2,1,0:T(8,128)S(1)}, u32[]{:S(2)}, u32[]{:S(2)}) collective-permute-start(f32[6,8,256]{2,1,0:T(8,128)S(1)} %get-tuple-element.68), channel_id=1, source_target_pairs={{16,32},{32,16},{48,64},{64,48},{80,96},{96,80},{112,128},{128,112... | collective-permute-start | bytes 147464 | tf_op jit(solution)/shard_map/ppermute | solution.py:187
  61.4 11.8 %collective-permute-start.17 = (f32[16,256]{1,0:T(8,128)S(1)}, f32[16,256]{1,0:T(8,128)S(1)}, u32[]{:S(2)}, u32[]{:S(2)}) collective-permute-start(f32[16,256]{1,0:T(8,128)S(1)} %get-tuple-element.69), channel_id=1, source_target_pairs={{0,1},{1,0},{2,3},{3,2},{4,5},{5,4},{6,7},{7,6},{8,9},{9,8},{10,11... | collective-permute-start | bytes 49160 | tf_op jit(solution)/shard_map/ppermute | solution.py:190
  61.5 11.7 %collective-permute-start.18 = (f32[16,256]{1,0:T(8,128)S(1)}, f32[16,256]{1,0:T(8,128)S(1)}, u32[]{:S(2)}, u32[]{:S(2)}) collective-permute-start(f32[16,256]{1,0:T(8,128)S(1)} %get-tuple-element.70), channel_id=1, source_target_pairs={{1,2},{2,1},{3,4},{4,3},{5,6},{6,5},{7,8},{8,7},{9,10},{10,9},{11,... | collective-permute-start | bytes 49160 | tf_op jit(solution)/shard_map/ppermute | solution.py:188
  65.2 7.9 %collective-permute-start.19 = (f32[8,128]{1,0:T(8,128)S(1)}, f32[8,128]{1,0:T(8,128)S(1)}, u32[]{:S(2)}, u32[]{:S(2)}) collective-permute-start(f32[8,128]{1,0:T(8,128)S(1)} %get-tuple-element.71), channel_id=1, source_target_pairs={{0,240},{16,224},{32,208},{48,192},{64,176},{80,160},{96,144},{112... | collective-permute-start | bytes 12296 | tf_op jit(solution)/shard_map/ppermute | solution.py:186
  73.8 14.8 %collective-permute-start.20 = (f32[6,8,256]{2,1,0:T(8,128)S(1)}, f32[6,8,256]{2,1,0:T(8,128)S(1)}, u32[]{:S(2)}, u32[]{:S(2)}) collective-permute-start(f32[6,8,256]{2,1,0:T(8,128)S(1)} %get-tuple-element.74), channel_id=1, source_target_pairs={{0,16},{16,0},{32,48},{48,32},{64,80},{80,64},{96,112},{112,96},{1... | collective-permute-start | bytes 147464 | tf_op jit(solution)/shard_map/ppermute | solution.py:189
  73.9 14.7 %collective-permute-start.21 = (f32[6,8,256]{2,1,0:T(8,128)S(1)}, f32[6,8,256]{2,1,0:T(8,128)S(1)}, u32[]{:S(2)}, u32[]{:S(2)}) collective-permute-start(f32[6,8,256]{2,1,0:T(8,128)S(1)} %get-tuple-element.75), channel_id=1, source_target_pairs={{16,32},{32,16},{48,64},{64,48},{80,96},{96,80},{112,128},{128,112... | collective-permute-start | bytes 147464 | tf_op jit(solution)/shard_map/ppermute | solution.py:187
  76.8 11.8 %collective-permute-start.22 = (f32[16,256]{1,0:T(8,128)S(1)}, f32[16,256]{1,0:T(8,128)S(1)}, u32[]{:S(2)}, u32[]{:S(2)}) collective-permute-start(f32[16,256]{1,0:T(8,128)S(1)} %get-tuple-element.76), channel_id=1, source_target_pairs={{0,1},{1,0},{2,3},{3,2},{4,5},{5,4},{6,7},{7,6},{8,9},{9,8},{10,11... | collective-permute-start | bytes 49160 | tf_op jit(solution)/shard_map/ppermute | solution.py:190
  76.9 11.7 %collective-permute-start.23 = (f32[16,256]{1,0:T(8,128)S(1)}, f32[16,256]{1,0:T(8,128)S(1)}, u32[]{:S(2)}, u32[]{:S(2)}) collective-permute-start(f32[16,256]{1,0:T(8,128)S(1)} %get-tuple-element.77), channel_id=1, source_target_pairs={{1,2},{2,1},{3,4},{4,3},{5,6},{6,5},{7,8},{8,7},{9,10},{10,9},{11,... | collective-permute-start | bytes 49160 | tf_op jit(solution)/shard_map/ppermute | solution.py:188
  80.5 8.1 %collective-permute-start.24 = (f32[8,128]{1,0:T(8,128)S(1)}, f32[8,128]{1,0:T(8,128)S(1)}, u32[]{:S(2)}, u32[]{:S(2)}) collective-permute-start(f32[8,128]{1,0:T(8,128)S(1)} %get-tuple-element.78), channel_id=1, source_target_pairs={{0,240},{16,224},{32,208},{48,192},{64,176},{80,160},{96,144},{112... | collective-permute-start | bytes 12296 | tf_op jit(solution)/shard_map/ppermute | solution.py:186
  89.2 17.6 %collective-permute-start.25 = (f32[6,8,256]{2,1,0:T(8,128)S(1)}, f32[6,8,256]{2,1,0:T(8,128)S(1)}, u32[]{:S(2)}, u32[]{:S(2)}) collective-permute-start(f32[6,8,256]{2,1,0:T(8,128)S(1)} %get-tuple-element.81), channel_id=1, source_target_pairs={{0,16},{16,0},{32,48},{48,32},{64,80},{80,64},{96,112},{112,96},{1... | collective-permute-start | bytes 147464 | tf_op jit(solution)/shard_map/ppermute | solution.py:189
  89.3 17.5 %collective-permute-start.26 = (f32[6,8,256]{2,1,0:T(8,128)S(1)}, f32[6,8,256]{2,1,0:T(8,128)S(1)}, u32[]{:S(2)}, u32[]{:S(2)}) collective-permute-start(f32[6,8,256]{2,1,0:T(8,128)S(1)} %get-tuple-element.82), channel_id=1, source_target_pairs={{16,32},{32,16},{48,64},{64,48},{80,96},{96,80},{112,128},{128,112... | collective-permute-start | bytes 147464 | tf_op jit(solution)/shard_map/ppermute | solution.py:187
  95.2 11.6 %collective-permute-start.27 = (f32[16,256]{1,0:T(8,128)S(1)}, f32[16,256]{1,0:T(8,128)S(1)}, u32[]{:S(2)}, u32[]{:S(2)}) collective-permute-start(f32[16,256]{1,0:T(8,128)S(1)} %get-tuple-element.83), channel_id=1, source_target_pairs={{0,1},{1,0},{2,3},{3,2},{4,5},{5,4},{6,7},{7,6},{8,9},{9,8},{10,11... | collective-permute-start | bytes 49160 | tf_op jit(solution)/shard_map/ppermute | solution.py:190
  95.3 11.5 %collective-permute-start.28 = (f32[16,256]{1,0:T(8,128)S(1)}, f32[16,256]{1,0:T(8,128)S(1)}, u32[]{:S(2)}, u32[]{:S(2)}) collective-permute-start(f32[16,256]{1,0:T(8,128)S(1)} %get-tuple-element.84), channel_id=1, source_target_pairs={{1,2},{2,1},{3,4},{4,3},{5,6},{6,5},{7,8},{8,7},{9,10},{10,9},{11,... | collective-permute-start | bytes 49160 | tf_op jit(solution)/shard_map/ppermute | solution.py:188
  98.9 7.9 %collective-permute-start.29 = (f32[8,128]{1,0:T(8,128)S(1)}, f32[8,128]{1,0:T(8,128)S(1)}, u32[]{:S(2)}, u32[]{:S(2)}) collective-permute-start(f32[8,128]{1,0:T(8,128)S(1)} %get-tuple-element.85), channel_id=1, source_target_pairs={{0,240},{16,224},{32,208},{48,192},{64,176},{80,160},{96,144},{112... | collective-permute-start | bytes 12296 | tf_op jit(solution)/shard_map/ppermute | solution.py:186
  (9 other events, 49.5 us)

commit v2 on v1

--- a/solution.py
+++ b/solution.py
@@ -28,47 +28,83 @@
     return out
 
 
+def product_lanes(blocks, lead, field):
+    out = [None] * 6
+    for a in range(6):
+        for b in range(6):
+            term = blocks[(*lead, a, b, slice(None), slice(0, 128))].astype(F32) * field[a][:, 0:128]
+            out[b] = term if a == 0 else out[b] + term
+    return out
+
+
+def inner(axis):
+    index = lax.axis_index(axis)
+    return (index > 0) & (index < lax.axis_size(axis) - 1)
+
+
 def iotas(shape):
     return lax.broadcasted_iota(jnp.int32, shape, 0), lax.broadcasted_iota(jnp.int32, shape, 1)
 
 
-def edges(source, couplings, field, even_chord, even_span, out):
-    part_ref, chord_even_ref, chord_odd_ref, span_even_ref, span_odd_ref, cut_ref = out
-    up = product_rows(couplings, (1,), field, 8)
-    down = product_rows(couplings, (0,), field, 0)
-    for b in range(6):
-        chord_odd_ref[b] = jnp.where(even_chord, down[b], up[b])
-        chord_even_ref[b] = jnp.where(even_chord, up[b], down[b])
-    plus = product(couplings, (3,), field)
-    minus = product(couplings, (2,), field)
-    for b in range(6):
-        for c in range(2):
-            top, bottom = (minus[b][8 * c : 8 * c + 1], plus[b][8 * c + 7 : 8 * c + 8])
-            at = 2 * b + c
-            span_odd_ref[at : at + 1] = jnp.where(even_span, top, bottom)
-            span_even_ref[at : at + 1] = jnp.where(even_span, bottom, top)
-    normal = product(couplings, (4,), field)
-    row, lane = iotas((16, 256))
-    row = row % 8
+def first_out(couplings, field, even_chord, out):
+    cut_ref, chord_odd_ref, chord_even_ref = out
+    normal = product_lanes(couplings, (4,), field)
+    cut_lane = iotas((8, 128))[1]
     cut = jnp.zeros((8, 128), F32)
-    cut_lane = iotas((8, 128))[1]
     for b in range(6):
         for c in range(2):
             column = normal[b][8 * c : 8 * c + 8, 0:1]
             cut = jnp.where(cut_lane == 2 * b + c, column, cut)
     cut_ref[...] = cut
+    inner_chord = inner("chord")
+    up = product_rows(couplings, (1,), field, 8)
+    down = product_rows(couplings, (0,), field, 0)
+    for b in range(6):
+        chord_odd_ref[b] = jnp.where(inner_chord, jnp.where(even_chord, down[b], up[b]), 0.0)
+        chord_even_ref[b] = jnp.where(even_chord, up[b], down[b])
+
+
+def edges_kernel(adjoint, source, couplings, held_ref, part_ref, chord_even_ref, span_odd_ref, span_even_ref):
+    even_span = lax.axis_index("span") % 2 == 0
+    chord_even_ref[...] = held_ref[...]
+    inner_span = inner("span")
+    field = [adjoint[a] for a in range(6)]
+    plus = product(couplings, (3,), field)
+    minus = product(couplings, (2,), field)
+    for b in range(6):
+        for c in range(2):
+            top, bottom = (minus[b][8 * c : 8 * c + 1], plus[b][8 * c + 7 : 8 * c + 8])
+            at = 2 * b + c
+            span_odd_ref[at : at + 1] = jnp.where(inner_span, jnp.where(even_span, top, bottom), 0.0)
+            span_even_ref[at : at + 1] = jnp.where(even_span, bottom, top)
+    row, lane = iotas((16, 256))
+    row = row % 8
     for b in range(6):
         inside = jnp.where(row == 0, 0.0, pltpu.roll(plus[b], 1, 0))
         inside = inside + jnp.where(row == 7, 0.0, pltpu.roll(minus[b], 15, 0))
-        inside = inside + jnp.where(lane == 255, 0.0, pltpu.roll(normal[b], 255, 1))
         part_ref[b] = source[b] - inside
 
 
-def first_kernel(source, couplings, adjoint, *out):
+def load_kernel(source, couplings, diag_block, line_inverse, adjoint, *out):
+    *held, cut_ref, chord_odd_ref, chord_even_ref, sems = out
+    held_adjoint, held_couplings, held_source, held_diag, held_line = held
+    order = [(4, 5), (0, 2), (2, 4), (5, 6)]
+    copies = [pltpu.make_async_copy(adjoint, held_adjoint, sems.at[0])]
+    for i, (low, high) in enumerate(order):
+        part = pl.ds(low, high - low)
+        copies.append(pltpu.make_async_copy(couplings.at[part], held_couplings.at[part], sems.at[1 + i]))
+    copies.append(pltpu.make_async_copy(source, held_source, sems.at[5]))
+    copies.append(pltpu.make_async_copy(diag_block, held_diag, sems.at[6]))
+    copies.append(pltpu.make_async_copy(line_inverse, held_line, sems.at[7]))
+    for copy in copies:
+        copy.start()
+    for copy in copies[:3]:
+        copy.wait()
     even_chord = lax.axis_index("chord") % 2 == 0
-    even_span = lax.axis_index("span") % 2 == 0
-    field = [adjoint[a] for a in range(6)]
-    edges(source, couplings, field, even_chord, even_span, out)
+    field = [held_adjoint[a] for a in range(6)]
+    first_out(held_couplings, field, even_chord, (cut_ref, chord_odd_ref, chord_even_ref))
+    for copy in copies[3:]:
+        copy.wait()
 
 
 def inside_kernel(part, diag_block, couplings, adjoint, out):
@@ -76,21 +112,24 @@
     own = product(diag_block, (), field)
     up = product_rows(couplings, (1,), field, 0)
     down = product_rows(couplings, (0,), field, 8)
-    normal = product(couplings, (5,), field)
+    plus = product(couplings, (5,), field)
+    minus = product(couplings, (4,), field)
     lane = iotas((16, 256))[1]
     for b in range(6):
-        inside = own[b] + jnp.where(lane == 0, 0.0, pltpu.roll(normal[b], 1, 1))
+        inside = own[b] + jnp.where(lane == 0, 0.0, pltpu.roll(plus[b], 1, 1))
+        inside = inside + jnp.where(lane == 255, 0.0, pltpu.roll(minus[b], 255, 1))
         inside = inside + jnp.concatenate([down[b], up[b]], axis=0)
         out[b] = part[b] - inside
 
 
 def finish(part, got, masks, line_inverse, adjoint, even_chord, even_span):
-    chord_even, chord_odd, span_even, span_odd, cut = got
+    cut, chord_odd, chord_even, span_odd, span_even = got
     row, lane = iotas((16, 256))
     row = row % 8
-    top = jnp.where(even_span, span_odd[...], span_even[...])
-    bottom = jnp.where(even_span, span_even[...], span_odd[...])
+    top = jnp.where(even_span, span_odd[...], span_even[0:16])
+    bottom = jnp.where(even_span, span_even[0:16], span_odd[...])
     arrived = cut[...]
+    wake = masks[2][:, 0:1] > 0
     odd_lane = lane % 2 == 1
     residual, even_part, odd_part = [], [], []
     for b in range(6):
@@ -104,7 +143,7 @@
         )
         outside = outside + jnp.where(row == 0, tops, jnp.where(row == 7, bottoms, 0.0))
         columns = jnp.concatenate([arrived[:, 2 * b + 1 : 2 * b + 2], arrived[:, 2 * b : 2 * b + 1]], axis=0)
-        outside = outside + jnp.where((lane == 0) & (masks[2][:, 0:1] > 0), columns, 0.0)
+        outside = outside + jnp.where((lane == 0) & wake, columns, 0.0)
         value = part[b] - outside
         if 1 <= b <= 3:
             value = value * jnp.where(lane == 0, masks[0][:, 0:1], 1.0)
@@ -124,23 +163,23 @@
 
 
 def middle_kernel(
-    part, chord_even, chord_odd, span_even, span_odd, cut, masks, line_inverse, adjoint, source, couplings, after_ref, *out
+    part, cut, chord_odd, chord_even, span_odd, span_even, masks, line_inverse, adjoint, couplings, after_ref, *out
 ):
     even_chord = lax.axis_index("chord") % 2 == 0
     even_span = lax.axis_index("span") % 2 == 0
-    got = (chord_even, chord_odd, span_even, span_odd, cut)
+    got = (cut, chord_odd, chord_even, span_odd, span_even)
     _, after = finish(part, got, masks, line_inverse, adjoint, even_chord, even_span)
     for a in range(6):
         after_ref[a] = after[a]
-    edges(source, couplings, after, even_chord, even_span, out)
+    first_out(couplings, after, even_chord, out)
 
 
 def last_kernel(
-    part, chord_even, chord_odd, span_even, span_odd, cut, masks, line_inverse, adjoint, after_ref, residual_ref
+    part, cut, chord_odd, chord_even, span_odd, span_even, masks, line_inverse, adjoint, after_ref, residual_ref
 ):
     even_chord = lax.axis_index("chord") % 2 == 0
     even_span = lax.axis_index("span") % 2 == 0
-    got = (chord_even, chord_odd, span_even, span_odd, cut)
+    got = (cut, chord_odd, chord_even, span_odd, span_even)
     residual, after = finish(part, got, masks, line_inverse, adjoint, even_chord, even_span)
     for a in range(6):
         after_ref[a] = after[a]
@@ -163,7 +202,28 @@
 
 
 FIELD = (6, 16, 256)
-SENT = [FIELD, (6, 8, 256), (6, 8, 256), (16, 256), (16, 256), (8, 128)]
+SLAB = (6, 8, 256)
+ROWS = (16, 256)
+FIRST = [(8, 128), SLAB, SLAB]
+SECOND = [FIELD, SLAB, ROWS, (56, 256)]
+
+
+def load(source, couplings, diag_block, line_inverse, adjoint):
+    vmem = pl.BlockSpec(memory_space=pltpu.VMEM)
+    operands = [
+        pltpu.with_memory_space_constraint(x, pltpu.HBM) for x in (source, couplings, diag_block, line_inverse, adjoint)
+    ]
+    held = [pltpu.VMEM(x.shape, x.dtype) for x in (adjoint, couplings, source, diag_block, line_inverse)]
+    return pl.pallas_call(
+        load_kernel,
+        name="load",
+        out_shape=[*held, *(pltpu.VMEM(s, F32) for s in FIRST)],
+        in_specs=[pl.BlockSpec(memory_space=pltpu.HBM)] * 5,
+        out_specs=[vmem] * 8,
+        scratch_shapes=[pltpu.SemaphoreType.DMA((8,))],
+        compiler_params=pltpu.CompilerParams(vmem_limit_bytes=VMEM_LIMIT),
+        cost_estimate=pl.CostEstimate(flops=1_000_000, bytes_accessed=0, transcendentals=0),
+    )(*operands)
 
 
 def wall_masks(partner, codes):
@@ -177,18 +237,20 @@
     found = []
     for i in range(start, count - 1, 2):
         found += [(i, i + 1), (i + 1, i)]
+    if start:
+        found += [(0, count - 1), (count - 1, 0)]
     return found
 
 
 def exchange(sent):
-    chord_even, chord_odd, span_even, span_odd, cut = sent
+    cut, chord_odd, chord_even, span_odd, span_even = sent
     chords, spans = lax.axis_size("chord"), lax.axis_size("span")
     cut = lax.ppermute(cut, "chord", [(i, chords - 1 - i) for i in range(chords)])
     chord_odd = lax.ppermute(chord_odd, "chord", pairs(chords, 1))
+    chord_even = lax.ppermute(chord_even, "chord", pairs(chords, 0))
     span_odd = lax.ppermute(span_odd, "span", pairs(spans, 1))
-    chord_even = lax.ppermute(chord_even, "chord", pairs(chords, 0))
     span_even = lax.ppermute(span_even, "span", pairs(spans, 0))
-    return chord_even, chord_odd, span_even, span_odd, cut
+    return cut, chord_odd, chord_even, span_odd, span_even
 
 
 def per_device(adjoint, source, diag_block, couplings, line_inverse, partner, codes):
@@ -198,17 +260,19 @@
     couplings = couplings.reshape(6, 6, 6, 16, 256)
     line_inverse = line_inverse.reshape(6, 6, 2, 16, 256)
     masks = wall_masks(partner, codes)
-    part, *sent = call(first_kernel, "first_edges", (source, couplings, adjoint), SENT, 5_000_000)
+    adjoint, couplings, source, diag_block, line_inverse, *far = load(
+        source, couplings, diag_block, line_inverse, adjoint
+    )
     for sweep in range(SWEEPS):
-        got = exchange(sent)
-        [part] = call(inside_kernel, "inside", (part, diag_block, couplings, adjoint), [FIELD], 4_000_000)
+        cut, chord_odd, held = far
+        part, *near = call(edges_kernel, "edges", (adjoint, source, couplings, held), SECOND, 1_000)
+        got = exchange((cut, chord_odd, *near))
+        [part] = call(inside_kernel, "inside", (part, diag_block, couplings, adjoint), [FIELD], 20_000_000_000)
         arguments = (part, *got, masks, line_inverse, adjoint)
         if sweep < SWEEPS - 1:
-            adjoint, part, *sent = call(
-                middle_kernel, "sweep", (*arguments, source, couplings), [FIELD, *SENT], 8_000_000
-            )
+            adjoint, *far = call(middle_kernel, "sweep", (*arguments, couplings), [FIELD, *FIRST], 1_000)
         else:
-            adjoint, residual = call(last_kernel, "last", arguments, [FIELD, FIELD], 3_000_000, False)
+            adjoint, residual = call(last_kernel, "last", arguments, [FIELD, FIELD], 1_000, False)
     return adjoint.reshape(6, 2, 8, 256), residual.reshape(6, 2, 8, 256)
 
 

time: 108 us -> 82 us (0.76)
  the two profiles are of different devices: /device:TPU:184 before, /device:TPU:8 now
where the time goes in v2:
time: 82 us; the launch traced here: 81.8 us
  starting transfers between devices  49.8 us (61%)
  waiting for transfers between devices  23.4 us (29%)
  Pallas kernels  7.47 us (9%)
    ppermute x6, starting transfers between devices, exchange(): lax.ppermute(cut, 'chord', [(i, chords - 1 - i) for i in range(chords)])  25.2 us
    ppermute x6, starting transfers between devices, exchange(): chord_odd = lax.ppermute(chord_odd, 'chord', pairs(chords, 1))  15.1 us
    ppermute x6, waiting for transfers between devices, exchange(): span_odd = lax.ppermute(span_odd, 'span', pairs(spans, 1))  13.7 us
    ppermute x6, waiting for transfers between devices, exchange(): chord_odd = lax.ppermute(chord_odd, 'chord', pairs(chords, 1))  8.98 us
    ppermute x6, starting transfers between devices, exchange(): span_even = lax.ppermute(span_even, 'span', pairs(spans, 0))  6.75 us
    pallas_call x18, Pallas kernels, call(): pl.pallas_call(kernel, name=name, out_shape=made, in_specs=[vmem] * len(h...  5.62 us
    pallas_call x1, Pallas kernels, load(): pl.pallas_call(load_kernel, name='load', out_shape=[*held, *(pltpu.VMEM(s...  1.85 us
    ppermute x6, starting transfers between devices, exchange(): span_odd = lax.ppermute(span_odd, 'span', pairs(spans, 1))  1.78 us
  transfers between devices with their start and end apart: 30, of which 13 were waited for; matrix products, arithmetic and copies ran while one was open for 0% of the time, Pallas kernels for 3%

profile of v2, /device:TPU:8, one launch (start us, length us, event | category | flops | bytes accessed | tf_op | source)
XLA Modules:
  0.0 81.8 jit_solution(18043609827749714131)
XLA Ops:
  0.7 1.9 %load.1 = (f32[6,16,256]{2,1,0:T(8,128)S(1)}, bf16[6,6,6,16,256]{4,3,2,1,0:T(8,128)(2,1)S(1)}, f32[6,16,256]{2,1,0:T(8,128)S(1)}, bf16[6,6,16,256]{3,2,1,0:T(8,1...) custom-call(f32[6,16,256]{2,1,0:T(8,128)} %bitcast.10, ...), custom_call_target="tpu_custom_call" | custom-call | flops 1000000 | tf_op jit(solution)/shard_map/load/pallas_call | solution.py:217
  2.5 8.6 %collective-permute-start = (f32[8,128]{1,0:T(8,128)S(1)}, f32[8,128]{1,0:T(8,128)S(1)}, u32[]{:S(2)}, u32[]{:S(2)}) collective-permute-start(f32[8,128]{1,0:T(8,128)S(1)} %get-tuple-element.62), channel_id=1, source_target_pairs={{0,240},{16,224},{32,208},{48,192},{64,176},{80,160},{96,144},{112... | collective-permute-start | bytes 12296 | tf_op jit(solution)/shard_map/ppermute | solution.py:248
  11.5 0.7 collective-permute-start.2
  12.2 0.8 collective-permute-start.4
  13.6 2.5 %collective-permute-done.3.span_odd = f32[16,256]{1,0:T(8,128)S(1)} collective-permute-done((f32[16,256]{1,0:T(8,128)S(1)}, f32[16,256]{1,0:T(8,128)S(1)}, u32[]{:S(2)}, u32[]{:S(2)}) %collective-permute-start.3) | collective-permute-done | bytes 16416 | tf_op jit(solution)/shard_map/ppermute | solution.py:251
  16.0 3.4 %collective-permute-done.1.chord_odd = f32[6,8,256]{2,1,0:T(8,128)S(1)} collective-permute-done((f32[6,8,256]{2,1,0:T(8,128)S(1)}, f32[6,8,256]{2,1,0:T(8,128)S(1)}, u32[]{:S(2)}, u32[]{:S(2)}) %collective-permute-start.1) | collective-permute-done | bytes 49184 | tf_op jit(solution)/shard_map/ppermute | solution.py:249
  19.9 2.9 %collective-permute-start.5 = (f32[8,128]{1,0:T(8,128)S(1)}, f32[8,128]{1,0:T(8,128)S(1)}, u32[]{:S(2)}, u32[]{:S(2)}) collective-permute-start(f32[8,128]{1,0:T(8,128)S(1)} %get-tuple-element.71), channel_id=1, source_target_pairs={{0,240},{16,224},{32,208},{48,192},{64,176},{80,160},{96,144},{112... | collective-permute-start | bytes 12296 | tf_op jit(solution)/shard_map/ppermute | solution.py:248
  22.9 3.4 %collective-permute-start.6 = (f32[6,8,256]{2,1,0:T(8,128)S(1)}, f32[6,8,256]{2,1,0:T(8,128)S(1)}, u32[]{:S(2)}, u32[]{:S(2)}) collective-permute-start(f32[6,8,256]{2,1,0:T(8,128)S(1)} %get-tuple-element.72), channel_id=1, source_target_pairs={{16,32},{32,16},{48,64},{64,48},{80,96},{96,80},{112,128},{128,112... | collective-permute-start | bytes 147464 | tf_op jit(solution)/shard_map/ppermute | solution.py:249
  26.6 1.5 %collective-permute-start.9 = (f32[56,256]{1,0:T(8,128)S(1)}, f32[56,256]{1,0:T(8,128)S(1)}, u32[]{:S(2)}, u32[]{:S(2)}) collective-permute-start(f32[56,256]{1,0:T(8,128)S(1)} %get-tuple-element.75), channel_id=1, source_target_pairs={{0,1},{1,0},{2,3},{3,2},{4,5},{5,4},{6,7},{7,6},{8,9},{9,8},{10,11... | collective-permute-start | bytes 172040 | tf_op jit(solution)/shard_map/ppermute | solution.py:252
  28.4 2.1 %collective-permute-done.8.span_odd = f32[16,256]{1,0:T(8,128)S(1)} collective-permute-done((f32[16,256]{1,0:T(8,128)S(1)}, f32[16,256]{1,0:T(8,128)S(1)}, u32[]{:S(2)}, u32[]{:S(2)}) %collective-permute-start.8) | collective-permute-done | bytes 16416 | tf_op jit(solution)/shard_map/ppermute | solution.py:251
  30.6 1.0 %collective-permute-done.6.chord_odd = f32[6,8,256]{2,1,0:T(8,128)S(1)} collective-permute-done((f32[6,8,256]{2,1,0:T(8,128)S(1)}, f32[6,8,256]{2,1,0:T(8,128)S(1)}, u32[]{:S(2)}, u32[]{:S(2)}) %collective-permute-start.6) | collective-permute-done | bytes 49184 | tf_op jit(solution)/shard_map/ppermute | solution.py:249
  32.0 3.1 %collective-permute-start.10 = (f32[8,128]{1,0:T(8,128)S(1)}, f32[8,128]{1,0:T(8,128)S(1)}, u32[]{:S(2)}, u32[]{:S(2)}) collective-permute-start(f32[8,128]{1,0:T(8,128)S(1)} %get-tuple-element.79), channel_id=1, source_target_pairs={{0,240},{16,224},{32,208},{48,192},{64,176},{80,160},{96,144},{112... | collective-permute-start | bytes 12296 | tf_op jit(solution)/shard_map/ppermute | solution.py:248
  35.1 3.2 %collective-permute-start.11 = (f32[6,8,256]{2,1,0:T(8,128)S(1)}, f32[6,8,256]{2,1,0:T(8,128)S(1)}, u32[]{:S(2)}, u32[]{:S(2)}) collective-permute-start(f32[6,8,256]{2,1,0:T(8,128)S(1)} %get-tuple-element.80), channel_id=1, source_target_pairs={{16,32},{32,16},{48,64},{64,48},{80,96},{96,80},{112,128},{128,112... | collective-permute-start | bytes 147464 | tf_op jit(solution)/shard_map/ppermute | solution.py:249
  38.7 1.1 %collective-permute-start.14 = (f32[56,256]{1,0:T(8,128)S(1)}, f32[56,256]{1,0:T(8,128)S(1)}, u32[]{:S(2)}, u32[]{:S(2)}) collective-permute-start(f32[56,256]{1,0:T(8,128)S(1)} %get-tuple-element.83), channel_id=1, source_target_pairs={{0,1},{1,0},{2,3},{3,2},{4,5},{5,4},{6,7},{7,6},{8,9},{9,8},{10,11... | collective-permute-start | bytes 172040 | tf_op jit(solution)/shard_map/ppermute | solution.py:252
  40.1 2.6 %collective-permute-done.13.span_odd = f32[16,256]{1,0:T(8,128)S(1)} collective-permute-done((f32[16,256]{1,0:T(8,128)S(1)}, f32[16,256]{1,0:T(8,128)S(1)}, u32[]{:S(2)}, u32[]{:S(2)}) %collective-permute-start.13) | collective-permute-done | bytes 16416 | tf_op jit(solution)/shard_map/ppermute | solution.py:251
  42.6 0.8 collective-permute-done.11.chord_odd
  43.9 4.0 %collective-permute-start.15 = (f32[8,128]{1,0:T(8,128)S(1)}, f32[8,128]{1,0:T(8,128)S(1)}, u32[]{:S(2)}, u32[]{:S(2)}) collective-permute-start(f32[8,128]{1,0:T(8,128)S(1)} %get-tuple-element.87), channel_id=1, source_target_pairs={{0,240},{16,224},{32,208},{48,192},{64,176},{80,160},{96,144},{112... | collective-permute-start | bytes 12296 | tf_op jit(solution)/shard_map/ppermute | solution.py:248
  47.9 2.3 %collective-permute-start.16 = (f32[6,8,256]{2,1,0:T(8,128)S(1)}, f32[6,8,256]{2,1,0:T(8,128)S(1)}, u32[]{:S(2)}, u32[]{:S(2)}) collective-permute-start(f32[6,8,256]{2,1,0:T(8,128)S(1)} %get-tuple-element.88), channel_id=1, source_target_pairs={{16,32},{32,16},{48,64},{64,48},{80,96},{96,80},{112,128},{128,112... | collective-permute-start | bytes 147464 | tf_op jit(solution)/shard_map/ppermute | solution.py:249
  50.9 1.6 %collective-permute-start.19 = (f32[56,256]{1,0:T(8,128)S(1)}, f32[56,256]{1,0:T(8,128)S(1)}, u32[]{:S(2)}, u32[]{:S(2)}) collective-permute-start(f32[56,256]{1,0:T(8,128)S(1)} %get-tuple-element.91), channel_id=1, source_target_pairs={{0,1},{1,0},{2,3},{3,2},{4,5},{5,4},{6,7},{7,6},{8,9},{9,8},{10,11... | collective-permute-start | bytes 172040 | tf_op jit(solution)/shard_map/ppermute | solution.py:252
  52.8 1.7 %collective-permute-done.18.span_odd = f32[16,256]{1,0:T(8,128)S(1)} collective-permute-done((f32[16,256]{1,0:T(8,128)S(1)}, f32[16,256]{1,0:T(8,128)S(1)}, u32[]{:S(2)}, u32[]{:S(2)}) %collective-permute-start.18) | collective-permute-done | bytes 16416 | tf_op jit(solution)/shard_map/ppermute | solution.py:251
  54.6 1.8 %collective-permute-done.16.chord_odd = f32[6,8,256]{2,1,0:T(8,128)S(1)} collective-permute-done((f32[6,8,256]{2,1,0:T(8,128)S(1)}, f32[6,8,256]{2,1,0:T(8,128)S(1)}, u32[]{:S(2)}, u32[]{:S(2)}) %collective-permute-start.16) | collective-permute-done | bytes 49184 | tf_op jit(solution)/shard_map/ppermute | solution.py:249
  56.8 2.3 %collective-permute-start.20 = (f32[8,128]{1,0:T(8,128)S(1)}, f32[8,128]{1,0:T(8,128)S(1)}, u32[]{:S(2)}, u32[]{:S(2)}) collective-permute-start(f32[8,128]{1,0:T(8,128)S(1)} %get-tuple-element.95), channel_id=1, source_target_pairs={{0,240},{16,224},{32,208},{48,192},{64,176},{80,160},{96,144},{112... | collective-permute-start | bytes 12296 | tf_op jit(solution)/shard_map/ppermute | solution.py:248
  59.1 4.0 %collective-permute-start.21 = (f32[6,8,256]{2,1,0:T(8,128)S(1)}, f32[6,8,256]{2,1,0:T(8,128)S(1)}, u32[]{:S(2)}, u32[]{:S(2)}) collective-permute-start(f32[6,8,256]{2,1,0:T(8,128)S(1)} %get-tuple-element.96), channel_id=1, source_target_pairs={{16,32},{32,16},{48,64},{64,48},{80,96},{96,80},{112,128},{128,112... | collective-permute-start | bytes 147464 | tf_op jit(solution)/shard_map/ppermute | solution.py:249
  63.5 0.6 collective-permute-start.24
  64.8 2.7 %collective-permute-done.23.span_odd = f32[16,256]{1,0:T(8,128)S(1)} collective-permute-done((f32[16,256]{1,0:T(8,128)S(1)}, f32[16,256]{1,0:T(8,128)S(1)}, u32[]{:S(2)}, u32[]{:S(2)}) %collective-permute-start.23) | collective-permute-done | bytes 16416 | tf_op jit(solution)/shard_map/ppermute | solution.py:251
  68.2 4.3 %collective-permute-start.25 = (f32[8,128]{1,0:T(8,128)S(1)}, f32[8,128]{1,0:T(8,128)S(1)}, u32[]{:S(2)}, u32[]{:S(2)}) collective-permute-start(f32[8,128]{1,0:T(8,128)S(1)} %get-tuple-element.103), channel_id=1, source_target_pairs={{0,240},{16,224},{32,208},{48,192},{64,176},{80,160},{96,144},{112... | collective-permute-start | bytes 12296 | tf_op jit(solution)/shard_map/ppermute | solution.py:248
  72.5 2.0 %collective-permute-start.26 = (f32[6,8,256]{2,1,0:T(8,128)S(1)}, f32[6,8,256]{2,1,0:T(8,128)S(1)}, u32[]{:S(2)}, u32[]{:S(2)}) collective-permute-start(f32[6,8,256]{2,1,0:T(8,128)S(1)} %get-tuple-element.104), channel_id=1, source_target_pairs={{16,32},{32,16},{48,64},{64,48},{80,96},{96,80},{112,128},{128,112... | collective-permute-start | bytes 147464 | tf_op jit(solution)/shard_map/ppermute | solution.py:249
  74.7 0.7 collective-permute-start.28
  75.5 1.1 %collective-permute-start.29 = (f32[56,256]{1,0:T(8,128)S(1)}, f32[56,256]{1,0:T(8,128)S(1)}, u32[]{:S(2)}, u32[]{:S(2)}) collective-permute-start(f32[56,256]{1,0:T(8,128)S(1)} %get-tuple-element.107), channel_id=1, source_target_pairs={{0,1},{1,0},{2,3},{3,2},{4,5},{5,4},{6,7},{7,6},{8,9},{9,8},{10,11... | collective-permute-start | bytes 172040 | tf_op jit(solution)/shard_map/ppermute | solution.py:252
  76.8 2.1 %collective-permute-done.28.span_odd = f32[16,256]{1,0:T(8,128)S(1)} collective-permute-done((f32[16,256]{1,0:T(8,128)S(1)}, f32[16,256]{1,0:T(8,128)S(1)}, u32[]{:S(2)}, u32[]{:S(2)}) %collective-permute-start.28) | collective-permute-done | bytes 16416 | tf_op jit(solution)/shard_map/ppermute | solution.py:251
  78.9 2.0 %collective-permute-done.26.chord_odd = f32[6,8,256]{2,1,0:T(8,128)S(1)} collective-permute-done((f32[6,8,256]{2,1,0:T(8,128)S(1)}, f32[6,8,256]{2,1,0:T(8,128)S(1)}, u32[]{:S(2)}, u32[]{:S(2)}) %collective-permute-start.26) | collective-permute-done | bytes 49184 | tf_op jit(solution)/shard_map/ppermute | solution.py:249
  80.9 0.9 %last.1 = (f32[6,16,256]{2,1,0:T(8,128)}, f32[6,16,256]{2,1,0:T(8,128)}) custom-call(f32[6,16,256]{2,1,0:T(8,128)S(1)} %inside.11.part, f32[8,128]{1,0:T(8,128)S(1)} %collective-permute-done.25.cut, f32[6,8,256]{2,1,0:T(8,128)S(1)} %collective-permute-done.26.chord_odd, f32[6,8,256]{2,1,0:T(8,128)S(1)} %collective-permute-done.27.chord_even, ...), custom_call_target="tpu_custom_call" | custom-call | flops 1000 | tf_op jit(solution)/shard_map/last/pallas_call | solution.py:193
  (59 shorter events, 7.1 us)
Async XLA Ops:
  0.6 12.3 %copy-start.1 = (s32[2]{0:T(128)S(1)}, s32[2]{0:T(128)}, u32[]{:S(2)}) copy-start(s32[2]{0:T(128)} %param.12) | copy-start | bytes 28
  0.6 12.5 %copy-start = (s32[2,8]{1,0:T(2,128)S(1)}, s32[2,8]{1,0:T(2,128)}, u32[]{:S(2)}) copy-start(s32[2,8]{1,0:T(2,128)} %param.13) | copy-start | bytes 196
  2.5 11.0 %collective-permute-start = (f32[8,128]{1,0:T(8,128)S(1)}, f32[8,128]{1,0:T(8,128)S(1)}, u32[]{:S(2)}, u32[]{:S(2)}) collective-permute-start(f32[8,128]{1,0:T(8,128)S(1)} %get-tuple-element.62), channel_id=1, source_target_pairs={{0,240},{16,224},{32,208},{48,192},{64,176},{80,160},{96,144},{112... | collective-permute-start | bytes 12296 | tf_op jit(solution)/shard_map/ppermute | solution.py:248
  11.1 8.3 %collective-permute-start.1 = (f32[6,8,256]{2,1,0:T(8,128)S(1)}, f32[6,8,256]{2,1,0:T(8,128)S(1)}, u32[]{:S(2)}, u32[]{:S(2)}) collective-permute-start(f32[6,8,256]{2,1,0:T(8,128)S(1)} %get-tuple-element.63), channel_id=1, source_target_pairs={{16,32},{32,16},{48,64},{64,48},{80,96},{96,80},{112,128},{128,112... | collective-permute-start | bytes 147464 | tf_op jit(solution)/shard_map/ppermute | solution.py:249
  11.4 4.7 %collective-permute-start.3 = (f32[16,256]{1,0:T(8,128)S(1)}, f32[16,256]{1,0:T(8,128)S(1)}, u32[]{:S(2)}, u32[]{:S(2)}) collective-permute-start(f32[16,256]{1,0:T(8,128)S(1)} %get-tuple-element.65), channel_id=1, source_target_pairs={{1,2},{2,1},{3,4},{4,3},{5,6},{6,5},{7,8},{8,7},{9,10},{10,9},{11,... | collective-permute-start | bytes 49160 | tf_op jit(solution)/shard_map/ppermute | solution.py:251
  11.5 7.9 %collective-permute-start.2 = (f32[6,8,256]{2,1,0:T(8,128)S(1)}, f32[6,8,256]{2,1,0:T(8,128)S(1)}, u32[]{:S(2)}, u32[]{:S(2)}) collective-permute-start(f32[6,8,256]{2,1,0:T(8,128)S(1)} %get-tuple-element.64), channel_id=1, source_target_pairs={{0,16},{16,0},{32,48},{48,32},{64,80},{80,64},{96,112},{112,96},{1... | collective-permute-start | bytes 147464 | tf_op jit(solution)/shard_map/ppermute | solution.py:250
  12.2 7.2 %collective-permute-start.4 = (f32[56,256]{1,0:T(8,128)S(1)}, f32[56,256]{1,0:T(8,128)S(1)}, u32[]{:S(2)}, u32[]{:S(2)}) collective-permute-start(f32[56,256]{1,0:T(8,128)S(1)} %get-tuple-element.66), channel_id=1, source_target_pairs={{0,1},{1,0},{2,3},{3,2},{4,5},{5,4},{6,7},{7,6},{8,9},{9,8},{10,11... | collective-permute-start | bytes 172040 | tf_op jit(solution)/shard_map/ppermute | solution.py:252
  19.9 8.5 %collective-permute-start.5 = (f32[8,128]{1,0:T(8,128)S(1)}, f32[8,128]{1,0:T(8,128)S(1)}, u32[]{:S(2)}, u32[]{:S(2)}) collective-permute-start(f32[8,128]{1,0:T(8,128)S(1)} %get-tuple-element.71), channel_id=1, source_target_pairs={{0,240},{16,224},{32,208},{48,192},{64,176},{80,160},{96,144},{112... | collective-permute-start | bytes 12296 | tf_op jit(solution)/shard_map/ppermute | solution.py:248
  22.9 8.7 %collective-permute-start.6 = (f32[6,8,256]{2,1,0:T(8,128)S(1)}, f32[6,8,256]{2,1,0:T(8,128)S(1)}, u32[]{:S(2)}, u32[]{:S(2)}) collective-permute-start(f32[6,8,256]{2,1,0:T(8,128)S(1)} %get-tuple-element.72), channel_id=1, source_target_pairs={{16,32},{32,16},{48,64},{64,48},{80,96},{96,80},{112,128},{128,112... | collective-permute-start | bytes 147464 | tf_op jit(solution)/shard_map/ppermute | solution.py:249
  26.4 4.2 %collective-permute-start.8 = (f32[16,256]{1,0:T(8,128)S(1)}, f32[16,256]{1,0:T(8,128)S(1)}, u32[]{:S(2)}, u32[]{:S(2)}) collective-permute-start(f32[16,256]{1,0:T(8,128)S(1)} %get-tuple-element.74), channel_id=1, source_target_pairs={{1,2},{2,1},{3,4},{4,3},{5,6},{6,5},{7,8},{8,7},{9,10},{10,9},{11,... | collective-permute-start | bytes 49160 | tf_op jit(solution)/shard_map/ppermute | solution.py:251
  26.5 5.0 %collective-permute-start.7 = (f32[6,8,256]{2,1,0:T(8,128)S(1)}, f32[6,8,256]{2,1,0:T(8,128)S(1)}, u32[]{:S(2)}, u32[]{:S(2)}) collective-permute-start(f32[6,8,256]{2,1,0:T(8,128)S(1)} %get-tuple-element.73), channel_id=1, source_target_pairs={{0,16},{16,0},{32,48},{48,32},{64,80},{80,64},{96,112},{112,96},{1... | collective-permute-start | bytes 147464 | tf_op jit(solution)/shard_map/ppermute | solution.py:250
  26.6 4.9 %collective-permute-start.9 = (f32[56,256]{1,0:T(8,128)S(1)}, f32[56,256]{1,0:T(8,128)S(1)}, u32[]{:S(2)}, u32[]{:S(2)}) collective-permute-start(f32[56,256]{1,0:T(8,128)S(1)} %get-tuple-element.75), channel_id=1, source_target_pairs={{0,1},{1,0},{2,3},{3,2},{4,5},{5,4},{6,7},{7,6},{8,9},{9,8},{10,11... | collective-permute-start | bytes 172040 | tf_op jit(solution)/shard_map/ppermute | solution.py:252
  32.0 8.1 %collective-permute-start.10 = (f32[8,128]{1,0:T(8,128)S(1)}, f32[8,128]{1,0:T(8,128)S(1)}, u32[]{:S(2)}, u32[]{:S(2)}) collective-permute-start(f32[8,128]{1,0:T(8,128)S(1)} %get-tuple-element.79), channel_id=1, source_target_pairs={{0,240},{16,224},{32,208},{48,192},{64,176},{80,160},{96,144},{112... | collective-permute-start | bytes 12296 | tf_op jit(solution)/shard_map/ppermute | solution.py:248
  35.1 8.4 %collective-permute-start.11 = (f32[6,8,256]{2,1,0:T(8,128)S(1)}, f32[6,8,256]{2,1,0:T(8,128)S(1)}, u32[]{:S(2)}, u32[]{:S(2)}) collective-permute-start(f32[6,8,256]{2,1,0:T(8,128)S(1)} %get-tuple-element.80), channel_id=1, source_target_pairs={{16,32},{32,16},{48,64},{64,48},{80,96},{96,80},{112,128},{128,112... | collective-permute-start | bytes 147464 | tf_op jit(solution)/shard_map/ppermute | solution.py:249
  38.5 4.2 %collective-permute-start.13 = (f32[16,256]{1,0:T(8,128)S(1)}, f32[16,256]{1,0:T(8,128)S(1)}, u32[]{:S(2)}, u32[]{:S(2)}) collective-permute-start(f32[16,256]{1,0:T(8,128)S(1)} %get-tuple-element.82), channel_id=1, source_target_pairs={{1,2},{2,1},{3,4},{4,3},{5,6},{6,5},{7,8},{8,7},{9,10},{10,9},{11,... | collective-permute-start | bytes 49160 | tf_op jit(solution)/shard_map/ppermute | solution.py:251
  38.7 4.8 %collective-permute-start.12 = (f32[6,8,256]{2,1,0:T(8,128)S(1)}, f32[6,8,256]{2,1,0:T(8,128)S(1)}, u32[]{:S(2)}, u32[]{:S(2)}) collective-permute-start(f32[6,8,256]{2,1,0:T(8,128)S(1)} %get-tuple-element.81), channel_id=1, source_target_pairs={{0,16},{16,0},{32,48},{48,32},{64,80},{80,64},{96,112},{112,96},{1... | collective-permute-start | bytes 147464 | tf_op jit(solution)/shard_map/ppermute | solution.py:250
  38.7 4.8 %collective-permute-start.14 = (f32[56,256]{1,0:T(8,128)S(1)}, f32[56,256]{1,0:T(8,128)S(1)}, u32[]{:S(2)}, u32[]{:S(2)}) collective-permute-start(f32[56,256]{1,0:T(8,128)S(1)} %get-tuple-element.83), channel_id=1, source_target_pairs={{0,1},{1,0},{2,3},{3,2},{4,5},{5,4},{6,7},{7,6},{8,9},{9,8},{10,11... | collective-permute-start | bytes 172040 | tf_op jit(solution)/shard_map/ppermute | solution.py:252
  43.9 8.9 %collective-permute-start.15 = (f32[8,128]{1,0:T(8,128)S(1)}, f32[8,128]{1,0:T(8,128)S(1)}, u32[]{:S(2)}, u32[]{:S(2)}) collective-permute-start(f32[8,128]{1,0:T(8,128)S(1)} %get-tuple-element.87), channel_id=1, source_target_pairs={{0,240},{16,224},{32,208},{48,192},{64,176},{80,160},{96,144},{112... | collective-permute-start | bytes 12296 | tf_op jit(solution)/shard_map/ppermute | solution.py:248
  47.9 8.5 %collective-permute-start.16 = (f32[6,8,256]{2,1,0:T(8,128)S(1)}, f32[6,8,256]{2,1,0:T(8,128)S(1)}, u32[]{:S(2)}, u32[]{:S(2)}) collective-permute-start(f32[6,8,256]{2,1,0:T(8,128)S(1)} %get-tuple-element.88), channel_id=1, source_target_pairs={{16,32},{32,16},{48,64},{64,48},{80,96},{96,80},{112,128},{128,112... | collective-permute-start | bytes 147464 | tf_op jit(solution)/shard_map/ppermute | solution.py:249
  50.4 4.2 %collective-permute-start.18 = (f32[16,256]{1,0:T(8,128)S(1)}, f32[16,256]{1,0:T(8,128)S(1)}, u32[]{:S(2)}, u32[]{:S(2)}) collective-permute-start(f32[16,256]{1,0:T(8,128)S(1)} %get-tuple-element.90), channel_id=1, source_target_pairs={{1,2},{2,1},{3,4},{4,3},{5,6},{6,5},{7,8},{8,7},{9,10},{10,9},{11,... | collective-permute-start | bytes 49160 | tf_op jit(solution)/shard_map/ppermute | solution.py:251
  50.9 5.5 %collective-permute-start.17 = (f32[6,8,256]{2,1,0:T(8,128)S(1)}, f32[6,8,256]{2,1,0:T(8,128)S(1)}, u32[]{:S(2)}, u32[]{:S(2)}) collective-permute-start(f32[6,8,256]{2,1,0:T(8,128)S(1)} %get-tuple-element.89), channel_id=1, source_target_pairs={{0,16},{16,0},{32,48},{48,32},{64,80},{80,64},{96,112},{112,96},{1... | collective-permute-start | bytes 147464 | tf_op jit(solution)/shard_map/ppermute | solution.py:250
  50.9 5.5 %collective-permute-start.19 = (f32[56,256]{1,0:T(8,128)S(1)}, f32[56,256]{1,0:T(8,128)S(1)}, u32[]{:S(2)}, u32[]{:S(2)}) collective-permute-start(f32[56,256]{1,0:T(8,128)S(1)} %get-tuple-element.91), channel_id=1, source_target_pairs={{0,1},{1,0},{2,3},{3,2},{4,5},{5,4},{6,7},{7,6},{8,9},{9,8},{10,11... | collective-permute-start | bytes 172040 | tf_op jit(solution)/shard_map/ppermute | solution.py:252
  56.8 7.9 %collective-permute-start.20 = (f32[8,128]{1,0:T(8,128)S(1)}, f32[8,128]{1,0:T(8,128)S(1)}, u32[]{:S(2)}, u32[]{:S(2)}) collective-permute-start(f32[8,128]{1,0:T(8,128)S(1)} %get-tuple-element.95), channel_id=1, source_target_pairs={{0,240},{16,224},{32,208},{48,192},{64,176},{80,160},{96,144},{112... | collective-permute-start | bytes 12296 | tf_op jit(solution)/shard_map/ppermute | solution.py:248
  59.1 8.4 %collective-permute-start.21 = (f32[6,8,256]{2,1,0:T(8,128)S(1)}, f32[6,8,256]{2,1,0:T(8,128)S(1)}, u32[]{:S(2)}, u32[]{:S(2)}) collective-permute-start(f32[6,8,256]{2,1,0:T(8,128)S(1)} %get-tuple-element.96), channel_id=1, source_target_pairs={{16,32},{32,16},{48,64},{64,48},{80,96},{96,80},{112,128},{128,112... | collective-permute-start | bytes 147464 | tf_op jit(solution)/shard_map/ppermute | solution.py:249
  63.3 4.2 %collective-permute-start.23 = (f32[16,256]{1,0:T(8,128)S(1)}, f32[16,256]{1,0:T(8,128)S(1)}, u32[]{:S(2)}, u32[]{:S(2)}) collective-permute-start(f32[16,256]{1,0:T(8,128)S(1)} %get-tuple-element.98), channel_id=1, source_target_pairs={{1,2},{2,1},{3,4},{4,3},{5,6},{6,5},{7,8},{8,7},{9,10},{10,9},{11,... | collective-permute-start | bytes 49160 | tf_op jit(solution)/shard_map/ppermute | solution.py:251
  63.4 4.4 %collective-permute-start.22 = (f32[6,8,256]{2,1,0:T(8,128)S(1)}, f32[6,8,256]{2,1,0:T(8,128)S(1)}, u32[]{:S(2)}, u32[]{:S(2)}) collective-permute-start(f32[6,8,256]{2,1,0:T(8,128)S(1)} %get-tuple-element.97), channel_id=1, source_target_pairs={{0,16},{16,0},{32,48},{48,32},{64,80},{80,64},{96,112},{112,96},{1... | collective-permute-start | bytes 147464 | tf_op jit(solution)/shard_map/ppermute | solution.py:250
  63.5 4.3 %collective-permute-start.24 = (f32[56,256]{1,0:T(8,128)S(1)}, f32[56,256]{1,0:T(8,128)S(1)}, u32[]{:S(2)}, u32[]{:S(2)}) collective-permute-start(f32[56,256]{1,0:T(8,128)S(1)} %get-tuple-element.99), channel_id=1, source_target_pairs={{0,1},{1,0},{2,3},{3,2},{4,5},{5,4},{6,7},{7,6},{8,9},{9,8},{10,11... | collective-permute-start | bytes 172040 | tf_op jit(solution)/shard_map/ppermute | solution.py:252
  68.2 8.6 %collective-permute-start.25 = (f32[8,128]{1,0:T(8,128)S(1)}, f32[8,128]{1,0:T(8,128)S(1)}, u32[]{:S(2)}, u32[]{:S(2)}) collective-permute-start(f32[8,128]{1,0:T(8,128)S(1)} %get-tuple-element.103), channel_id=1, source_target_pairs={{0,240},{16,224},{32,208},{48,192},{64,176},{80,160},{96,144},{112... | collective-permute-start | bytes 12296 | tf_op jit(solution)/shard_map/ppermute | solution.py:248
  72.5 8.3 %collective-permute-start.26 = (f32[6,8,256]{2,1,0:T(8,128)S(1)}, f32[6,8,256]{2,1,0:T(8,128)S(1)}, u32[]{:S(2)}, u32[]{:S(2)}) collective-permute-start(f32[6,8,256]{2,1,0:T(8,128)S(1)} %get-tuple-element.104), channel_id=1, source_target_pairs={{16,32},{32,16},{48,64},{64,48},{80,96},{96,80},{112,128},{128,112... | collective-permute-start | bytes 147464 | tf_op jit(solution)/shard_map/ppermute | solution.py:249
  74.7 4.2 %collective-permute-start.28 = (f32[16,256]{1,0:T(8,128)S(1)}, f32[16,256]{1,0:T(8,128)S(1)}, u32[]{:S(2)}, u32[]{:S(2)}) collective-permute-start(f32[16,256]{1,0:T(8,128)S(1)} %get-tuple-element.106), channel_id=1, source_target_pairs={{1,2},{2,1},{3,4},{4,3},{5,6},{6,5},{7,8},{8,7},{9,10},{10,9},{11,... | collective-permute-start | bytes 49160 | tf_op jit(solution)/shard_map/ppermute | solution.py:251
  75.5 5.4 %collective-permute-start.27 = (f32[6,8,256]{2,1,0:T(8,128)S(1)}, f32[6,8,256]{2,1,0:T(8,128)S(1)}, u32[]{:S(2)}, u32[]{:S(2)}) collective-permute-start(f32[6,8,256]{2,1,0:T(8,128)S(1)} %get-tuple-element.105), channel_id=1, source_target_pairs={{0,16},{16,0},{32,48},{48,32},{64,80},{80,64},{96,112},{112,96},{1... | collective-permute-start | bytes 147464 | tf_op jit(solution)/shard_map/ppermute | solution.py:250
  75.5 5.4 %collective-permute-start.29 = (f32[56,256]{1,0:T(8,128)S(1)}, f32[56,256]{1,0:T(8,128)S(1)}, u32[]{:S(2)}, u32[]{:S(2)}) collective-permute-start(f32[56,256]{1,0:T(8,128)S(1)} %get-tuple-element.107), channel_id=1, source_target_pairs={{0,1},{1,0},{2,3},{3,2},{4,5},{5,4},{6,7},{7,6},{8,9},{9,8},{10,11... | collective-permute-start | bytes 172040 | tf_op jit(solution)/shard_map/ppermute | solution.py:252

commit v3 on v2

--- a/solution.py
+++ b/solution.py
@@ -8,6 +8,7 @@
 SWEEPS = 6
 F32 = jnp.float32
 VMEM_LIMIT = 24 * 2**20
+INSIDE = 400_000_000
 
 
 def product(blocks, lead, field):
@@ -48,6 +49,7 @@
 
 def first_out(couplings, field, even_chord, out):
     cut_ref, chord_odd_ref, chord_even_ref = out
+    inner_chord = inner("chord")
     normal = product_lanes(couplings, (4,), field)
     cut_lane = iotas((8, 128))[1]
     cut = jnp.zeros((8, 128), F32)
@@ -56,7 +58,6 @@
             column = normal[b][8 * c : 8 * c + 8, 0:1]
             cut = jnp.where(cut_lane == 2 * b + c, column, cut)
     cut_ref[...] = cut
-    inner_chord = inner("chord")
     up = product_rows(couplings, (1,), field, 8)
     down = product_rows(couplings, (0,), field, 0)
     for b in range(6):
@@ -64,9 +65,8 @@
         chord_even_ref[b] = jnp.where(even_chord, up[b], down[b])
 
 
-def edges_kernel(adjoint, source, couplings, held_ref, part_ref, chord_even_ref, span_odd_ref, span_even_ref):
+def edges_kernel(adjoint, source, couplings, part_ref, span_odd_ref, span_even_ref):
     even_span = lax.axis_index("span") % 2 == 0
-    chord_even_ref[...] = held_ref[...]
     inner_span = inner("span")
     field = [adjoint[a] for a in range(6)]
     plus = product(couplings, (3,), field)
@@ -88,14 +88,10 @@
 def load_kernel(source, couplings, diag_block, line_inverse, adjoint, *out):
     *held, cut_ref, chord_odd_ref, chord_even_ref, sems = out
     held_adjoint, held_couplings, held_source, held_diag, held_line = held
-    order = [(4, 5), (0, 2), (2, 4), (5, 6)]
-    copies = [pltpu.make_async_copy(adjoint, held_adjoint, sems.at[0])]
-    for i, (low, high) in enumerate(order):
-        part = pl.ds(low, high - low)
-        copies.append(pltpu.make_async_copy(couplings.at[part], held_couplings.at[part], sems.at[1 + i]))
-    copies.append(pltpu.make_async_copy(source, held_source, sems.at[5]))
-    copies.append(pltpu.make_async_copy(diag_block, held_diag, sems.at[6]))
-    copies.append(pltpu.make_async_copy(line_inverse, held_line, sems.at[7]))
+    moved = [(adjoint, held_adjoint, slice(None))]
+    moved += [(couplings, held_couplings, pl.ds(low, high - low)) for low, high in ((0, 2), (4, 5), (2, 4), (5, 6))]
+    moved += [(source, held_source, slice(None)), (diag_block, held_diag, slice(None)), (line_inverse, held_line, slice(None))]
+    copies = [pltpu.make_async_copy(a.at[i], b.at[i], sems.at[n]) for n, (a, b, i) in enumerate(moved)]
     for copy in copies:
         copy.start()
     for copy in copies[:3]:
@@ -122,7 +118,23 @@
         out[b] = part[b] - inside
 
 
-def finish(part, got, masks, line_inverse, adjoint, even_chord, even_span):
+def first_inside_kernel(part, diag_block, couplings, adjoint, partner, codes, out, masks_ref):
+    inside_kernel(part, diag_block, couplings, adjoint, out)
+    here, there = iotas((8, 8))
+    for c in range(2):
+        rows = jnp.broadcast_to(codes[c : c + 1, :], (8, 8))
+        code = jnp.sum(jnp.where(here == there, rows, 0), axis=1, keepdims=True)
+        wall = jnp.broadcast_to(partner[:, c : c + 1], (8, 1)) < 0
+        factors = (
+            jnp.where(wall & (code == 0), 0.0, 1.0),
+            jnp.where(wall, 0.0, 1.0),
+            jnp.where(wall, 0.0, 1.0),
+        )
+        for i, factor in enumerate(factors):
+            masks_ref[i, 8 * c : 8 * c + 8, :] = jnp.broadcast_to(factor.astype(F32), (8, 128))
+
+
+def sweep_residual(part, got, masks, even_chord, even_span):
     cut, chord_odd, chord_even, span_odd, span_even = got
     row, lane = iotas((16, 256))
     row = row % 8
@@ -152,14 +164,15 @@
         residual.append(value)
         even_part.append(jnp.where(odd_lane, pltpu.roll(value, 1, 1), value))
         odd_part.append(jnp.where(odd_lane, value, pltpu.roll(value, 255, 1)))
-    after = []
-    for a in range(6):
-        total = adjoint[a]
-        for b in range(6):
-            total = total + line_inverse[a, b, 0].astype(F32) * even_part[b]
-            total = total + line_inverse[a, b, 1].astype(F32) * odd_part[b]
-        after.append(total)
-    return residual, after
+    return residual, (even_part, odd_part)
+
+
+def line_update(line_inverse, adjoint, parts, a):
+    total = adjoint[a]
+    for b in range(6):
+        for q in range(2):
+            total = total + line_inverse[a, b, q].astype(F32) * parts[q][b]
+    return total
 
 
 def middle_kernel(
@@ -168,34 +181,46 @@
     even_chord = lax.axis_index("chord") % 2 == 0
     even_span = lax.axis_index("span") % 2 == 0
     got = (cut, chord_odd, chord_even, span_odd, span_even)
-    _, after = finish(part, got, masks, line_inverse, adjoint, even_chord, even_span)
+    _, parts = sweep_residual(part, got, masks, even_chord, even_span)
+    after = [line_update(line_inverse, adjoint, parts, a) for a in range(6)]
     for a in range(6):
         after_ref[a] = after[a]
     first_out(couplings, after, even_chord, out)
 
 
 def last_kernel(
-    part, cut, chord_odd, chord_even, span_odd, span_even, masks, line_inverse, adjoint, after_ref, residual_ref
+    part, cut, chord_odd, chord_even, span_odd, span_even, masks, line_inverse, adjoint, after_ref, residual_ref,
+    held_after, held_residual, sems
 ):
     even_chord = lax.axis_index("chord") % 2 == 0
     even_span = lax.axis_index("span") % 2 == 0
     got = (cut, chord_odd, chord_even, span_odd, span_even)
-    residual, after = finish(part, got, masks, line_inverse, adjoint, even_chord, even_span)
-    for a in range(6):
-        after_ref[a] = after[a]
-        residual_ref[a] = residual[a]
+    residual, parts = sweep_residual(part, got, masks, even_chord, even_span)
+    for a in range(6):
+        held_residual[a] = residual[a]
+    copies = [pltpu.make_async_copy(held_residual, residual_ref, sems.at[0])]
+    copies[0].start()
+    for half in range(2):
+        for a in range(3 * half, 3 * half + 3):
+            held_after[a] = line_update(line_inverse, adjoint, parts, a)
+        rows = pl.ds(3 * half, 3)
+        copies.append(pltpu.make_async_copy(held_after.at[rows], after_ref.at[rows], sems.at[1 + half]))
+        copies[-1].start()
+    for copy in copies:
+        copy.wait()
 
 
 def call(kernel, name, operands, shapes, flops, in_vmem=True):
     vmem = pl.BlockSpec(memory_space=pltpu.VMEM)
-    made = [pltpu.VMEM(s, F32) if in_vmem else jax.ShapeDtypeStruct(s, F32) for s in shapes]
+    space = pltpu.VMEM if in_vmem else pltpu.HBM
     held = [pltpu.with_memory_space_constraint(x, pltpu.VMEM) for x in operands]
     return pl.pallas_call(
         kernel,
         name=name,
-        out_shape=made,
+        out_shape=[space(s, F32) for s in shapes],
         in_specs=[vmem] * len(held),
-        out_specs=[vmem] * len(shapes),
+        out_specs=[pl.BlockSpec(memory_space=space)] * len(shapes),
+        scratch_shapes=[] if in_vmem else [*(pltpu.VMEM(s, F32) for s in shapes), pltpu.SemaphoreType.DMA((3,))],
         compiler_params=pltpu.CompilerParams(vmem_limit_bytes=VMEM_LIMIT),
         cost_estimate=pl.CostEstimate(flops=flops, bytes_accessed=0, transcendentals=0),
     )(*held)
@@ -205,7 +230,7 @@
 SLAB = (6, 8, 256)
 ROWS = (16, 256)
 FIRST = [(8, 128), SLAB, SLAB]
-SECOND = [FIELD, SLAB, ROWS, (56, 256)]
+SECOND = [FIELD, ROWS, (24, 256)]
 
 
 def load(source, couplings, diag_block, line_inverse, adjoint):
@@ -226,19 +251,17 @@
     )(*operands)
 
 
-def wall_masks(partner, codes):
-    wall = jnp.repeat(partner < 0, 8)
-    stuck = wall & (codes.reshape(16) == 0)
-    rows = jnp.stack([jnp.where(stuck, 0.0, 1.0), jnp.where(wall, 0.0, 1.0), jnp.where(wall, 0.0, 1.0)])
-    return jnp.broadcast_to(rows[:, :, None], (3, 16, 128)).astype(F32)
-
-
-def pairs(count, start):
+def pairs(chords, spans, axis, start):
     found = []
-    for i in range(start, count - 1, 2):
-        found += [(i, i + 1), (i + 1, i)]
-    if start:
-        found += [(0, count - 1), (count - 1, 0)]
+    for chord in range(chords):
+        for span in range(spans):
+            index, count = (chord, chords) if axis == "chord" else (span, spans)
+            other = index + 1 if (index - start) % 2 == 0 else index - 1
+            if 0 <= other < count:
+                to = (other, span) if axis == "chord" else (chord, other)
+            else:
+                to = (chord, span ^ 1) if axis == "chord" else (chord ^ 1, span)
+            found.append((chord * spans + span, to[0] * spans + to[1]))
     return found
 
 
@@ -246,10 +269,10 @@
     cut, chord_odd, chord_even, span_odd, span_even = sent
     chords, spans = lax.axis_size("chord"), lax.axis_size("span")
     cut = lax.ppermute(cut, "chord", [(i, chords - 1 - i) for i in range(chords)])
-    chord_odd = lax.ppermute(chord_odd, "chord", pairs(chords, 1))
-    chord_even = lax.ppermute(chord_even, "chord", pairs(chords, 0))
-    span_odd = lax.ppermute(span_odd, "span", pairs(spans, 1))
-    span_even = lax.ppermute(span_even, "span", pairs(spans, 0))
+    chord_odd = lax.ppermute(chord_odd, ("chord", "span"), pairs(chords, spans, "chord", 1))
+    chord_even = lax.ppermute(chord_even, ("chord", "span"), pairs(chords, spans, "chord", 0))
+    span_odd = lax.ppermute(span_odd, ("chord", "span"), pairs(chords, spans, "span", 1))
+    span_even = lax.ppermute(span_even, ("chord", "span"), pairs(chords, spans, "span", 0))
     return cut, chord_odd, chord_even, span_odd, span_even
 
 
@@ -259,15 +282,19 @@
     diag_block = diag_block.reshape(6, 6, 16, 256)
     couplings = couplings.reshape(6, 6, 6, 16, 256)
     line_inverse = line_inverse.reshape(6, 6, 2, 16, 256)
-    masks = wall_masks(partner, codes)
     adjoint, couplings, source, diag_block, line_inverse, *far = load(
         source, couplings, diag_block, line_inverse, adjoint
     )
     for sweep in range(SWEEPS):
-        cut, chord_odd, held = far
-        part, *near = call(edges_kernel, "edges", (adjoint, source, couplings, held), SECOND, 1_000)
-        got = exchange((cut, chord_odd, *near))
-        [part] = call(inside_kernel, "inside", (part, diag_block, couplings, adjoint), [FIELD], 20_000_000_000)
+        part, *near = call(edges_kernel, "edges", (adjoint, source, couplings), SECOND, 1_000)
+        got = exchange((*far, *near))
+        held = (part, diag_block, couplings, adjoint)
+        if sweep == 0:
+            part, masks = call(
+                first_inside_kernel, "inside_masks", (*held, partner.reshape(1, 2), codes), [FIELD, (3, 16, 128)], INSIDE
+            )
+        else:
+            [part] = call(inside_kernel, "inside", held, [FIELD], INSIDE)
         arguments = (part, *got, masks, line_inverse, adjoint)
         if sweep < SWEEPS - 1:
             adjoint, *far = call(middle_kernel, "sweep", (*arguments, couplings), [FIELD, *FIRST], 1_000)

time: 82 us -> 73.8 us (0.90)
  starting transfers between devices: 49.8 us -> 45.7 us
  waiting for transfers between devices: 23.4 us -> 19.4 us
    ppermute x24, waiting for transfers between devices: 23 us -> 2.72 us  [the longest x6 2.67 us: exchange(): lax.ppermute(span_odd, ('chord', 'span'), pairs(chords, spans, 'span', 1))]
    ppermute x6, waiting for transfers between devices: 0.36 us -> 16.6 us  [exchange(): lax.ppermute(cut, 'chord', [(i, chords - 1 - i) for i in range(chords)])]
    ppermute x6, starting transfers between devices: 25.2 us -> 21.8 us  [exchange(): lax.ppermute(cut, 'chord', [(i, chords - 1 - i) for i in range(chords)])]
  transfers between devices with their start and end apart: 30 -> 30, of which waited for: 13 -> 6; matrix products, arithmetic and copies ran while one was open for 0% -> 0% of each run, Pallas kernels for 3% -> 3%
where the time goes in v3:
time: 73.8 us; the launch traced here: 73.7 us
  starting transfers between devices  45.7 us (62%)
  waiting for transfers between devices  19.4 us (26%)
  Pallas kernels  7.55 us (10%)
  between operations  1.03 us (1%)
    ppermute x6, starting transfers between devices, exchange(): lax.ppermute(cut, 'chord', [(i, chords - 1 - i) for i in range(chords)])  21.8 us
    ppermute x6, starting transfers between devices, exchange(): lax.ppermute(chord_even, ('chord', 'span'), pairs(chords, spans, 'chord',...  16.8 us
    ppermute x6, waiting for transfers between devices, exchange(): lax.ppermute(cut, 'chord', [(i, chords - 1 - i) for i in range(chords)])  16.6 us
    ppermute x6, starting transfers between devices, exchange(): lax.ppermute(span_even, ('chord', 'span'), pairs(chords, spans, 'span', 0))  6.03 us
    pallas_call x18, Pallas kernels, call(): pl.pallas_call(kernel, name=name, out_shape=[space(s, F32) for s in shape...  5.69 us
    ppermute x6, waiting for transfers between devices, exchange(): lax.ppermute(span_odd, ('chord', 'span'), pairs(chords, spans, 'span', 1))  2.67 us
    pallas_call x1, Pallas kernels, load(): pl.pallas_call(load_kernel, name='load', out_shape=[*held, *(pltpu.VMEM(s...  1.85 us
  transfers between devices with their start and end apart: 30, of which 6 were waited for; matrix products, arithmetic and copies ran while one was open for 0% of the time, Pallas kernels for 3%

profile of v3, /device:TPU:8, one launch (start us, length us, event | category | flops | bytes accessed | tf_op | source)
XLA Modules:
  0.0 73.7 jit_solution(10175955576621849084)
XLA Ops:
  0.7 1.9 %load.1 = (f32[6,16,256]{2,1,0:T(8,128)S(1)}, bf16[6,6,6,16,256]{4,3,2,1,0:T(8,128)(2,1)S(1)}, f32[6,16,256]{2,1,0:T(8,128)S(1)}, bf16[6,6,16,256]{3,2,1,0:T(8,1...) custom-call(f32[6,16,256]{2,1,0:T(8,128)} %bitcast.12, ...), custom_call_target="tpu_custom_call" | custom-call | flops 1000000 | tf_op jit(solution)/shard_map/load/pallas_call | solution.py:242
  2.6 3.0 %collective-permute-start.2 = (f32[6,8,256]{2,1,0:T(8,128)S(1)}, f32[6,8,256]{2,1,0:T(8,128)S(1)}, u32[]{:S(2)}, u32[]{:S(2)}) collective-permute-start(f32[6,8,256]{2,1,0:T(8,128)S(1)} %get-tuple-element.60), channel_id=1, source_target_pairs={{0,16},{1,17},{2,18},{3,19},{4,20},{5,21},{6,22},{7,23},{8,24},{9,... | collective-permute-start | bytes 147464 | tf_op jit(solution)/shard_map/ppermute | solution.py:273
  5.6 6.9 %collective-permute-start = (f32[8,128]{1,0:T(8,128)S(1)}, f32[8,128]{1,0:T(8,128)S(1)}, u32[]{:S(2)}, u32[]{:S(2)}) collective-permute-start(f32[8,128]{1,0:T(8,128)S(1)} %get-tuple-element.58), channel_id=1, source_target_pairs={{0,240},{16,224},{32,208},{48,192},{64,176},{80,160},{96,144},{112... | collective-permute-start | bytes 12296 | tf_op jit(solution)/shard_map/ppermute | solution.py:271
  12.7 1.1 %collective-permute-start.4 = (f32[24,256]{1,0:T(8,128)S(1)}, f32[24,256]{1,0:T(8,128)S(1)}, u32[]{:S(2)}, u32[]{:S(2)}) collective-permute-start(f32[24,256]{1,0:T(8,128)S(1)} %get-tuple-element.62), channel_id=1, source_target_pairs={{0,1},{1,0},{2,3},{3,2},{4,5},{5,4},{6,7},{7,6},{8,9},{9,8},{10,11... | collective-permute-start | bytes 73736 | tf_op jit(solution)/shard_map/ppermute | solution.py:275
  14.1 2.7 %collective-permute-done.3.span_odd = f32[16,256]{1,0:T(8,128)S(1)} collective-permute-done((f32[16,256]{1,0:T(8,128)S(1)}, f32[16,256]{1,0:T(8,128)S(1)}, u32[]{:S(2)}, u32[]{:S(2)}) %collective-permute-start.3) | collective-permute-done | bytes 16416 | tf_op jit(solution)/shard_map/ppermute | solution.py:274
  16.8 0.4 sweep.5
  17.3 3.6 %collective-permute-start.7 = (f32[6,8,256]{2,1,0:T(8,128)S(1)}, f32[6,8,256]{2,1,0:T(8,128)S(1)}, u32[]{:S(2)}, u32[]{:S(2)}) collective-permute-start(f32[6,8,256]{2,1,0:T(8,128)S(1)} %get-tuple-element.69), channel_id=1, source_target_pairs={{0,16},{1,17},{2,18},{3,19},{4,20},{5,21},{6,22},{7,23},{8,24},{9,... | collective-permute-start | bytes 147464 | tf_op jit(solution)/shard_map/ppermute | solution.py:273
  20.9 2.9 %collective-permute-start.5 = (f32[8,128]{1,0:T(8,128)S(1)}, f32[8,128]{1,0:T(8,128)S(1)}, u32[]{:S(2)}, u32[]{:S(2)}) collective-permute-start(f32[8,128]{1,0:T(8,128)S(1)} %get-tuple-element.67), channel_id=1, source_target_pairs={{0,240},{16,224},{32,208},{48,192},{64,176},{80,160},{96,144},{112... | collective-permute-start | bytes 12296 | tf_op jit(solution)/shard_map/ppermute | solution.py:271
  24.1 1.1 %collective-permute-start.9 = (f32[24,256]{1,0:T(8,128)S(1)}, f32[24,256]{1,0:T(8,128)S(1)}, u32[]{:S(2)}, u32[]{:S(2)}) collective-permute-start(f32[24,256]{1,0:T(8,128)S(1)} %get-tuple-element.71), channel_id=1, source_target_pairs={{0,1},{1,0},{2,3},{3,2},{4,5},{5,4},{6,7},{7,6},{8,9},{9,8},{10,11... | collective-permute-start | bytes 73736 | tf_op jit(solution)/shard_map/ppermute | solution.py:275
  25.5 3.3 %collective-permute-done.5.cut = f32[8,128]{1,0:T(8,128)S(1)} collective-permute-done((f32[8,128]{1,0:T(8,128)S(1)}, f32[8,128]{1,0:T(8,128)S(1)}, u32[]{:S(2)}, u32[]{:S(2)}) %collective-permute-start.5) | collective-permute-done | bytes 4128 | tf_op jit(solution)/shard_map/ppermute | solution.py:271
  28.8 0.4 sweep.6
  29.3 1.4 %collective-permute-start.12 = (f32[6,8,256]{2,1,0:T(8,128)S(1)}, f32[6,8,256]{2,1,0:T(8,128)S(1)}, u32[]{:S(2)}, u32[]{:S(2)}) collective-permute-start(f32[6,8,256]{2,1,0:T(8,128)S(1)} %get-tuple-element.76), channel_id=1, source_target_pairs={{0,16},{1,17},{2,18},{3,19},{4,20},{5,21},{6,22},{7,23},{8,24},{9,... | collective-permute-start | bytes 147464 | tf_op jit(solution)/shard_map/ppermute | solution.py:273
  30.7 2.9 %collective-permute-start.10 = (f32[8,128]{1,0:T(8,128)S(1)}, f32[8,128]{1,0:T(8,128)S(1)}, u32[]{:S(2)}, u32[]{:S(2)}) collective-permute-start(f32[8,128]{1,0:T(8,128)S(1)} %get-tuple-element.74), channel_id=1, source_target_pairs={{0,240},{16,224},{32,208},{48,192},{64,176},{80,160},{96,144},{112... | collective-permute-start | bytes 12296 | tf_op jit(solution)/shard_map/ppermute | solution.py:271
  33.9 1.1 %collective-permute-start.14 = (f32[24,256]{1,0:T(8,128)S(1)}, f32[24,256]{1,0:T(8,128)S(1)}, u32[]{:S(2)}, u32[]{:S(2)}) collective-permute-start(f32[24,256]{1,0:T(8,128)S(1)} %get-tuple-element.78), channel_id=1, source_target_pairs={{0,1},{1,0},{2,3},{3,2},{4,5},{5,4},{6,7},{7,6},{8,9},{9,8},{10,11... | collective-permute-start | bytes 73736 | tf_op jit(solution)/shard_map/ppermute | solution.py:275
  35.2 3.3 %collective-permute-done.10.cut = f32[8,128]{1,0:T(8,128)S(1)} collective-permute-done((f32[8,128]{1,0:T(8,128)S(1)}, f32[8,128]{1,0:T(8,128)S(1)}, u32[]{:S(2)}, u32[]{:S(2)}) %collective-permute-start.10) | collective-permute-done | bytes 4128 | tf_op jit(solution)/shard_map/ppermute | solution.py:271
  38.5 0.4 sweep.7
  39.1 3.6 %collective-permute-start.17 = (f32[6,8,256]{2,1,0:T(8,128)S(1)}, f32[6,8,256]{2,1,0:T(8,128)S(1)}, u32[]{:S(2)}, u32[]{:S(2)}) collective-permute-start(f32[6,8,256]{2,1,0:T(8,128)S(1)} %get-tuple-element.83), channel_id=1, source_target_pairs={{0,16},{1,17},{2,18},{3,19},{4,20},{5,21},{6,22},{7,23},{8,24},{9,... | collective-permute-start | bytes 147464 | tf_op jit(solution)/shard_map/ppermute | solution.py:273
  42.7 2.9 %collective-permute-start.15 = (f32[8,128]{1,0:T(8,128)S(1)}, f32[8,128]{1,0:T(8,128)S(1)}, u32[]{:S(2)}, u32[]{:S(2)}) collective-permute-start(f32[8,128]{1,0:T(8,128)S(1)} %get-tuple-element.81), channel_id=1, source_target_pairs={{0,240},{16,224},{32,208},{48,192},{64,176},{80,160},{96,144},{112... | collective-permute-start | bytes 12296 | tf_op jit(solution)/shard_map/ppermute | solution.py:271
  45.9 1.1 %collective-permute-start.19 = (f32[24,256]{1,0:T(8,128)S(1)}, f32[24,256]{1,0:T(8,128)S(1)}, u32[]{:S(2)}, u32[]{:S(2)}) collective-permute-start(f32[24,256]{1,0:T(8,128)S(1)} %get-tuple-element.85), channel_id=1, source_target_pairs={{0,1},{1,0},{2,3},{3,2},{4,5},{5,4},{6,7},{7,6},{8,9},{9,8},{10,11... | collective-permute-start | bytes 73736 | tf_op jit(solution)/shard_map/ppermute | solution.py:275
  47.0 0.3 inside.7.part
  47.3 3.3 %collective-permute-done.15.cut = f32[8,128]{1,0:T(8,128)S(1)} collective-permute-done((f32[8,128]{1,0:T(8,128)S(1)}, f32[8,128]{1,0:T(8,128)S(1)}, u32[]{:S(2)}, u32[]{:S(2)}) %collective-permute-start.15) | collective-permute-done | bytes 4128 | tf_op jit(solution)/shard_map/ppermute | solution.py:271
  50.6 0.4 sweep.8
  51.1 2.0 %collective-permute-start.22 = (f32[6,8,256]{2,1,0:T(8,128)S(1)}, f32[6,8,256]{2,1,0:T(8,128)S(1)}, u32[]{:S(2)}, u32[]{:S(2)}) collective-permute-start(f32[6,8,256]{2,1,0:T(8,128)S(1)} %get-tuple-element.90), channel_id=1, source_target_pairs={{0,16},{1,17},{2,18},{3,19},{4,20},{5,21},{6,22},{7,23},{8,24},{9,... | collective-permute-start | bytes 147464 | tf_op jit(solution)/shard_map/ppermute | solution.py:273
  53.1 3.3 %collective-permute-start.20 = (f32[8,128]{1,0:T(8,128)S(1)}, f32[8,128]{1,0:T(8,128)S(1)}, u32[]{:S(2)}, u32[]{:S(2)}) collective-permute-start(f32[8,128]{1,0:T(8,128)S(1)} %get-tuple-element.88), channel_id=1, source_target_pairs={{0,240},{16,224},{32,208},{48,192},{64,176},{80,160},{96,144},{112... | collective-permute-start | bytes 12296 | tf_op jit(solution)/shard_map/ppermute | solution.py:271
  56.6 0.7 collective-permute-start.24
  57.5 3.4 %collective-permute-done.20.cut = f32[8,128]{1,0:T(8,128)S(1)} collective-permute-done((f32[8,128]{1,0:T(8,128)S(1)}, f32[8,128]{1,0:T(8,128)S(1)}, u32[]{:S(2)}, u32[]{:S(2)}) %collective-permute-start.20) | collective-permute-done | bytes 4128 | tf_op jit(solution)/shard_map/ppermute | solution.py:271
  60.9 0.4 sweep.9
  61.5 3.2 %collective-permute-start.27 = (f32[6,8,256]{2,1,0:T(8,128)S(1)}, f32[6,8,256]{2,1,0:T(8,128)S(1)}, u32[]{:S(2)}, u32[]{:S(2)}) collective-permute-start(f32[6,8,256]{2,1,0:T(8,128)S(1)} %get-tuple-element.97), channel_id=1, source_target_pairs={{0,16},{1,17},{2,18},{3,19},{4,20},{5,21},{6,22},{7,23},{8,24},{9,... | collective-permute-start | bytes 147464 | tf_op jit(solution)/shard_map/ppermute | solution.py:273
  64.7 3.0 %collective-permute-start.25 = (f32[8,128]{1,0:T(8,128)S(1)}, f32[8,128]{1,0:T(8,128)S(1)}, u32[]{:S(2)}, u32[]{:S(2)}) collective-permute-start(f32[8,128]{1,0:T(8,128)S(1)} %get-tuple-element.95), channel_id=1, source_target_pairs={{0,240},{16,224},{32,208},{48,192},{64,176},{80,160},{96,144},{112... | collective-permute-start | bytes 12296 | tf_op jit(solution)/shard_map/ppermute | solution.py:271
  68.0 0.9 %collective-permute-start.29 = (f32[24,256]{1,0:T(8,128)S(1)}, f32[24,256]{1,0:T(8,128)S(1)}, u32[]{:S(2)}, u32[]{:S(2)}) collective-permute-start(f32[24,256]{1,0:T(8,128)S(1)} %get-tuple-element.99), channel_id=1, source_target_pairs={{0,1},{1,0},{2,3},{3,2},{4,5},{5,4},{6,7},{7,6},{8,9},{9,8},{10,11... | collective-permute-start | bytes 73736 | tf_op jit(solution)/shard_map/ppermute | solution.py:275
  69.1 3.5 %collective-permute-done.25.cut = f32[8,128]{1,0:T(8,128)S(1)} collective-permute-done((f32[8,128]{1,0:T(8,128)S(1)}, f32[8,128]{1,0:T(8,128)S(1)}, u32[]{:S(2)}, u32[]{:S(2)}) %collective-permute-start.25) | collective-permute-done | bytes 4128 | tf_op jit(solution)/shard_map/ppermute | solution.py:271
  72.6 1.0 %last.1 = (f32[6,16,256]{2,1,0:T(8,128)}, f32[6,16,256]{2,1,0:T(8,128)}) custom-call(f32[6,16,256]{2,1,0:T(8,128)S(1)} %inside.9.part, f32[8,128]{1,0:T(8,128)S(1)} %collective-permute-done.25.cut, f32[6,8,256]{2,1,0:T(8,128)S(1)} %collective-permute-done.26.chord_odd, f32[6,8,256]{2,1,0:T(8,128)S(1)} %collective-permute-done.27.chord_even, ...), custom_call_target="tpu_custom_call" | custom-call | flops 1000 | tf_op jit(solution)/shard_map/last/pallas_call | solution.py:217
  (51 shorter events, 3.4 us)
Async XLA Ops:
  0.6 13.2 %copy-start = (s32[2,8]{1,0:T(2,128)S(1)}, s32[2,8]{1,0:T(2,128)}, u32[]{:S(2)}) copy-start(s32[2,8]{1,0:T(2,128)} %codes.1) | copy-start | bytes 196
  0.6 13.2 %copy-start.1 = (s32[2]{0:T(128)S(1)}, s32[2]{0:T(128)}, u32[]{:S(2)}) copy-start(s32[2]{0:T(128)} %param.12) | copy-start | bytes 28
  2.5 14.3 %collective-permute-start.1 = (f32[6,8,256]{2,1,0:T(8,128)S(1)}, f32[6,8,256]{2,1,0:T(8,128)S(1)}, u32[]{:S(2)}, u32[]{:S(2)}) collective-permute-start(f32[6,8,256]{2,1,0:T(8,128)S(1)} %get-tuple-element.59), channel_id=1, source_target_pairs={{0,1},{1,0},{2,3},{3,2},{4,5},{5,4},{6,7},{7,6},{8,9},{9,8},{10,11... | collective-permute-start | bytes 147464 | tf_op jit(solution)/shard_map/ppermute | solution.py:272
  2.6 14.2 %collective-permute-start.2 = (f32[6,8,256]{2,1,0:T(8,128)S(1)}, f32[6,8,256]{2,1,0:T(8,128)S(1)}, u32[]{:S(2)}, u32[]{:S(2)}) collective-permute-start(f32[6,8,256]{2,1,0:T(8,128)S(1)} %get-tuple-element.60), channel_id=1, source_target_pairs={{0,16},{1,17},{2,18},{3,19},{4,20},{5,21},{6,22},{7,23},{8,24},{9,... | collective-permute-start | bytes 147464 | tf_op jit(solution)/shard_map/ppermute | solution.py:273
  5.6 8.5 %collective-permute-start = (f32[8,128]{1,0:T(8,128)S(1)}, f32[8,128]{1,0:T(8,128)S(1)}, u32[]{:S(2)}, u32[]{:S(2)}) collective-permute-start(f32[8,128]{1,0:T(8,128)S(1)} %get-tuple-element.58), channel_id=1, source_target_pairs={{0,240},{16,224},{32,208},{48,192},{64,176},{80,160},{96,144},{112... | collective-permute-start | bytes 12296 | tf_op jit(solution)/shard_map/ppermute | solution.py:271
  12.6 4.2 %collective-permute-start.3 = (f32[16,256]{1,0:T(8,128)S(1)}, f32[16,256]{1,0:T(8,128)S(1)}, u32[]{:S(2)}, u32[]{:S(2)}) collective-permute-start(f32[16,256]{1,0:T(8,128)S(1)} %get-tuple-element.61), channel_id=1, source_target_pairs={{0,16},{1,2},{2,1},{3,4},{4,3},{5,6},{6,5},{7,8},{8,7},{9,10},{10,... | collective-permute-start | bytes 49160 | tf_op jit(solution)/shard_map/ppermute | solution.py:274
  12.7 4.1 %collective-permute-start.4 = (f32[24,256]{1,0:T(8,128)S(1)}, f32[24,256]{1,0:T(8,128)S(1)}, u32[]{:S(2)}, u32[]{:S(2)}) collective-permute-start(f32[24,256]{1,0:T(8,128)S(1)} %get-tuple-element.62), channel_id=1, source_target_pairs={{0,1},{1,0},{2,3},{3,2},{4,5},{5,4},{6,7},{7,6},{8,9},{9,8},{10,11... | collective-permute-start | bytes 73736 | tf_op jit(solution)/shard_map/ppermute | solution.py:275
  17.2 11.5 %collective-permute-start.6 = (f32[6,8,256]{2,1,0:T(8,128)S(1)}, f32[6,8,256]{2,1,0:T(8,128)S(1)}, u32[]{:S(2)}, u32[]{:S(2)}) collective-permute-start(f32[6,8,256]{2,1,0:T(8,128)S(1)} %get-tuple-element.68), channel_id=1, source_target_pairs={{0,1},{1,0},{2,3},{3,2},{4,5},{5,4},{6,7},{7,6},{8,9},{9,8},{10,11... | collective-permute-start | bytes 147464 | tf_op jit(solution)/shard_map/ppermute | solution.py:272
  17.3 11.4 %collective-permute-start.7 = (f32[6,8,256]{2,1,0:T(8,128)S(1)}, f32[6,8,256]{2,1,0:T(8,128)S(1)}, u32[]{:S(2)}, u32[]{:S(2)}) collective-permute-start(f32[6,8,256]{2,1,0:T(8,128)S(1)} %get-tuple-element.69), channel_id=1, source_target_pairs={{0,16},{1,17},{2,18},{3,19},{4,20},{5,21},{6,22},{7,23},{8,24},{9,... | collective-permute-start | bytes 147464 | tf_op jit(solution)/shard_map/ppermute | solution.py:273
  20.9 7.8 %collective-permute-start.5 = (f32[8,128]{1,0:T(8,128)S(1)}, f32[8,128]{1,0:T(8,128)S(1)}, u32[]{:S(2)}, u32[]{:S(2)}) collective-permute-start(f32[8,128]{1,0:T(8,128)S(1)} %get-tuple-element.67), channel_id=1, source_target_pairs={{0,240},{16,224},{32,208},{48,192},{64,176},{80,160},{96,144},{112... | collective-permute-start | bytes 12296 | tf_op jit(solution)/shard_map/ppermute | solution.py:271
  24.0 4.7 %collective-permute-start.8 = (f32[16,256]{1,0:T(8,128)S(1)}, f32[16,256]{1,0:T(8,128)S(1)}, u32[]{:S(2)}, u32[]{:S(2)}) collective-permute-start(f32[16,256]{1,0:T(8,128)S(1)} %get-tuple-element.70), channel_id=1, source_target_pairs={{0,16},{1,2},{2,1},{3,4},{4,3},{5,6},{6,5},{7,8},{8,7},{9,10},{10,... | collective-permute-start | bytes 49160 | tf_op jit(solution)/shard_map/ppermute | solution.py:274
  24.1 4.6 %collective-permute-start.9 = (f32[24,256]{1,0:T(8,128)S(1)}, f32[24,256]{1,0:T(8,128)S(1)}, u32[]{:S(2)}, u32[]{:S(2)}) collective-permute-start(f32[24,256]{1,0:T(8,128)S(1)} %get-tuple-element.71), channel_id=1, source_target_pairs={{0,1},{1,0},{2,3},{3,2},{4,5},{5,4},{6,7},{7,6},{8,9},{9,8},{10,11... | collective-permute-start | bytes 73736 | tf_op jit(solution)/shard_map/ppermute | solution.py:275
  29.2 9.3 %collective-permute-start.11 = (f32[6,8,256]{2,1,0:T(8,128)S(1)}, f32[6,8,256]{2,1,0:T(8,128)S(1)}, u32[]{:S(2)}, u32[]{:S(2)}) collective-permute-start(f32[6,8,256]{2,1,0:T(8,128)S(1)} %get-tuple-element.75), channel_id=1, source_target_pairs={{0,1},{1,0},{2,3},{3,2},{4,5},{5,4},{6,7},{7,6},{8,9},{9,8},{10,11... | collective-permute-start | bytes 147464 | tf_op jit(solution)/shard_map/ppermute | solution.py:272
  29.3 9.2 %collective-permute-start.12 = (f32[6,8,256]{2,1,0:T(8,128)S(1)}, f32[6,8,256]{2,1,0:T(8,128)S(1)}, u32[]{:S(2)}, u32[]{:S(2)}) collective-permute-start(f32[6,8,256]{2,1,0:T(8,128)S(1)} %get-tuple-element.76), channel_id=1, source_target_pairs={{0,16},{1,17},{2,18},{3,19},{4,20},{5,21},{6,22},{7,23},{8,24},{9,... | collective-permute-start | bytes 147464 | tf_op jit(solution)/shard_map/ppermute | solution.py:273
  30.7 7.8 %collective-permute-start.10 = (f32[8,128]{1,0:T(8,128)S(1)}, f32[8,128]{1,0:T(8,128)S(1)}, u32[]{:S(2)}, u32[]{:S(2)}) collective-permute-start(f32[8,128]{1,0:T(8,128)S(1)} %get-tuple-element.74), channel_id=1, source_target_pairs={{0,240},{16,224},{32,208},{48,192},{64,176},{80,160},{96,144},{112... | collective-permute-start | bytes 12296 | tf_op jit(solution)/shard_map/ppermute | solution.py:271
  33.8 4.8 %collective-permute-start.13 = (f32[16,256]{1,0:T(8,128)S(1)}, f32[16,256]{1,0:T(8,128)S(1)}, u32[]{:S(2)}, u32[]{:S(2)}) collective-permute-start(f32[16,256]{1,0:T(8,128)S(1)} %get-tuple-element.77), channel_id=1, source_target_pairs={{0,16},{1,2},{2,1},{3,4},{4,3},{5,6},{6,5},{7,8},{8,7},{9,10},{10,... | collective-permute-start | bytes 49160 | tf_op jit(solution)/shard_map/ppermute | solution.py:274
  33.9 4.7 %collective-permute-start.14 = (f32[24,256]{1,0:T(8,128)S(1)}, f32[24,256]{1,0:T(8,128)S(1)}, u32[]{:S(2)}, u32[]{:S(2)}) collective-permute-start(f32[24,256]{1,0:T(8,128)S(1)} %get-tuple-element.78), channel_id=1, source_target_pairs={{0,1},{1,0},{2,3},{3,2},{4,5},{5,4},{6,7},{7,6},{8,9},{9,8},{10,11... | collective-permute-start | bytes 73736 | tf_op jit(solution)/shard_map/ppermute | solution.py:275
  39.0 11.6 %collective-permute-start.16 = (f32[6,8,256]{2,1,0:T(8,128)S(1)}, f32[6,8,256]{2,1,0:T(8,128)S(1)}, u32[]{:S(2)}, u32[]{:S(2)}) collective-permute-start(f32[6,8,256]{2,1,0:T(8,128)S(1)} %get-tuple-element.82), channel_id=1, source_target_pairs={{0,1},{1,0},{2,3},{3,2},{4,5},{5,4},{6,7},{7,6},{8,9},{9,8},{10,11... | collective-permute-start | bytes 147464 | tf_op jit(solution)/shard_map/ppermute | solution.py:272
  39.1 11.5 %collective-permute-start.17 = (f32[6,8,256]{2,1,0:T(8,128)S(1)}, f32[6,8,256]{2,1,0:T(8,128)S(1)}, u32[]{:S(2)}, u32[]{:S(2)}) collective-permute-start(f32[6,8,256]{2,1,0:T(8,128)S(1)} %get-tuple-element.83), channel_id=1, source_target_pairs={{0,16},{1,17},{2,18},{3,19},{4,20},{5,21},{6,22},{7,23},{8,24},{9,... | collective-permute-start | bytes 147464 | tf_op jit(solution)/shard_map/ppermute | solution.py:273
  42.7 7.8 %collective-permute-start.15 = (f32[8,128]{1,0:T(8,128)S(1)}, f32[8,128]{1,0:T(8,128)S(1)}, u32[]{:S(2)}, u32[]{:S(2)}) collective-permute-start(f32[8,128]{1,0:T(8,128)S(1)} %get-tuple-element.81), channel_id=1, source_target_pairs={{0,240},{16,224},{32,208},{48,192},{64,176},{80,160},{96,144},{112... | collective-permute-start | bytes 12296 | tf_op jit(solution)/shard_map/ppermute | solution.py:271
  45.8 4.7 %collective-permute-start.18 = (f32[16,256]{1,0:T(8,128)S(1)}, f32[16,256]{1,0:T(8,128)S(1)}, u32[]{:S(2)}, u32[]{:S(2)}) collective-permute-start(f32[16,256]{1,0:T(8,128)S(1)} %get-tuple-element.84), channel_id=1, source_target_pairs={{0,16},{1,2},{2,1},{3,4},{4,3},{5,6},{6,5},{7,8},{8,7},{9,10},{10,... | collective-permute-start | bytes 49160 | tf_op jit(solution)/shard_map/ppermute | solution.py:274
  45.9 4.6 %collective-permute-start.19 = (f32[24,256]{1,0:T(8,128)S(1)}, f32[24,256]{1,0:T(8,128)S(1)}, u32[]{:S(2)}, u32[]{:S(2)}) collective-permute-start(f32[24,256]{1,0:T(8,128)S(1)} %get-tuple-element.85), channel_id=1, source_target_pairs={{0,1},{1,0},{2,3},{3,2},{4,5},{5,4},{6,7},{7,6},{8,9},{9,8},{10,11... | collective-permute-start | bytes 73736 | tf_op jit(solution)/shard_map/ppermute | solution.py:275
  51.0 9.9 %collective-permute-start.21 = (f32[6,8,256]{2,1,0:T(8,128)S(1)}, f32[6,8,256]{2,1,0:T(8,128)S(1)}, u32[]{:S(2)}, u32[]{:S(2)}) collective-permute-start(f32[6,8,256]{2,1,0:T(8,128)S(1)} %get-tuple-element.89), channel_id=1, source_target_pairs={{0,1},{1,0},{2,3},{3,2},{4,5},{5,4},{6,7},{7,6},{8,9},{9,8},{10,11... | collective-permute-start | bytes 147464 | tf_op jit(solution)/shard_map/ppermute | solution.py:272
  51.1 9.8 %collective-permute-start.22 = (f32[6,8,256]{2,1,0:T(8,128)S(1)}, f32[6,8,256]{2,1,0:T(8,128)S(1)}, u32[]{:S(2)}, u32[]{:S(2)}) collective-permute-start(f32[6,8,256]{2,1,0:T(8,128)S(1)} %get-tuple-element.90), channel_id=1, source_target_pairs={{0,16},{1,17},{2,18},{3,19},{4,20},{5,21},{6,22},{7,23},{8,24},{9,... | collective-permute-start | bytes 147464 | tf_op jit(solution)/shard_map/ppermute | solution.py:273
  53.1 7.8 %collective-permute-start.20 = (f32[8,128]{1,0:T(8,128)S(1)}, f32[8,128]{1,0:T(8,128)S(1)}, u32[]{:S(2)}, u32[]{:S(2)}) collective-permute-start(f32[8,128]{1,0:T(8,128)S(1)} %get-tuple-element.88), channel_id=1, source_target_pairs={{0,240},{16,224},{32,208},{48,192},{64,176},{80,160},{96,144},{112... | collective-permute-start | bytes 12296 | tf_op jit(solution)/shard_map/ppermute | solution.py:271
  56.5 4.4 %collective-permute-start.23 = (f32[16,256]{1,0:T(8,128)S(1)}, f32[16,256]{1,0:T(8,128)S(1)}, u32[]{:S(2)}, u32[]{:S(2)}) collective-permute-start(f32[16,256]{1,0:T(8,128)S(1)} %get-tuple-element.91), channel_id=1, source_target_pairs={{0,16},{1,2},{2,1},{3,4},{4,3},{5,6},{6,5},{7,8},{8,7},{9,10},{10,... | collective-permute-start | bytes 49160 | tf_op jit(solution)/shard_map/ppermute | solution.py:274
  56.6 4.3 %collective-permute-start.24 = (f32[24,256]{1,0:T(8,128)S(1)}, f32[24,256]{1,0:T(8,128)S(1)}, u32[]{:S(2)}, u32[]{:S(2)}) collective-permute-start(f32[24,256]{1,0:T(8,128)S(1)} %get-tuple-element.92), channel_id=1, source_target_pairs={{0,1},{1,0},{2,3},{3,2},{4,5},{5,4},{6,7},{7,6},{8,9},{9,8},{10,11... | collective-permute-start | bytes 73736 | tf_op jit(solution)/shard_map/ppermute | solution.py:275
  61.4 11.2 %collective-permute-start.26 = (f32[6,8,256]{2,1,0:T(8,128)S(1)}, f32[6,8,256]{2,1,0:T(8,128)S(1)}, u32[]{:S(2)}, u32[]{:S(2)}) collective-permute-start(f32[6,8,256]{2,1,0:T(8,128)S(1)} %get-tuple-element.96), channel_id=1, source_target_pairs={{0,1},{1,0},{2,3},{3,2},{4,5},{5,4},{6,7},{7,6},{8,9},{9,8},{10,11... | collective-permute-start | bytes 147464 | tf_op jit(solution)/shard_map/ppermute | solution.py:272
  61.5 11.1 %collective-permute-start.27 = (f32[6,8,256]{2,1,0:T(8,128)S(1)}, f32[6,8,256]{2,1,0:T(8,128)S(1)}, u32[]{:S(2)}, u32[]{:S(2)}) collective-permute-start(f32[6,8,256]{2,1,0:T(8,128)S(1)} %get-tuple-element.97), channel_id=1, source_target_pairs={{0,16},{1,17},{2,18},{3,19},{4,20},{5,21},{6,22},{7,23},{8,24},{9,... | collective-permute-start | bytes 147464 | tf_op jit(solution)/shard_map/ppermute | solution.py:273
  64.7 7.8 %collective-permute-start.25 = (f32[8,128]{1,0:T(8,128)S(1)}, f32[8,128]{1,0:T(8,128)S(1)}, u32[]{:S(2)}, u32[]{:S(2)}) collective-permute-start(f32[8,128]{1,0:T(8,128)S(1)} %get-tuple-element.95), channel_id=1, source_target_pairs={{0,240},{16,224},{32,208},{48,192},{64,176},{80,160},{96,144},{112... | collective-permute-start | bytes 12296 | tf_op jit(solution)/shard_map/ppermute | solution.py:271
  67.9 4.7 %collective-permute-start.28 = (f32[16,256]{1,0:T(8,128)S(1)}, f32[16,256]{1,0:T(8,128)S(1)}, u32[]{:S(2)}, u32[]{:S(2)}) collective-permute-start(f32[16,256]{1,0:T(8,128)S(1)} %get-tuple-element.98), channel_id=1, source_target_pairs={{0,16},{1,2},{2,1},{3,4},{4,3},{5,6},{6,5},{7,8},{8,7},{9,10},{10,... | collective-permute-start | bytes 49160 | tf_op jit(solution)/shard_map/ppermute | solution.py:274
  68.0 4.6 %collective-permute-start.29 = (f32[24,256]{1,0:T(8,128)S(1)}, f32[24,256]{1,0:T(8,128)S(1)}, u32[]{:S(2)}, u32[]{:S(2)}) collective-permute-start(f32[24,256]{1,0:T(8,128)S(1)} %get-tuple-element.99), channel_id=1, source_target_pairs={{0,1},{1,0},{2,3},{3,2},{4,5},{5,4},{6,7},{7,6},{8,9},{9,8},{10,11... | collective-permute-start | bytes 73736 | tf_op jit(solution)/shard_map/ppermute | solution.py:275

commit v4 on v3

--- a/solution.py
+++ b/solution.py
@@ -8,6 +8,7 @@
 SWEEPS = 6
 F32 = jnp.float32
 VMEM_LIMIT = 24 * 2**20
+SETTLE = 1_000
 INSIDE = 400_000_000
 
 
@@ -20,11 +21,12 @@
     return out
 
 
-def product_rows(blocks, lead, field, low):
+def product_rows(blocks, lead, field, low, lanes=256):
     out = [None] * 6
     for a in range(6):
         for b in range(6):
-            term = blocks[(*lead, a, b)].astype(F32)[low : low + 8] * field[a][low : low + 8]
+            block = blocks[(*lead, a, b, slice(None), slice(0, lanes))].astype(F32)
+            term = block[low : low + 8] * field[a][low : low + 8]
             out[b] = term if a == 0 else out[b] + term
     return out
 
@@ -43,26 +45,43 @@
     return (index > 0) & (index < lax.axis_size(axis) - 1)
 
 
+def beside_mirror():
+    half = lax.axis_size("chord") // 2
+    index = lax.axis_index("chord")
+    return (index == half - 1) | (index == half)
+
+
 def iotas(shape):
     return lax.broadcasted_iota(jnp.int32, shape, 0), lax.broadcasted_iota(jnp.int32, shape, 1)
 
 
-def first_out(couplings, field, even_chord, out):
-    cut_ref, chord_odd_ref, chord_even_ref = out
-    inner_chord = inner("chord")
+def cut_row(couplings, field):
     normal = product_lanes(couplings, (4,), field)
-    cut_lane = iotas((8, 128))[1]
-    cut = jnp.zeros((8, 128), F32)
+    lane = iotas((8, 128))[1]
+    row = jnp.zeros((8, 128), F32)
     for b in range(6):
         for c in range(2):
             column = normal[b][8 * c : 8 * c + 8, 0:1]
-            cut = jnp.where(cut_lane == 2 * b + c, column, cut)
-    cut_ref[...] = cut
+            row = jnp.where(lane // 2 == 2 * b + c, column, row)
+    return row
+
+
+def chord_products(up, down, odd_ref, even_ref):
+    even_chord = lax.axis_index("chord") % 2 == 0
+    inner_chord = inner("chord")
+    for b in range(6):
+        odd_ref[b] = jnp.where(inner_chord, jnp.where(even_chord, down[b], up[b]), 0.0)
+        even_ref[b] = jnp.where(even_chord, up[b], down[b])
+
+
+def first_out(couplings, field, out):
+    cut_ref, chord_odd_ref, chord_even_ref = out
+    row = cut_row(couplings, field)
+    cut_ref[...] = row
+    chord_odd_ref[6, :, 0:128] = row
     up = product_rows(couplings, (1,), field, 8)
     down = product_rows(couplings, (0,), field, 0)
-    for b in range(6):
-        chord_odd_ref[b] = jnp.where(inner_chord, jnp.where(even_chord, down[b], up[b]), 0.0)
-        chord_even_ref[b] = jnp.where(even_chord, up[b], down[b])
+    chord_products(up, down, chord_odd_ref, chord_even_ref)
 
 
 def edges_kernel(adjoint, source, couplings, part_ref, span_odd_ref, span_even_ref):
@@ -85,20 +104,18 @@
         part_ref[b] = source[b] - inside
 
 
-def load_kernel(source, couplings, diag_block, line_inverse, adjoint, *out):
+def load_kernel(couplings, adjoint, *out):
     *held, cut_ref, chord_odd_ref, chord_even_ref, sems = out
-    held_adjoint, held_couplings, held_source, held_diag, held_line = held
+    held_adjoint, held_couplings = held
     moved = [(adjoint, held_adjoint, slice(None))]
     moved += [(couplings, held_couplings, pl.ds(low, high - low)) for low, high in ((0, 2), (4, 5), (2, 4), (5, 6))]
-    moved += [(source, held_source, slice(None)), (diag_block, held_diag, slice(None)), (line_inverse, held_line, slice(None))]
     copies = [pltpu.make_async_copy(a.at[i], b.at[i], sems.at[n]) for n, (a, b, i) in enumerate(moved)]
     for copy in copies:
         copy.start()
     for copy in copies[:3]:
         copy.wait()
-    even_chord = lax.axis_index("chord") % 2 == 0
     field = [held_adjoint[a] for a in range(6)]
-    first_out(held_couplings, field, even_chord, (cut_ref, chord_odd_ref, chord_even_ref))
+    first_out(held_couplings, field, (cut_ref, chord_odd_ref, chord_even_ref))
     for copy in copies[3:]:
         copy.wait()
 
@@ -135,13 +152,11 @@
 
 
 def sweep_residual(part, got, masks, even_chord, even_span):
-    cut, chord_odd, chord_even, span_odd, span_even = got
+    chord_odd, chord_even, span_odd, span_even = got
     row, lane = iotas((16, 256))
     row = row % 8
     top = jnp.where(even_span, span_odd[...], span_even[0:16])
     bottom = jnp.where(even_span, span_even[0:16], span_odd[...])
-    arrived = cut[...]
-    wake = masks[2][:, 0:1] > 0
     odd_lane = lane % 2 == 1
     residual, even_part, odd_part = [], [], []
     for b in range(6):
@@ -154,8 +169,6 @@
             [jnp.broadcast_to(bottom[2 * b + c : 2 * b + c + 1], (8, 256)) for c in range(2)], axis=0
         )
         outside = outside + jnp.where(row == 0, tops, jnp.where(row == 7, bottoms, 0.0))
-        columns = jnp.concatenate([arrived[:, 2 * b + 1 : 2 * b + 2], arrived[:, 2 * b : 2 * b + 1]], axis=0)
-        outside = outside + jnp.where((lane == 0) & wake, columns, 0.0)
         value = part[b] - outside
         if 1 <= b <= 3:
             value = value * jnp.where(lane == 0, masks[0][:, 0:1], 1.0)
@@ -175,36 +188,87 @@
     return total
 
 
-def middle_kernel(
-    part, cut, chord_odd, chord_even, span_odd, span_even, masks, line_inverse, adjoint, couplings, after_ref, *out
-):
+def settle(part, got, masks, line_inverse, adjoint):
     even_chord = lax.axis_index("chord") % 2 == 0
     even_span = lax.axis_index("span") % 2 == 0
-    got = (cut, chord_odd, chord_even, span_odd, span_even)
-    _, parts = sweep_residual(part, got, masks, even_chord, even_span)
-    after = [line_update(line_inverse, adjoint, parts, a) for a in range(6)]
+    residual, parts = sweep_residual(part, got, masks, even_chord, even_span)
+    return residual, [line_update(line_inverse, adjoint, parts, a) for a in range(6)]
+
+
+def settle_kernel(
+    part, chord_odd, chord_even, span_odd, span_even, masks, line_inverse, adjoint, couplings, after_ref, odd_ref, even_ref
+):
+    _, after = settle(part, (chord_odd, chord_even, span_odd, span_even), masks, line_inverse, adjoint)
     for a in range(6):
         after_ref[a] = after[a]
-    first_out(couplings, after, even_chord, out)
-
-
-def last_kernel(
-    part, cut, chord_odd, chord_even, span_odd, span_even, masks, line_inverse, adjoint, after_ref, residual_ref,
-    held_after, held_residual, sems
+    up = product_rows(couplings, (1,), after, 8)
+    down = product_rows(couplings, (0,), after, 0)
+    chord_products(up, down, odd_ref, even_ref)
+
+
+def last_settle_kernel(
+    part, chord_odd, chord_even, span_odd, span_even, masks, line_inverse, adjoint, after_ref, residual_ref
 ):
+    residual, after = settle(part, (chord_odd, chord_even, span_odd, span_even), masks, line_inverse, adjoint)
+    for a in range(6):
+        after_ref[a] = after[a]
+        residual_ref[a] = residual[a]
+
+
+def cut_change(cut, chord_odd, masks, line_inverse):
+    arrived = jnp.where(beside_mirror(), chord_odd[6, :, 0:128], cut[...])
+    wake = masks[2] > 0
+    lane = iotas((16, 128))[1]
+    columns = []
+    for b in range(6):
+        slabs = [pltpu.roll(arrived, (128 - 4 * b - 2 * c) % 128, 1) for c in (1, 0)]
+        columns.append(jnp.where(wake, -jnp.concatenate(slabs, axis=0), 0.0))
+    change = [jnp.where(lane == 0, column, 0.0) for column in columns]
+    delta = []
+    for a in range(6):
+        total = None
+        for b in range(6):
+            term = line_inverse[a, b, 0, :, 0:128].astype(F32) * columns[b]
+            total = term if b == 0 else total + term
+        delta.append(jnp.where(lane < 2, total, 0.0))
+    return change, delta
+
+
+def cut_kernel(
+    cut, chord_odd, masks, line_inverse, couplings, main, odd, even, after_ref, cut_ref, chord_odd_ref, chord_even_ref
+):
+    _, delta = cut_change(cut, chord_odd, masks, line_inverse)
+    near = [main[a, :, 0:128] + delta[a] for a in range(6)]
+    for a in range(6):
+        after_ref[a, :, 0:128] = near[a]
+        after_ref[a, :, 128:256] = main[a, :, 128:256]
+    row = cut_row(couplings, near)
+    cut_ref[...] = row
+    chord_odd_ref[6, :, 0:128] = row
+    chord_odd_ref[0:6] = odd[...]
+    chord_even_ref[...] = even[...]
+    up = product_rows(couplings, (1,), delta, 8, 128)
+    down = product_rows(couplings, (0,), delta, 0, 128)
     even_chord = lax.axis_index("chord") % 2 == 0
-    even_span = lax.axis_index("span") % 2 == 0
-    got = (cut, chord_odd, chord_even, span_odd, span_even)
-    residual, parts = sweep_residual(part, got, masks, even_chord, even_span)
-    for a in range(6):
-        held_residual[a] = residual[a]
-    copies = [pltpu.make_async_copy(held_residual, residual_ref, sems.at[0])]
-    copies[0].start()
-    for half in range(2):
-        for a in range(3 * half, 3 * half + 3):
-            held_after[a] = line_update(line_inverse, adjoint, parts, a)
-        rows = pl.ds(3 * half, 3)
-        copies.append(pltpu.make_async_copy(held_after.at[rows], after_ref.at[rows], sems.at[1 + half]))
+    inner_chord = inner("chord")
+    for b in range(6):
+        first = jnp.where(inner_chord, jnp.where(even_chord, down[b], up[b]), 0.0)
+        chord_odd_ref[b, :, 0:128] = odd[b, :, 0:128] + first
+        chord_even_ref[b, :, 0:128] = even[b, :, 0:128] + jnp.where(even_chord, up[b], down[b])
+
+
+def last_cut_kernel(
+    cut, chord_odd, masks, line_inverse, main, held, after_ref, residual_ref, after_scratch, residual_scratch, sems
+):
+    change, delta = cut_change(cut, chord_odd, masks, line_inverse)
+    copies = []
+    for i, (old, added, scratch, to) in enumerate(
+        ((held, change, residual_scratch, residual_ref), (main, delta, after_scratch, after_ref))
+    ):
+        for a in range(6):
+            scratch[a, :, 0:128] = old[a, :, 0:128] + added[a]
+            scratch[a, :, 128:256] = old[a, :, 128:256]
+        copies.append(pltpu.make_async_copy(scratch, to, sems.at[i]))
         copies[-1].start()
     for copy in copies:
         copy.wait()
@@ -220,7 +284,7 @@
         out_shape=[space(s, F32) for s in shapes],
         in_specs=[vmem] * len(held),
         out_specs=[pl.BlockSpec(memory_space=space)] * len(shapes),
-        scratch_shapes=[] if in_vmem else [*(pltpu.VMEM(s, F32) for s in shapes), pltpu.SemaphoreType.DMA((3,))],
+        scratch_shapes=[] if in_vmem else [*(pltpu.VMEM(s, F32) for s in shapes), pltpu.SemaphoreType.DMA((2,))],
         compiler_params=pltpu.CompilerParams(vmem_limit_bytes=VMEM_LIMIT),
         cost_estimate=pl.CostEstimate(flops=flops, bytes_accessed=0, transcendentals=0),
     )(*held)
@@ -229,23 +293,23 @@
 FIELD = (6, 16, 256)
 SLAB = (6, 8, 256)
 ROWS = (16, 256)
-FIRST = [(8, 128), SLAB, SLAB]
+FIRST = [(8, 128), (7, 8, 256), SLAB]
 SECOND = [FIELD, ROWS, (24, 256)]
 
 
-def load(source, couplings, diag_block, line_inverse, adjoint):
+def load(couplings, adjoint):
     vmem = pl.BlockSpec(memory_space=pltpu.VMEM)
     operands = [
-        pltpu.with_memory_space_constraint(x, pltpu.HBM) for x in (source, couplings, diag_block, line_inverse, adjoint)
+        pltpu.with_memory_space_constraint(x, pltpu.HBM) for x in (couplings, adjoint)
     ]
-    held = [pltpu.VMEM(x.shape, x.dtype) for x in (adjoint, couplings, source, diag_block, line_inverse)]
+    held = [pltpu.VMEM(x.shape, x.dtype) for x in (adjoint, couplings)]
     return pl.pallas_call(
         load_kernel,
         name="load",
         out_shape=[*held, *(pltpu.VMEM(s, F32) for s in FIRST)],
-        in_specs=[pl.BlockSpec(memory_space=pltpu.HBM)] * 5,
-        out_specs=[vmem] * 8,
-        scratch_shapes=[pltpu.SemaphoreType.DMA((8,))],
+        in_specs=[pl.BlockSpec(memory_space=pltpu.HBM)] * 2,
+        out_specs=[vmem] * 5,
+        scratch_shapes=[pltpu.SemaphoreType.DMA((5,))],
         compiler_params=pltpu.CompilerParams(vmem_limit_bytes=VMEM_LIMIT),
         cost_estimate=pl.CostEstimate(flops=1_000_000, bytes_accessed=0, transcendentals=0),
     )(*operands)
@@ -265,10 +329,22 @@
     return found
 
 
+def mirrors(chords, spans):
+    found = []
+    for chord in range(chords):
+        for span in range(spans):
+            if abs(2 * chord + 1 - chords) == 1:
+                to = (chord, span ^ 1)
+            else:
+                to = (chords - 1 - chord, span)
+            found.append((chord * spans + span, to[0] * spans + to[1]))
+    return found
+
+
 def exchange(sent):
     cut, chord_odd, chord_even, span_odd, span_even = sent
     chords, spans = lax.axis_size("chord"), lax.axis_size("span")
-    cut = lax.ppermute(cut, "chord", [(i, chords - 1 - i) for i in range(chords)])
+    cut = lax.ppermute(cut, ("chord", "span"), mirrors(chords, spans))
     chord_odd = lax.ppermute(chord_odd, ("chord", "span"), pairs(chords, spans, "chord", 1))
     chord_even = lax.ppermute(chord_even, ("chord", "span"), pairs(chords, spans, "chord", 0))
     span_odd = lax.ppermute(span_odd, ("chord", "span"), pairs(chords, spans, "span", 1))
@@ -282,9 +358,7 @@
     diag_block = diag_block.reshape(6, 6, 16, 256)
     couplings = couplings.reshape(6, 6, 6, 16, 256)
     line_inverse = line_inverse.reshape(6, 6, 2, 16, 256)
-    adjoint, couplings, source, diag_block, line_inverse, *far = load(
-        source, couplings, diag_block, line_inverse, adjoint
-    )
+    adjoint, couplings, *far = load(couplings, adjoint)
     for sweep in range(SWEEPS):
         part, *near = call(edges_kernel, "edges", (adjoint, source, couplings), SECOND, 1_000)
         got = exchange((*far, *near))
@@ -295,11 +369,15 @@
             )
         else:
             [part] = call(inside_kernel, "inside", held, [FIELD], INSIDE)
-        arguments = (part, *got, masks, line_inverse, adjoint)
+        cut, *beside = got
+        arguments = (part, *beside, masks, line_inverse, adjoint)
+        late = (cut, beside[0], masks, line_inverse)
         if sweep < SWEEPS - 1:
-            adjoint, *far = call(middle_kernel, "sweep", (*arguments, couplings), [FIELD, *FIRST], 1_000)
+            main, odd, even = call(settle_kernel, "settle", (*arguments, couplings), [FIELD, SLAB, SLAB], SETTLE)
+            adjoint, *far = call(cut_kernel, "cut", (*late, couplings, main, odd, even), [FIELD, *FIRST], 1_000)
         else:
-            adjoint, residual = call(last_kernel, "last", arguments, [FIELD, FIELD], 1_000, False)
+            main, held = call(last_settle_kernel, "last_settle", arguments, [FIELD, FIELD], SETTLE)
+            adjoint, residual = call(last_cut_kernel, "last", (*late, main, held), [FIELD, FIELD], 1_000, False)
     return adjoint.reshape(6, 2, 8, 256), residual.reshape(6, 2, 8, 256)
 
 

time: 73.8 us -> 72.4 us (0.981)
  starting transfers between devices: 45.7 us -> 44 us
    ppermute x6, waiting for transfers between devices: 16.6 us -> 1 us  [exchange(): cut = lax.ppermute(cut, ('chord', 'span'), mirrors(chords, spans))]
    ppermute x6, waiting for transfers between devices: 2.67 us -> 18.3 us  [exchange(): lax.ppermute(span_odd, ('chord', 'span'), pairs(chords, spans, 'span', 1))]
    ppermute x6, starting transfers between devices: 6.03 us -> 4.48 us  [exchange(): lax.ppermute(span_even, ('chord', 'span'), pairs(chords, spans, 'span', 0))]
    pallas_call x18 -> x24, Pallas kernels: 5.69 us -> 6.27 us  [call(): pl.pallas_call(kernel, name=name, out_shape=[space(s, F32) for s in shape...]
  transfers between devices with their start and end apart: 30 -> 30, of which waited for: 6 -> 10; matrix products, arithmetic and copies ran while one was open for 0% -> 0% of each run, Pallas kernels for 3% -> 6%
where the time goes in v4:
time: 72.4 us; the launch traced here: 72.2 us
  starting transfers between devices  44 us (61%)
  waiting for transfers between devices  19.3 us (27%)
  Pallas kernels  7.81 us (11%)
  between operations  1.07 us (1%)
    ppermute x6, starting transfers between devices, exchange(): cut = lax.ppermute(cut, ('chord', 'span'), mirrors(chords, spans))  21.9 us
    ppermute x6, waiting for transfers between devices, exchange(): lax.ppermute(span_odd, ('chord', 'span'), pairs(chords, spans, 'span', 1))  18.3 us
    ppermute x6, starting transfers between devices, exchange(): lax.ppermute(chord_even, ('chord', 'span'), pairs(chords, spans, 'chord',...  16.5 us
    pallas_call x24, Pallas kernels, call(): pl.pallas_call(kernel, name=name, out_shape=[space(s, F32) for s in shape...  6.27 us
    ppermute x6, starting transfers between devices, exchange(): lax.ppermute(span_even, ('chord', 'span'), pairs(chords, spans, 'span', 0))  4.48 us
    pallas_call x1, Pallas kernels, load(): pl.pallas_call(load_kernel, name='load', out_shape=[*held, *(pltpu.VMEM(s...  1.54 us
  transfers between devices with their start and end apart: 30, of which 10 were waited for; matrix products, arithmetic and copies ran while one was open for 0% of the time, Pallas kernels for 6%

profile of v4, /device:TPU:8, one launch (start us, length us, event | category | flops | bytes accessed | tf_op | source)
XLA Modules:
  0.0 72.2 jit_solution(13657238931487764948)
XLA Ops:
  0.7 1.5 %load.1 = (f32[6,16,256]{2,1,0:T(8,128)S(1)}, bf16[6,6,6,16,256]{4,3,2,1,0:T(8,128)(2,1)S(1)}, f32[8,128]{1,0:T(8,128)S(1)}, f32[7,8,256]{2,1,0:T(8,128)S(1)}, f32[6,8,256]{2,1,0:T(8,128)S(1)}) custom-call(bf16[6,6,6,16,256]{4,3,2,1,0:T(8,128)(2,1)} %bitcast.33, f32[6,16,256]{2,1,0:T(8,128)} %bitcast.34), custom_call_target="tpu_custom_call" | custom-call | flops 1000000 | tf_op jit(solution)/shard_map/load/pallas_call | solution.py:306
  2.3 3.0 %collective-permute-start.2 = (f32[6,8,256]{2,1,0:T(8,128)S(1)}, f32[6,8,256]{2,1,0:T(8,128)S(1)}, u32[]{:S(2)}, u32[]{:S(2)}) collective-permute-start(f32[6,8,256]{2,1,0:T(8,128)S(1)} %get-tuple-element.73), channel_id=1, source_target_pairs={{0,16},{1,17},{2,18},{3,19},{4,20},{5,21},{6,22},{7,23},{8,24},{9,... | collective-permute-start | bytes 147464 | tf_op jit(solution)/shard_map/ppermute | solution.py:349
  5.3 6.9 %collective-permute-start = (f32[8,128]{1,0:T(8,128)S(1)}, f32[8,128]{1,0:T(8,128)S(1)}, u32[]{:S(2)}, u32[]{:S(2)}) collective-permute-start(f32[8,128]{1,0:T(8,128)S(1)} %get-tuple-element.66), channel_id=1, source_target_pairs={{0,240},{1,241},{2,242},{3,243},{4,244},{5,245},{6,246},{7,247},{8... | collective-permute-start | bytes 12296 | tf_op jit(solution)/shard_map/ppermute | solution.py:347
  12.4 1.1 %collective-permute-start.4 = (f32[24,256]{1,0:T(8,128)S(1)}, f32[24,256]{1,0:T(8,128)S(1)}, u32[]{:S(2)}, u32[]{:S(2)}) collective-permute-start(f32[24,256]{1,0:T(8,128)S(1)} %get-tuple-element.75), channel_id=1, source_target_pairs={{0,1},{1,0},{2,3},{3,2},{4,5},{5,4},{6,7},{7,6},{8,9},{9,8},{10,11... | collective-permute-start | bytes 73736 | tf_op jit(solution)/shard_map/ppermute | solution.py:351
  13.8 2.7 %collective-permute-done.3.span_odd = f32[16,256]{1,0:T(8,128)S(1)} collective-permute-done((f32[16,256]{1,0:T(8,128)S(1)}, f32[16,256]{1,0:T(8,128)S(1)}, u32[]{:S(2)}, u32[]{:S(2)}) %collective-permute-start.3) | collective-permute-done | bytes 16416 | tf_op jit(solution)/shard_map/ppermute | solution.py:350
  16.5 0.3 settle.5
  17.2 3.6 %collective-permute-start.7 = (f32[6,8,256]{2,1,0:T(8,128)S(1)}, f32[6,8,256]{2,1,0:T(8,128)S(1)}, u32[]{:S(2)}, u32[]{:S(2)}) collective-permute-start(f32[6,8,256]{2,1,0:T(8,128)S(1)} %get-tuple-element.83), channel_id=1, source_target_pairs={{0,16},{1,17},{2,18},{3,19},{4,20},{5,21},{6,22},{7,23},{8,24},{9,... | collective-permute-start | bytes 147464 | tf_op jit(solution)/shard_map/ppermute | solution.py:349
  20.8 2.5 %collective-permute-start.5 = (f32[8,128]{1,0:T(8,128)S(1)}, f32[8,128]{1,0:T(8,128)S(1)}, u32[]{:S(2)}, u32[]{:S(2)}) collective-permute-start(f32[8,128]{1,0:T(8,128)S(1)} %get-tuple-element.79), channel_id=1, source_target_pairs={{0,240},{1,241},{2,242},{3,243},{4,244},{5,245},{6,246},{7,247},{8... | collective-permute-start | bytes 12296 | tf_op jit(solution)/shard_map/ppermute | solution.py:347
  23.6 1.1 %collective-permute-start.9 = (f32[24,256]{1,0:T(8,128)S(1)}, f32[24,256]{1,0:T(8,128)S(1)}, u32[]{:S(2)}, u32[]{:S(2)}) collective-permute-start(f32[24,256]{1,0:T(8,128)S(1)} %get-tuple-element.85), channel_id=1, source_target_pairs={{0,1},{1,0},{2,3},{3,2},{4,5},{5,4},{6,7},{7,6},{8,9},{9,8},{10,11... | collective-permute-start | bytes 73736 | tf_op jit(solution)/shard_map/ppermute | solution.py:351
  24.9 2.7 %collective-permute-done.8.span_odd = f32[16,256]{1,0:T(8,128)S(1)} collective-permute-done((f32[16,256]{1,0:T(8,128)S(1)}, f32[16,256]{1,0:T(8,128)S(1)}, u32[]{:S(2)}, u32[]{:S(2)}) %collective-permute-start.8) | collective-permute-done | bytes 16416 | tf_op jit(solution)/shard_map/ppermute | solution.py:350
  27.6 0.3 settle.6
  27.9 0.6 collective-permute-done.5.cut
  28.9 1.4 %collective-permute-start.12 = (f32[6,8,256]{2,1,0:T(8,128)S(1)}, f32[6,8,256]{2,1,0:T(8,128)S(1)}, u32[]{:S(2)}, u32[]{:S(2)}) collective-permute-start(f32[6,8,256]{2,1,0:T(8,128)S(1)} %get-tuple-element.93), channel_id=1, source_target_pairs={{0,16},{1,17},{2,18},{3,19},{4,20},{5,21},{6,22},{7,23},{8,24},{9,... | collective-permute-start | bytes 147464 | tf_op jit(solution)/shard_map/ppermute | solution.py:349
  30.3 3.1 %collective-permute-start.10 = (f32[8,128]{1,0:T(8,128)S(1)}, f32[8,128]{1,0:T(8,128)S(1)}, u32[]{:S(2)}, u32[]{:S(2)}) collective-permute-start(f32[8,128]{1,0:T(8,128)S(1)} %get-tuple-element.89), channel_id=1, source_target_pairs={{0,240},{1,241},{2,242},{3,243},{4,244},{5,245},{6,246},{7,247},{8... | collective-permute-start | bytes 12296 | tf_op jit(solution)/shard_map/ppermute | solution.py:347
  33.6 0.6 collective-permute-start.14
  34.5 3.2 %collective-permute-done.13.span_odd = f32[16,256]{1,0:T(8,128)S(1)} collective-permute-done((f32[16,256]{1,0:T(8,128)S(1)}, f32[16,256]{1,0:T(8,128)S(1)}, u32[]{:S(2)}, u32[]{:S(2)}) %collective-permute-start.13) | collective-permute-done | bytes 16416 | tf_op jit(solution)/shard_map/ppermute | solution.py:350
  37.7 0.3 settle.7
  38.5 3.6 %collective-permute-start.17 = (f32[6,8,256]{2,1,0:T(8,128)S(1)}, f32[6,8,256]{2,1,0:T(8,128)S(1)}, u32[]{:S(2)}, u32[]{:S(2)}) collective-permute-start(f32[6,8,256]{2,1,0:T(8,128)S(1)} %get-tuple-element.103), channel_id=1, source_target_pairs={{0,16},{1,17},{2,18},{3,19},{4,20},{5,21},{6,22},{7,23},{8,24},{9,... | collective-permute-start | bytes 147464 | tf_op jit(solution)/shard_map/ppermute | solution.py:349
  42.1 3.1 %collective-permute-start.15 = (f32[8,128]{1,0:T(8,128)S(1)}, f32[8,128]{1,0:T(8,128)S(1)}, u32[]{:S(2)}, u32[]{:S(2)}) collective-permute-start(f32[8,128]{1,0:T(8,128)S(1)} %get-tuple-element.99), channel_id=1, source_target_pairs={{0,240},{1,241},{2,242},{3,243},{4,244},{5,245},{6,246},{7,247},{8... | collective-permute-start | bytes 12296 | tf_op jit(solution)/shard_map/ppermute | solution.py:347
  45.5 0.6 collective-permute-start.19
  46.3 3.2 %collective-permute-done.18.span_odd = f32[16,256]{1,0:T(8,128)S(1)} collective-permute-done((f32[16,256]{1,0:T(8,128)S(1)}, f32[16,256]{1,0:T(8,128)S(1)}, u32[]{:S(2)}, u32[]{:S(2)}) %collective-permute-start.18) | collective-permute-done | bytes 16416 | tf_op jit(solution)/shard_map/ppermute | solution.py:350
  49.5 0.3 settle.8
  50.3 1.4 %collective-permute-start.22 = (f32[6,8,256]{2,1,0:T(8,128)S(1)}, f32[6,8,256]{2,1,0:T(8,128)S(1)}, u32[]{:S(2)}, u32[]{:S(2)}) collective-permute-start(f32[6,8,256]{2,1,0:T(8,128)S(1)} %get-tuple-element.113), channel_id=1, source_target_pairs={{0,16},{1,17},{2,18},{3,19},{4,20},{5,21},{6,22},{7,23},{8,24},{9,... | collective-permute-start | bytes 147464 | tf_op jit(solution)/shard_map/ppermute | solution.py:349
  51.7 3.2 %collective-permute-start.20 = (f32[8,128]{1,0:T(8,128)S(1)}, f32[8,128]{1,0:T(8,128)S(1)}, u32[]{:S(2)}, u32[]{:S(2)}) collective-permute-start(f32[8,128]{1,0:T(8,128)S(1)} %get-tuple-element.109), channel_id=1, source_target_pairs={{0,240},{1,241},{2,242},{3,243},{4,244},{5,245},{6,246},{7,247},{8... | collective-permute-start | bytes 12296 | tf_op jit(solution)/shard_map/ppermute | solution.py:347
  55.1 0.5 collective-permute-start.24
  55.8 3.3 %collective-permute-done.23.span_odd = f32[16,256]{1,0:T(8,128)S(1)} collective-permute-done((f32[16,256]{1,0:T(8,128)S(1)}, f32[16,256]{1,0:T(8,128)S(1)}, u32[]{:S(2)}, u32[]{:S(2)}) %collective-permute-start.23) | collective-permute-done | bytes 16416 | tf_op jit(solution)/shard_map/ppermute | solution.py:350
  59.2 0.3 settle.9
  59.9 3.6 %collective-permute-start.27 = (f32[6,8,256]{2,1,0:T(8,128)S(1)}, f32[6,8,256]{2,1,0:T(8,128)S(1)}, u32[]{:S(2)}, u32[]{:S(2)}) collective-permute-start(f32[6,8,256]{2,1,0:T(8,128)S(1)} %get-tuple-element.123), channel_id=1, source_target_pairs={{0,16},{1,17},{2,18},{3,19},{4,20},{5,21},{6,22},{7,23},{8,24},{9,... | collective-permute-start | bytes 147464 | tf_op jit(solution)/shard_map/ppermute | solution.py:349
  63.4 3.1 %collective-permute-start.25 = (f32[8,128]{1,0:T(8,128)S(1)}, f32[8,128]{1,0:T(8,128)S(1)}, u32[]{:S(2)}, u32[]{:S(2)}) collective-permute-start(f32[8,128]{1,0:T(8,128)S(1)} %get-tuple-element.119), channel_id=1, source_target_pairs={{0,240},{1,241},{2,242},{3,243},{4,244},{5,245},{6,246},{7,247},{8... | collective-permute-start | bytes 12296 | tf_op jit(solution)/shard_map/ppermute | solution.py:347
  66.8 0.6 collective-permute-start.29
  67.6 3.2 %collective-permute-done.28.span_odd = f32[16,256]{1,0:T(8,128)S(1)} collective-permute-done((f32[16,256]{1,0:T(8,128)S(1)}, f32[16,256]{1,0:T(8,128)S(1)}, u32[]{:S(2)}, u32[]{:S(2)}) %collective-permute-start.28) | collective-permute-done | bytes 16416 | tf_op jit(solution)/shard_map/ppermute | solution.py:350
  71.3 0.8 %last.1 = (f32[6,16,256]{2,1,0:T(8,128)}, f32[6,16,256]{2,1,0:T(8,128)}) custom-call(f32[8,128]{1,0:T(8,128)S(1)} %collective-permute-done.25.cut, f32[7,8,256]{2,1,0:T(8,128)S(1)} %collective-permute-done.26.chord_odd, f32[3,16,128]{2,1,0:T(8,128)S(1)} %get-tuple-element.71.masks, bf16[6,6,2,16,256]{4,3,2,1,0:T(8,128)(2,1)S(1)} %bitcast.19, ...), custom_call_target="tpu_custom_call" | custom-call | flops 1000 | tf_op jit(solution)/shard_map/last/pallas_call | solution.py:281
  (63 shorter events, 5.5 us)
Async XLA Ops:
  0.6 12.9 %copy-start.1 = (bf16[6,6,2,8,256]{4,3,2,1,0:T(8,128)(2,1)S(1)}, bf16[6,6,2,8,256]{4,3,2,1,0:T(8,128)(2,1)}, u32[]{:S(2)}) copy-start(bf16[6,6,2,8,256]{4,3,2,1,0:T(8,128)(2,1)} %param.9) | copy-start | bytes 884740
  0.7 12.9 %copy-start.3 = (s32[2,8]{1,0:T(2,128)S(1)}, s32[2,8]{1,0:T(2,128)}, u32[]{:S(2)}) copy-start(s32[2,8]{1,0:T(2,128)} %codes.1) | copy-start | bytes 196
  2.2 14.3 %collective-permute-start.1 = (f32[7,8,256]{2,1,0:T(8,128)S(1)}, f32[7,8,256]{2,1,0:T(8,128)S(1)}, u32[]{:S(2)}, u32[]{:S(2)}) collective-permute-start(f32[7,8,256]{2,1,0:T(8,128)S(1)} %get-tuple-element.67), channel_id=1, source_target_pairs={{0,1},{1,0},{2,3},{3,2},{4,5},{5,4},{6,7},{7,6},{8,9},{9,8},{10,11... | collective-permute-start | bytes 172040 | tf_op jit(solution)/shard_map/ppermute | solution.py:348
  2.3 14.2 %collective-permute-start.2 = (f32[6,8,256]{2,1,0:T(8,128)S(1)}, f32[6,8,256]{2,1,0:T(8,128)S(1)}, u32[]{:S(2)}, u32[]{:S(2)}) collective-permute-start(f32[6,8,256]{2,1,0:T(8,128)S(1)} %get-tuple-element.73), channel_id=1, source_target_pairs={{0,16},{1,17},{2,18},{3,19},{4,20},{5,21},{6,22},{7,23},{8,24},{9,... | collective-permute-start | bytes 147464 | tf_op jit(solution)/shard_map/ppermute | solution.py:349
  5.3 11.5 %collective-permute-start = (f32[8,128]{1,0:T(8,128)S(1)}, f32[8,128]{1,0:T(8,128)S(1)}, u32[]{:S(2)}, u32[]{:S(2)}) collective-permute-start(f32[8,128]{1,0:T(8,128)S(1)} %get-tuple-element.66), channel_id=1, source_target_pairs={{0,240},{1,241},{2,242},{3,243},{4,244},{5,245},{6,246},{7,247},{8... | collective-permute-start | bytes 12296 | tf_op jit(solution)/shard_map/ppermute | solution.py:347
  12.3 4.2 %collective-permute-start.3 = (f32[16,256]{1,0:T(8,128)S(1)}, f32[16,256]{1,0:T(8,128)S(1)}, u32[]{:S(2)}, u32[]{:S(2)}) collective-permute-start(f32[16,256]{1,0:T(8,128)S(1)} %get-tuple-element.74), channel_id=1, source_target_pairs={{0,16},{1,2},{2,1},{3,4},{4,3},{5,6},{6,5},{7,8},{8,7},{9,10},{10,... | collective-permute-start | bytes 49160 | tf_op jit(solution)/shard_map/ppermute | solution.py:350
  12.4 4.1 %collective-permute-start.4 = (f32[24,256]{1,0:T(8,128)S(1)}, f32[24,256]{1,0:T(8,128)S(1)}, u32[]{:S(2)}, u32[]{:S(2)}) collective-permute-start(f32[24,256]{1,0:T(8,128)S(1)} %get-tuple-element.75), channel_id=1, source_target_pairs={{0,1},{1,0},{2,3},{3,2},{4,5},{5,4},{6,7},{7,6},{8,9},{9,8},{10,11... | collective-permute-start | bytes 73736 | tf_op jit(solution)/shard_map/ppermute | solution.py:351
  17.1 10.5 %collective-permute-start.6 = (f32[7,8,256]{2,1,0:T(8,128)S(1)}, f32[7,8,256]{2,1,0:T(8,128)S(1)}, u32[]{:S(2)}, u32[]{:S(2)}) collective-permute-start(f32[7,8,256]{2,1,0:T(8,128)S(1)} %get-tuple-element.80), channel_id=1, source_target_pairs={{0,1},{1,0},{2,3},{3,2},{4,5},{5,4},{6,7},{7,6},{8,9},{9,8},{10,11... | collective-permute-start | bytes 172040 | tf_op jit(solution)/shard_map/ppermute | solution.py:348
  17.2 10.4 %collective-permute-start.7 = (f32[6,8,256]{2,1,0:T(8,128)S(1)}, f32[6,8,256]{2,1,0:T(8,128)S(1)}, u32[]{:S(2)}, u32[]{:S(2)}) collective-permute-start(f32[6,8,256]{2,1,0:T(8,128)S(1)} %get-tuple-element.83), channel_id=1, source_target_pairs={{0,16},{1,17},{2,18},{3,19},{4,20},{5,21},{6,22},{7,23},{8,24},{9,... | collective-permute-start | bytes 147464 | tf_op jit(solution)/shard_map/ppermute | solution.py:349
  20.8 7.8 %collective-permute-start.5 = (f32[8,128]{1,0:T(8,128)S(1)}, f32[8,128]{1,0:T(8,128)S(1)}, u32[]{:S(2)}, u32[]{:S(2)}) collective-permute-start(f32[8,128]{1,0:T(8,128)S(1)} %get-tuple-element.79), channel_id=1, source_target_pairs={{0,240},{1,241},{2,242},{3,243},{4,244},{5,245},{6,246},{7,247},{8... | collective-permute-start | bytes 12296 | tf_op jit(solution)/shard_map/ppermute | solution.py:347
  23.5 4.2 %collective-permute-start.8 = (f32[16,256]{1,0:T(8,128)S(1)}, f32[16,256]{1,0:T(8,128)S(1)}, u32[]{:S(2)}, u32[]{:S(2)}) collective-permute-start(f32[16,256]{1,0:T(8,128)S(1)} %get-tuple-element.84), channel_id=1, source_target_pairs={{0,16},{1,2},{2,1},{3,4},{4,3},{5,6},{6,5},{7,8},{8,7},{9,10},{10,... | collective-permute-start | bytes 49160 | tf_op jit(solution)/shard_map/ppermute | solution.py:350
  23.6 4.1 %collective-permute-start.9 = (f32[24,256]{1,0:T(8,128)S(1)}, f32[24,256]{1,0:T(8,128)S(1)}, u32[]{:S(2)}, u32[]{:S(2)}) collective-permute-start(f32[24,256]{1,0:T(8,128)S(1)} %get-tuple-element.85), channel_id=1, source_target_pairs={{0,1},{1,0},{2,3},{3,2},{4,5},{5,4},{6,7},{7,6},{8,9},{9,8},{10,11... | collective-permute-start | bytes 73736 | tf_op jit(solution)/shard_map/ppermute | solution.py:351
  28.8 8.9 %collective-permute-start.11 = (f32[7,8,256]{2,1,0:T(8,128)S(1)}, f32[7,8,256]{2,1,0:T(8,128)S(1)}, u32[]{:S(2)}, u32[]{:S(2)}) collective-permute-start(f32[7,8,256]{2,1,0:T(8,128)S(1)} %get-tuple-element.90), channel_id=1, source_target_pairs={{0,1},{1,0},{2,3},{3,2},{4,5},{5,4},{6,7},{7,6},{8,9},{9,8},{10,11... | collective-permute-start | bytes 172040 | tf_op jit(solution)/shard_map/ppermute | solution.py:348
  28.9 8.8 %collective-permute-start.12 = (f32[6,8,256]{2,1,0:T(8,128)S(1)}, f32[6,8,256]{2,1,0:T(8,128)S(1)}, u32[]{:S(2)}, u32[]{:S(2)}) collective-permute-start(f32[6,8,256]{2,1,0:T(8,128)S(1)} %get-tuple-element.93), channel_id=1, source_target_pairs={{0,16},{1,17},{2,18},{3,19},{4,20},{5,21},{6,22},{7,23},{8,24},{9,... | collective-permute-start | bytes 147464 | tf_op jit(solution)/shard_map/ppermute | solution.py:349
  30.3 7.8 %collective-permute-start.10 = (f32[8,128]{1,0:T(8,128)S(1)}, f32[8,128]{1,0:T(8,128)S(1)}, u32[]{:S(2)}, u32[]{:S(2)}) collective-permute-start(f32[8,128]{1,0:T(8,128)S(1)} %get-tuple-element.89), channel_id=1, source_target_pairs={{0,240},{1,241},{2,242},{3,243},{4,244},{5,245},{6,246},{7,247},{8... | collective-permute-start | bytes 12296 | tf_op jit(solution)/shard_map/ppermute | solution.py:347
  33.5 4.2 %collective-permute-start.13 = (f32[16,256]{1,0:T(8,128)S(1)}, f32[16,256]{1,0:T(8,128)S(1)}, u32[]{:S(2)}, u32[]{:S(2)}) collective-permute-start(f32[16,256]{1,0:T(8,128)S(1)} %get-tuple-element.94), channel_id=1, source_target_pairs={{0,16},{1,2},{2,1},{3,4},{4,3},{5,6},{6,5},{7,8},{8,7},{9,10},{10,... | collective-permute-start | bytes 49160 | tf_op jit(solution)/shard_map/ppermute | solution.py:350
  33.6 4.1 %collective-permute-start.14 = (f32[24,256]{1,0:T(8,128)S(1)}, f32[24,256]{1,0:T(8,128)S(1)}, u32[]{:S(2)}, u32[]{:S(2)}) collective-permute-start(f32[24,256]{1,0:T(8,128)S(1)} %get-tuple-element.95), channel_id=1, source_target_pairs={{0,1},{1,0},{2,3},{3,2},{4,5},{5,4},{6,7},{7,6},{8,9},{9,8},{10,11... | collective-permute-start | bytes 73736 | tf_op jit(solution)/shard_map/ppermute | solution.py:351
  38.4 11.2 %collective-permute-start.16 = (f32[7,8,256]{2,1,0:T(8,128)S(1)}, f32[7,8,256]{2,1,0:T(8,128)S(1)}, u32[]{:S(2)}, u32[]{:S(2)}) collective-permute-start(f32[7,8,256]{2,1,0:T(8,128)S(1)} %get-tuple-element.100), channel_id=1, source_target_pairs={{0,1},{1,0},{2,3},{3,2},{4,5},{5,4},{6,7},{7,6},{8,9},{9,8},{10,11... | collective-permute-start | bytes 172040 | tf_op jit(solution)/shard_map/ppermute | solution.py:348
  38.5 11.1 %collective-permute-start.17 = (f32[6,8,256]{2,1,0:T(8,128)S(1)}, f32[6,8,256]{2,1,0:T(8,128)S(1)}, u32[]{:S(2)}, u32[]{:S(2)}) collective-permute-start(f32[6,8,256]{2,1,0:T(8,128)S(1)} %get-tuple-element.103), channel_id=1, source_target_pairs={{0,16},{1,17},{2,18},{3,19},{4,20},{5,21},{6,22},{7,23},{8,24},{9,... | collective-permute-start | bytes 147464 | tf_op jit(solution)/shard_map/ppermute | solution.py:349
  42.1 7.8 %collective-permute-start.15 = (f32[8,128]{1,0:T(8,128)S(1)}, f32[8,128]{1,0:T(8,128)S(1)}, u32[]{:S(2)}, u32[]{:S(2)}) collective-permute-start(f32[8,128]{1,0:T(8,128)S(1)} %get-tuple-element.99), channel_id=1, source_target_pairs={{0,240},{1,241},{2,242},{3,243},{4,244},{5,245},{6,246},{7,247},{8... | collective-permute-start | bytes 12296 | tf_op jit(solution)/shard_map/ppermute | solution.py:347
  45.4 4.2 %collective-permute-start.18 = (f32[16,256]{1,0:T(8,128)S(1)}, f32[16,256]{1,0:T(8,128)S(1)}, u32[]{:S(2)}, u32[]{:S(2)}) collective-permute-start(f32[16,256]{1,0:T(8,128)S(1)} %get-tuple-element.104), channel_id=1, source_target_pairs={{0,16},{1,2},{2,1},{3,4},{4,3},{5,6},{6,5},{7,8},{8,7},{9,10},{10,... | collective-permute-start | bytes 49160 | tf_op jit(solution)/shard_map/ppermute | solution.py:350
  45.5 4.1 %collective-permute-start.19 = (f32[24,256]{1,0:T(8,128)S(1)}, f32[24,256]{1,0:T(8,128)S(1)}, u32[]{:S(2)}, u32[]{:S(2)}) collective-permute-start(f32[24,256]{1,0:T(8,128)S(1)} %get-tuple-element.105), channel_id=1, source_target_pairs={{0,1},{1,0},{2,3},{3,2},{4,5},{5,4},{6,7},{7,6},{8,9},{9,8},{10,11... | collective-permute-start | bytes 73736 | tf_op jit(solution)/shard_map/ppermute | solution.py:351
  50.2 9.0 %collective-permute-start.21 = (f32[7,8,256]{2,1,0:T(8,128)S(1)}, f32[7,8,256]{2,1,0:T(8,128)S(1)}, u32[]{:S(2)}, u32[]{:S(2)}) collective-permute-start(f32[7,8,256]{2,1,0:T(8,128)S(1)} %get-tuple-element.110), channel_id=1, source_target_pairs={{0,1},{1,0},{2,3},{3,2},{4,5},{5,4},{6,7},{7,6},{8,9},{9,8},{10,11... | collective-permute-start | bytes 172040 | tf_op jit(solution)/shard_map/ppermute | solution.py:348
  50.3 8.9 %collective-permute-start.22 = (f32[6,8,256]{2,1,0:T(8,128)S(1)}, f32[6,8,256]{2,1,0:T(8,128)S(1)}, u32[]{:S(2)}, u32[]{:S(2)}) collective-permute-start(f32[6,8,256]{2,1,0:T(8,128)S(1)} %get-tuple-element.113), channel_id=1, source_target_pairs={{0,16},{1,17},{2,18},{3,19},{4,20},{5,21},{6,22},{7,23},{8,24},{9,... | collective-permute-start | bytes 147464 | tf_op jit(solution)/shard_map/ppermute | solution.py:349
  51.7 7.8 %collective-permute-start.20 = (f32[8,128]{1,0:T(8,128)S(1)}, f32[8,128]{1,0:T(8,128)S(1)}, u32[]{:S(2)}, u32[]{:S(2)}) collective-permute-start(f32[8,128]{1,0:T(8,128)S(1)} %get-tuple-element.109), channel_id=1, source_target_pairs={{0,240},{1,241},{2,242},{3,243},{4,244},{5,245},{6,246},{7,247},{8... | collective-permute-start | bytes 12296 | tf_op jit(solution)/shard_map/ppermute | solution.py:347
  55.0 4.2 %collective-permute-start.23 = (f32[16,256]{1,0:T(8,128)S(1)}, f32[16,256]{1,0:T(8,128)S(1)}, u32[]{:S(2)}, u32[]{:S(2)}) collective-permute-start(f32[16,256]{1,0:T(8,128)S(1)} %get-tuple-element.114), channel_id=1, source_target_pairs={{0,16},{1,2},{2,1},{3,4},{4,3},{5,6},{6,5},{7,8},{8,7},{9,10},{10,... | collective-permute-start | bytes 49160 | tf_op jit(solution)/shard_map/ppermute | solution.py:350
  55.1 4.1 %collective-permute-start.24 = (f32[24,256]{1,0:T(8,128)S(1)}, f32[24,256]{1,0:T(8,128)S(1)}, u32[]{:S(2)}, u32[]{:S(2)}) collective-permute-start(f32[24,256]{1,0:T(8,128)S(1)} %get-tuple-element.115), channel_id=1, source_target_pairs={{0,1},{1,0},{2,3},{3,2},{4,5},{5,4},{6,7},{7,6},{8,9},{9,8},{10,11... | collective-permute-start | bytes 73736 | tf_op jit(solution)/shard_map/ppermute | solution.py:351
  59.8 11.1 %collective-permute-start.26 = (f32[7,8,256]{2,1,0:T(8,128)S(1)}, f32[7,8,256]{2,1,0:T(8,128)S(1)}, u32[]{:S(2)}, u32[]{:S(2)}) collective-permute-start(f32[7,8,256]{2,1,0:T(8,128)S(1)} %get-tuple-element.120), channel_id=1, source_target_pairs={{0,1},{1,0},{2,3},{3,2},{4,5},{5,4},{6,7},{7,6},{8,9},{9,8},{10,11... | collective-permute-start | bytes 172040 | tf_op jit(solution)/shard_map/ppermute | solution.py:348
  59.9 11.0 %collective-permute-start.27 = (f32[6,8,256]{2,1,0:T(8,128)S(1)}, f32[6,8,256]{2,1,0:T(8,128)S(1)}, u32[]{:S(2)}, u32[]{:S(2)}) collective-permute-start(f32[6,8,256]{2,1,0:T(8,128)S(1)} %get-tuple-element.123), channel_id=1, source_target_pairs={{0,16},{1,17},{2,18},{3,19},{4,20},{5,21},{6,22},{7,23},{8,24},{9,... | collective-permute-start | bytes 147464 | tf_op jit(solution)/shard_map/ppermute | solution.py:349
  63.4 7.8 %collective-permute-start.25 = (f32[8,128]{1,0:T(8,128)S(1)}, f32[8,128]{1,0:T(8,128)S(1)}, u32[]{:S(2)}, u32[]{:S(2)}) collective-permute-start(f32[8,128]{1,0:T(8,128)S(1)} %get-tuple-element.119), channel_id=1, source_target_pairs={{0,240},{1,241},{2,242},{3,243},{4,244},{5,245},{6,246},{7,247},{8... | collective-permute-start | bytes 12296 | tf_op jit(solution)/shard_map/ppermute | solution.py:347
  66.7 4.2 %collective-permute-start.28 = (f32[16,256]{1,0:T(8,128)S(1)}, f32[16,256]{1,0:T(8,128)S(1)}, u32[]{:S(2)}, u32[]{:S(2)}) collective-permute-start(f32[16,256]{1,0:T(8,128)S(1)} %get-tuple-element.124), channel_id=1, source_target_pairs={{0,16},{1,2},{2,1},{3,4},{4,3},{5,6},{6,5},{7,8},{8,7},{9,10},{10,... | collective-permute-start | bytes 49160 | tf_op jit(solution)/shard_map/ppermute | solution.py:350
  66.8 4.1 %collective-permute-start.29 = (f32[24,256]{1,0:T(8,128)S(1)}, f32[24,256]{1,0:T(8,128)S(1)}, u32[]{:S(2)}, u32[]{:S(2)}) collective-permute-start(f32[24,256]{1,0:T(8,128)S(1)} %get-tuple-element.125), channel_id=1, source_target_pairs={{0,1},{1,0},{2,3},{3,2},{4,5},{5,4},{6,7},{7,6},{8,9},{9,8},{10,11... | collective-permute-start | bytes 73736 | tf_op jit(solution)/shard_map/ppermute | solution.py:351
  (3 other events, 28.8 us)

commit v5 on v4

--- a/solution.py
+++ b/solution.py
@@ -84,24 +84,22 @@
     chord_products(up, down, chord_odd_ref, chord_even_ref)
 
 
-def edges_kernel(adjoint, source, couplings, part_ref, span_odd_ref, span_even_ref):
+def edges_kernel(adjoint, couplings, span_odd_ref, span_even_ref):
     even_span = lax.axis_index("span") % 2 == 0
     inner_span = inner("span")
-    field = [adjoint[a] for a in range(6)]
-    plus = product(couplings, (3,), field)
-    minus = product(couplings, (2,), field)
+    last = iotas((16, 256))[0] % 8 == 7
+    made = [None] * 6
+    for a in range(6):
+        for b in range(6):
+            block = jnp.where(last, couplings[3, a, b], couplings[2, a, b]).astype(F32)
+            term = block * adjoint[a]
+            made[b] = term if a == 0 else made[b] + term
     for b in range(6):
         for c in range(2):
-            top, bottom = (minus[b][8 * c : 8 * c + 1], plus[b][8 * c + 7 : 8 * c + 8])
+            top, bottom = (made[b][8 * c : 8 * c + 1], made[b][8 * c + 7 : 8 * c + 8])
             at = 2 * b + c
             span_odd_ref[at : at + 1] = jnp.where(inner_span, jnp.where(even_span, top, bottom), 0.0)
             span_even_ref[at : at + 1] = jnp.where(even_span, bottom, top)
-    row, lane = iotas((16, 256))
-    row = row % 8
-    for b in range(6):
-        inside = jnp.where(row == 0, 0.0, pltpu.roll(plus[b], 1, 0))
-        inside = inside + jnp.where(row == 7, 0.0, pltpu.roll(minus[b], 15, 0))
-        part_ref[b] = source[b] - inside
 
 
 def load_kernel(couplings, adjoint, *out):
@@ -120,23 +118,30 @@
         copy.wait()
 
 
-def inside_kernel(part, diag_block, couplings, adjoint, out):
+def inside_kernel(sent, source, diag_block, couplings, adjoint, out):
     field = [adjoint[a] for a in range(6)]
+    row, lane = iotas((16, 256))
+    row = row % 8
+    span_plus = product(couplings, (3,), field)
+    span_minus = product(couplings, (2,), field)
+    for b in range(6):
+        inside = jnp.where(row == 0, 0.0, pltpu.roll(span_plus[b], 1, 0))
+        inside = inside + jnp.where(row == 7, 0.0, pltpu.roll(span_minus[b], 15, 0))
+        out[b] = source[b] - inside
     own = product(diag_block, (), field)
     up = product_rows(couplings, (1,), field, 0)
     down = product_rows(couplings, (0,), field, 8)
     plus = product(couplings, (5,), field)
     minus = product(couplings, (4,), field)
-    lane = iotas((16, 256))[1]
     for b in range(6):
         inside = own[b] + jnp.where(lane == 0, 0.0, pltpu.roll(plus[b], 1, 1))
         inside = inside + jnp.where(lane == 255, 0.0, pltpu.roll(minus[b], 255, 1))
         inside = inside + jnp.concatenate([down[b], up[b]], axis=0)
-        out[b] = part[b] - inside
-
-
-def first_inside_kernel(part, diag_block, couplings, adjoint, partner, codes, out, masks_ref):
-    inside_kernel(part, diag_block, couplings, adjoint, out)
+        out[b] = out[b] - inside
+
+
+def first_inside_kernel(sent, source, diag_block, couplings, adjoint, partner, codes, out, masks_ref):
+    inside_kernel(sent, source, diag_block, couplings, adjoint, out)
     here, there = iotas((8, 8))
     for c in range(2):
         rows = jnp.broadcast_to(codes[c : c + 1, :], (8, 8))
@@ -294,7 +299,7 @@
 SLAB = (6, 8, 256)
 ROWS = (16, 256)
 FIRST = [(8, 128), (7, 8, 256), SLAB]
-SECOND = [FIELD, ROWS, (24, 256)]
+SECOND = [ROWS, (24, 256)]
 
 
 def load(couplings, adjoint):
@@ -360,9 +365,9 @@
     line_inverse = line_inverse.reshape(6, 6, 2, 16, 256)
     adjoint, couplings, *far = load(couplings, adjoint)
     for sweep in range(SWEEPS):
-        part, *near = call(edges_kernel, "edges", (adjoint, source, couplings), SECOND, 1_000)
+        near = call(edges_kernel, "edges", (adjoint, couplings), SECOND, 1_000)
         got = exchange((*far, *near))
-        held = (part, diag_block, couplings, adjoint)
+        held = (near[0], source, diag_block, couplings, adjoint)
         if sweep == 0:
             part, masks = call(
                 first_inside_kernel, "inside_masks", (*held, partner.reshape(1, 2), codes), [FIELD, (3, 16, 128)], INSIDE

time: 72.4 us -> 72.3 us (level)
  waiting for transfers between devices: 19.3 us -> 18.4 us
    ppermute x6, waiting for transfers between devices: 18.3 us -> 17 us  [exchange(): lax.ppermute(span_odd, ('chord', 'span'), pairs(chords, spans, 'span', 1))]
  transfers between devices with their start and end apart: 30 -> 30, of which waited for: 10 -> 11; matrix products, arithmetic and copies ran while one was open for 0% -> 0% of each run, Pallas kernels for 6% -> 7%
where the time goes in v5:
time: 72.3 us; the launch traced here: 72.2 us
  starting transfers between devices  44.3 us (61%)
  waiting for transfers between devices  18.4 us (25%)
  Pallas kernels  8.3 us (11%)
  between operations  1.08 us (1%)
    ppermute x6, starting transfers between devices, exchange(): cut = lax.ppermute(cut, ('chord', 'span'), mirrors(chords, spans))  21.7 us
    ppermute x6, waiting for transfers between devices, exchange(): lax.ppermute(span_odd, ('chord', 'span'), pairs(chords, spans, 'span', 1))  17 us
    ppermute x6, starting transfers between devices, exchange(): lax.ppermute(chord_even, ('chord', 'span'), pairs(chords, spans, 'chord',...  16.5 us
    pallas_call x24, Pallas kernels, call(): pl.pallas_call(kernel, name=name, out_shape=[space(s, F32) for s in shape...  6.76 us
    ppermute x6, starting transfers between devices, exchange(): lax.ppermute(span_even, ('chord', 'span'), pairs(chords, spans, 'span', 0))  4.96 us
    pallas_call x1, Pallas kernels, load(): pl.pallas_call(load_kernel, name='load', out_shape=[*held, *(pltpu.VMEM(s...  1.54 us
  transfers between devices with their start and end apart: 30, of which 11 were waited for; matrix products, arithmetic and copies ran while one was open for 0% of the time, Pallas kernels for 7%

profile of v5, /device:TPU:8, one launch (start us, length us, event | category | flops | bytes accessed | tf_op | source)
XLA Modules:
  0.0 72.2 jit_solution(4056316280499789425)
XLA Ops:
  0.7 1.5 %load.1 = (f32[6,16,256]{2,1,0:T(8,128)S(1)}, bf16[6,6,6,16,256]{4,3,2,1,0:T(8,128)(2,1)S(1)}, f32[8,128]{1,0:T(8,128)S(1)}, f32[7,8,256]{2,1,0:T(8,128)S(1)}, f32[6,8,256]{2,1,0:T(8,128)S(1)}) custom-call(bf16[6,6,6,16,256]{4,3,2,1,0:T(8,128)(2,1)} %bitcast.33, f32[6,16,256]{2,1,0:T(8,128)} %bitcast.34), custom_call_target="tpu_custom_call" | custom-call | flops 1000000 | tf_op jit(solution)/shard_map/load/pallas_call | solution.py:311
  2.3 3.0 %collective-permute-start.2 = (f32[6,8,256]{2,1,0:T(8,128)S(1)}, f32[6,8,256]{2,1,0:T(8,128)S(1)}, u32[]{:S(2)}, u32[]{:S(2)}) collective-permute-start(f32[6,8,256]{2,1,0:T(8,128)S(1)} %get-tuple-element.67), channel_id=1, source_target_pairs={{0,16},{1,17},{2,18},{3,19},{4,20},{5,21},{6,22},{7,23},{8,24},{9,... | collective-permute-start | bytes 147464 | tf_op jit(solution)/shard_map/ppermute | solution.py:354
  5.3 6.9 %collective-permute-start = (f32[8,128]{1,0:T(8,128)S(1)}, f32[8,128]{1,0:T(8,128)S(1)}, u32[]{:S(2)}, u32[]{:S(2)}) collective-permute-start(f32[8,128]{1,0:T(8,128)S(1)} %get-tuple-element.60), channel_id=1, source_target_pairs={{0,240},{1,241},{2,242},{3,243},{4,244},{5,245},{6,246},{7,247},{8... | collective-permute-start | bytes 12296 | tf_op jit(solution)/shard_map/ppermute | solution.py:352
  12.4 1.1 %collective-permute-start.4 = (f32[24,256]{1,0:T(8,128)S(1)}, f32[24,256]{1,0:T(8,128)S(1)}, u32[]{:S(2)}, u32[]{:S(2)}) collective-permute-start(f32[24,256]{1,0:T(8,128)S(1)} %get-tuple-element.68), channel_id=1, source_target_pairs={{0,1},{1,0},{2,3},{3,2},{4,5},{5,4},{6,7},{7,6},{8,9},{9,8},{10,11... | collective-permute-start | bytes 73736 | tf_op jit(solution)/shard_map/ppermute | solution.py:356
  13.5 0.4 inside_masks.1
  13.9 2.5 %collective-permute-done.3.span_odd = f32[16,256]{1,0:T(8,128)S(1)} collective-permute-done((f32[16,256]{1,0:T(8,128)S(1)}, f32[16,256]{1,0:T(8,128)S(1)}, u32[]{:S(2)}, u32[]{:S(2)}) %collective-permute-start.3) | collective-permute-done | bytes 16416 | tf_op jit(solution)/shard_map/ppermute | solution.py:355
  17.1 3.6 %collective-permute-start.7 = (f32[6,8,256]{2,1,0:T(8,128)S(1)}, f32[6,8,256]{2,1,0:T(8,128)S(1)}, u32[]{:S(2)}, u32[]{:S(2)}) collective-permute-start(f32[6,8,256]{2,1,0:T(8,128)S(1)} %get-tuple-element.76), channel_id=1, source_target_pairs={{0,16},{1,17},{2,18},{3,19},{4,20},{5,21},{6,22},{7,23},{8,24},{9,... | collective-permute-start | bytes 147464 | tf_op jit(solution)/shard_map/ppermute | solution.py:354
  20.7 2.6 %collective-permute-start.5 = (f32[8,128]{1,0:T(8,128)S(1)}, f32[8,128]{1,0:T(8,128)S(1)}, u32[]{:S(2)}, u32[]{:S(2)}) collective-permute-start(f32[8,128]{1,0:T(8,128)S(1)} %get-tuple-element.72), channel_id=1, source_target_pairs={{0,240},{1,241},{2,242},{3,243},{4,244},{5,245},{6,246},{7,247},{8... | collective-permute-start | bytes 12296 | tf_op jit(solution)/shard_map/ppermute | solution.py:352
  23.5 1.1 %collective-permute-start.9 = (f32[24,256]{1,0:T(8,128)S(1)}, f32[24,256]{1,0:T(8,128)S(1)}, u32[]{:S(2)}, u32[]{:S(2)}) collective-permute-start(f32[24,256]{1,0:T(8,128)S(1)} %get-tuple-element.77), channel_id=1, source_target_pairs={{0,1},{1,0},{2,3},{3,2},{4,5},{5,4},{6,7},{7,6},{8,9},{9,8},{10,11... | collective-permute-start | bytes 73736 | tf_op jit(solution)/shard_map/ppermute | solution.py:356
  24.6 0.4 inside.5.part
  25.0 2.5 %collective-permute-done.8.span_odd = f32[16,256]{1,0:T(8,128)S(1)} collective-permute-done((f32[16,256]{1,0:T(8,128)S(1)}, f32[16,256]{1,0:T(8,128)S(1)}, u32[]{:S(2)}, u32[]{:S(2)}) %collective-permute-start.8) | collective-permute-done | bytes 16416 | tf_op jit(solution)/shard_map/ppermute | solution.py:355
  27.9 0.6 collective-permute-done.5.cut
  28.9 1.4 %collective-permute-start.12 = (f32[6,8,256]{2,1,0:T(8,128)S(1)}, f32[6,8,256]{2,1,0:T(8,128)S(1)}, u32[]{:S(2)}, u32[]{:S(2)}) collective-permute-start(f32[6,8,256]{2,1,0:T(8,128)S(1)} %get-tuple-element.85), channel_id=1, source_target_pairs={{0,16},{1,17},{2,18},{3,19},{4,20},{5,21},{6,22},{7,23},{8,24},{9,... | collective-permute-start | bytes 147464 | tf_op jit(solution)/shard_map/ppermute | solution.py:354
  30.2 3.0 %collective-permute-start.10 = (f32[8,128]{1,0:T(8,128)S(1)}, f32[8,128]{1,0:T(8,128)S(1)}, u32[]{:S(2)}, u32[]{:S(2)}) collective-permute-start(f32[8,128]{1,0:T(8,128)S(1)} %get-tuple-element.81), channel_id=1, source_target_pairs={{0,240},{1,241},{2,242},{3,243},{4,244},{5,245},{6,246},{7,247},{8... | collective-permute-start | bytes 12296 | tf_op jit(solution)/shard_map/ppermute | solution.py:352
  33.5 0.7 collective-permute-start.14
  34.2 0.4 inside.6.part
  34.6 2.9 %collective-permute-done.13.span_odd = f32[16,256]{1,0:T(8,128)S(1)} collective-permute-done((f32[16,256]{1,0:T(8,128)S(1)}, f32[16,256]{1,0:T(8,128)S(1)}, u32[]{:S(2)}, u32[]{:S(2)}) %collective-permute-start.13) | collective-permute-done | bytes 16416 | tf_op jit(solution)/shard_map/ppermute | solution.py:355
  38.4 3.6 %collective-permute-start.17 = (f32[6,8,256]{2,1,0:T(8,128)S(1)}, f32[6,8,256]{2,1,0:T(8,128)S(1)}, u32[]{:S(2)}, u32[]{:S(2)}) collective-permute-start(f32[6,8,256]{2,1,0:T(8,128)S(1)} %get-tuple-element.94), channel_id=1, source_target_pairs={{0,16},{1,17},{2,18},{3,19},{4,20},{5,21},{6,22},{7,23},{8,24},{9,... | collective-permute-start | bytes 147464 | tf_op jit(solution)/shard_map/ppermute | solution.py:354
  42.0 3.0 %collective-permute-start.15 = (f32[8,128]{1,0:T(8,128)S(1)}, f32[8,128]{1,0:T(8,128)S(1)}, u32[]{:S(2)}, u32[]{:S(2)}) collective-permute-start(f32[8,128]{1,0:T(8,128)S(1)} %get-tuple-element.90), channel_id=1, source_target_pairs={{0,240},{1,241},{2,242},{3,243},{4,244},{5,245},{6,246},{7,247},{8... | collective-permute-start | bytes 12296 | tf_op jit(solution)/shard_map/ppermute | solution.py:352
  45.3 0.7 collective-permute-start.19
  46.0 0.4 inside.7.part
  46.4 2.9 %collective-permute-done.18.span_odd = f32[16,256]{1,0:T(8,128)S(1)} collective-permute-done((f32[16,256]{1,0:T(8,128)S(1)}, f32[16,256]{1,0:T(8,128)S(1)}, u32[]{:S(2)}, u32[]{:S(2)}) %collective-permute-start.18) | collective-permute-done | bytes 16416 | tf_op jit(solution)/shard_map/ppermute | solution.py:355
  50.2 1.4 %collective-permute-start.22 = (f32[6,8,256]{2,1,0:T(8,128)S(1)}, f32[6,8,256]{2,1,0:T(8,128)S(1)}, u32[]{:S(2)}, u32[]{:S(2)}) collective-permute-start(f32[6,8,256]{2,1,0:T(8,128)S(1)} %get-tuple-element.103), channel_id=1, source_target_pairs={{0,16},{1,17},{2,18},{3,19},{4,20},{5,21},{6,22},{7,23},{8,24},{9,... | collective-permute-start | bytes 147464 | tf_op jit(solution)/shard_map/ppermute | solution.py:354
  51.6 3.2 %collective-permute-start.20 = (f32[8,128]{1,0:T(8,128)S(1)}, f32[8,128]{1,0:T(8,128)S(1)}, u32[]{:S(2)}, u32[]{:S(2)}) collective-permute-start(f32[8,128]{1,0:T(8,128)S(1)} %get-tuple-element.99), channel_id=1, source_target_pairs={{0,240},{1,241},{2,242},{3,243},{4,244},{5,245},{6,246},{7,247},{8... | collective-permute-start | bytes 12296 | tf_op jit(solution)/shard_map/ppermute | solution.py:352
  54.9 0.6 collective-permute-start.24
  55.9 3.1 %collective-permute-done.23.span_odd = f32[16,256]{1,0:T(8,128)S(1)} collective-permute-done((f32[16,256]{1,0:T(8,128)S(1)}, f32[16,256]{1,0:T(8,128)S(1)}, u32[]{:S(2)}, u32[]{:S(2)}) %collective-permute-start.23) | collective-permute-done | bytes 16416 | tf_op jit(solution)/shard_map/ppermute | solution.py:355
  59.7 3.6 %collective-permute-start.27 = (f32[6,8,256]{2,1,0:T(8,128)S(1)}, f32[6,8,256]{2,1,0:T(8,128)S(1)}, u32[]{:S(2)}, u32[]{:S(2)}) collective-permute-start(f32[6,8,256]{2,1,0:T(8,128)S(1)} %get-tuple-element.112), channel_id=1, source_target_pairs={{0,16},{1,17},{2,18},{3,19},{4,20},{5,21},{6,22},{7,23},{8,24},{9,... | collective-permute-start | bytes 147464 | tf_op jit(solution)/shard_map/ppermute | solution.py:354
  63.4 3.0 %collective-permute-start.25 = (f32[8,128]{1,0:T(8,128)S(1)}, f32[8,128]{1,0:T(8,128)S(1)}, u32[]{:S(2)}, u32[]{:S(2)}) collective-permute-start(f32[8,128]{1,0:T(8,128)S(1)} %get-tuple-element.108), channel_id=1, source_target_pairs={{0,240},{1,241},{2,242},{3,243},{4,244},{5,245},{6,246},{7,247},{8... | collective-permute-start | bytes 12296 | tf_op jit(solution)/shard_map/ppermute | solution.py:352
  66.6 0.7 collective-permute-start.29
  67.3 0.4 inside.9.part
  67.7 2.9 %collective-permute-done.28.span_odd = f32[16,256]{1,0:T(8,128)S(1)} collective-permute-done((f32[16,256]{1,0:T(8,128)S(1)}, f32[16,256]{1,0:T(8,128)S(1)}, u32[]{:S(2)}, u32[]{:S(2)}) %collective-permute-start.28) | collective-permute-done | bytes 16416 | tf_op jit(solution)/shard_map/ppermute | solution.py:355
  71.2 0.8 %last.1 = (f32[6,16,256]{2,1,0:T(8,128)}, f32[6,16,256]{2,1,0:T(8,128)}) custom-call(f32[8,128]{1,0:T(8,128)S(1)} %collective-permute-done.25.cut, f32[7,8,256]{2,1,0:T(8,128)S(1)} %collective-permute-done.26.chord_odd, f32[3,16,128]{2,1,0:T(8,128)S(1)} %get-tuple-element.65.masks, bf16[6,6,2,16,256]{4,3,2,1,0:T(8,128)(2,1)S(1)} %bitcast.19, ...), custom_call_target="tpu_custom_call" | custom-call | flops 1000 | tf_op jit(solution)/shard_map/last/pallas_call | solution.py:286
  (63 shorter events, 6.0 us)
Async XLA Ops:
  0.6 12.9 %copy-start.1 = (bf16[6,6,2,8,256]{4,3,2,1,0:T(8,128)(2,1)S(1)}, bf16[6,6,2,8,256]{4,3,2,1,0:T(8,128)(2,1)}, u32[]{:S(2)}) copy-start(bf16[6,6,2,8,256]{4,3,2,1,0:T(8,128)(2,1)} %param.9) | copy-start | bytes 884740
  0.6 12.9 %copy-start.2 = (f32[6,2,8,256]{3,2,1,0:T(8,128)S(1)}, f32[6,2,8,256]{3,2,1,0:T(8,128)}, u32[]{:S(2)}) copy-start(f32[6,2,8,256]{3,2,1,0:T(8,128)} %param.8) | copy-start | bytes 294916
  2.2 14.2 %collective-permute-start.1 = (f32[7,8,256]{2,1,0:T(8,128)S(1)}, f32[7,8,256]{2,1,0:T(8,128)S(1)}, u32[]{:S(2)}, u32[]{:S(2)}) collective-permute-start(f32[7,8,256]{2,1,0:T(8,128)S(1)} %get-tuple-element.61), channel_id=1, source_target_pairs={{0,1},{1,0},{2,3},{3,2},{4,5},{5,4},{6,7},{7,6},{8,9},{9,8},{10,11... | collective-permute-start | bytes 172040 | tf_op jit(solution)/shard_map/ppermute | solution.py:353
  2.3 14.1 %collective-permute-start.2 = (f32[6,8,256]{2,1,0:T(8,128)S(1)}, f32[6,8,256]{2,1,0:T(8,128)S(1)}, u32[]{:S(2)}, u32[]{:S(2)}) collective-permute-start(f32[6,8,256]{2,1,0:T(8,128)S(1)} %get-tuple-element.67), channel_id=1, source_target_pairs={{0,16},{1,17},{2,18},{3,19},{4,20},{5,21},{6,22},{7,23},{8,24},{9,... | collective-permute-start | bytes 147464 | tf_op jit(solution)/shard_map/ppermute | solution.py:354
  5.3 11.5 %collective-permute-start = (f32[8,128]{1,0:T(8,128)S(1)}, f32[8,128]{1,0:T(8,128)S(1)}, u32[]{:S(2)}, u32[]{:S(2)}) collective-permute-start(f32[8,128]{1,0:T(8,128)S(1)} %get-tuple-element.60), channel_id=1, source_target_pairs={{0,240},{1,241},{2,242},{3,243},{4,244},{5,245},{6,246},{7,247},{8... | collective-permute-start | bytes 12296 | tf_op jit(solution)/shard_map/ppermute | solution.py:352
  12.3 4.2 %collective-permute-start.3 = (f32[16,256]{1,0:T(8,128)S(1)}, f32[16,256]{1,0:T(8,128)S(1)}, u32[]{:S(2)}, u32[]{:S(2)}) collective-permute-start(f32[16,256]{1,0:T(8,128)S(1)} %get-tuple-element.64.sent), channel_id=1, source_target_pairs={{0,16},{1,2},{2,1},{3,4},{4,3},{5,6},{6,5},{7,8},{8,7},{9,10},{10,... | collective-permute-start | bytes 49160 | tf_op jit(solution)/shard_map/ppermute | solution.py:355
  12.4 4.1 %collective-permute-start.4 = (f32[24,256]{1,0:T(8,128)S(1)}, f32[24,256]{1,0:T(8,128)S(1)}, u32[]{:S(2)}, u32[]{:S(2)}) collective-permute-start(f32[24,256]{1,0:T(8,128)S(1)} %get-tuple-element.68), channel_id=1, source_target_pairs={{0,1},{1,0},{2,3},{3,2},{4,5},{5,4},{6,7},{7,6},{8,9},{9,8},{10,11... | collective-permute-start | bytes 73736 | tf_op jit(solution)/shard_map/ppermute | solution.py:356
  17.0 10.5 %collective-permute-start.6 = (f32[7,8,256]{2,1,0:T(8,128)S(1)}, f32[7,8,256]{2,1,0:T(8,128)S(1)}, u32[]{:S(2)}, u32[]{:S(2)}) collective-permute-start(f32[7,8,256]{2,1,0:T(8,128)S(1)} %get-tuple-element.73), channel_id=1, source_target_pairs={{0,1},{1,0},{2,3},{3,2},{4,5},{5,4},{6,7},{7,6},{8,9},{9,8},{10,11... | collective-permute-start | bytes 172040 | tf_op jit(solution)/shard_map/ppermute | solution.py:353
  17.1 10.4 %collective-permute-start.7 = (f32[6,8,256]{2,1,0:T(8,128)S(1)}, f32[6,8,256]{2,1,0:T(8,128)S(1)}, u32[]{:S(2)}, u32[]{:S(2)}) collective-permute-start(f32[6,8,256]{2,1,0:T(8,128)S(1)} %get-tuple-element.76), channel_id=1, source_target_pairs={{0,16},{1,17},{2,18},{3,19},{4,20},{5,21},{6,22},{7,23},{8,24},{9,... | collective-permute-start | bytes 147464 | tf_op jit(solution)/shard_map/ppermute | solution.py:354
  20.7 7.8 %collective-permute-start.5 = (f32[8,128]{1,0:T(8,128)S(1)}, f32[8,128]{1,0:T(8,128)S(1)}, u32[]{:S(2)}, u32[]{:S(2)}) collective-permute-start(f32[8,128]{1,0:T(8,128)S(1)} %get-tuple-element.72), channel_id=1, source_target_pairs={{0,240},{1,241},{2,242},{3,243},{4,244},{5,245},{6,246},{7,247},{8... | collective-permute-start | bytes 12296 | tf_op jit(solution)/shard_map/ppermute | solution.py:352
  23.4 4.2 %collective-permute-start.8 = (f32[16,256]{1,0:T(8,128)S(1)}, f32[16,256]{1,0:T(8,128)S(1)}, u32[]{:S(2)}, u32[]{:S(2)}) collective-permute-start(f32[16,256]{1,0:T(8,128)S(1)} %get-tuple-element.75.sent), channel_id=1, source_target_pairs={{0,16},{1,2},{2,1},{3,4},{4,3},{5,6},{6,5},{7,8},{8,7},{9,10},{10,... | collective-permute-start | bytes 49160 | tf_op jit(solution)/shard_map/ppermute | solution.py:355
  23.5 4.1 %collective-permute-start.9 = (f32[24,256]{1,0:T(8,128)S(1)}, f32[24,256]{1,0:T(8,128)S(1)}, u32[]{:S(2)}, u32[]{:S(2)}) collective-permute-start(f32[24,256]{1,0:T(8,128)S(1)} %get-tuple-element.77), channel_id=1, source_target_pairs={{0,1},{1,0},{2,3},{3,2},{4,5},{5,4},{6,7},{7,6},{8,9},{9,8},{10,11... | collective-permute-start | bytes 73736 | tf_op jit(solution)/shard_map/ppermute | solution.py:356
  28.8 8.8 %collective-permute-start.11 = (f32[7,8,256]{2,1,0:T(8,128)S(1)}, f32[7,8,256]{2,1,0:T(8,128)S(1)}, u32[]{:S(2)}, u32[]{:S(2)}) collective-permute-start(f32[7,8,256]{2,1,0:T(8,128)S(1)} %get-tuple-element.82), channel_id=1, source_target_pairs={{0,1},{1,0},{2,3},{3,2},{4,5},{5,4},{6,7},{7,6},{8,9},{9,8},{10,11... | collective-permute-start | bytes 172040 | tf_op jit(solution)/shard_map/ppermute | solution.py:353
  28.9 8.7 %collective-permute-start.12 = (f32[6,8,256]{2,1,0:T(8,128)S(1)}, f32[6,8,256]{2,1,0:T(8,128)S(1)}, u32[]{:S(2)}, u32[]{:S(2)}) collective-permute-start(f32[6,8,256]{2,1,0:T(8,128)S(1)} %get-tuple-element.85), channel_id=1, source_target_pairs={{0,16},{1,17},{2,18},{3,19},{4,20},{5,21},{6,22},{7,23},{8,24},{9,... | collective-permute-start | bytes 147464 | tf_op jit(solution)/shard_map/ppermute | solution.py:354
  30.2 7.8 %collective-permute-start.10 = (f32[8,128]{1,0:T(8,128)S(1)}, f32[8,128]{1,0:T(8,128)S(1)}, u32[]{:S(2)}, u32[]{:S(2)}) collective-permute-start(f32[8,128]{1,0:T(8,128)S(1)} %get-tuple-element.81), channel_id=1, source_target_pairs={{0,240},{1,241},{2,242},{3,243},{4,244},{5,245},{6,246},{7,247},{8... | collective-permute-start | bytes 12296 | tf_op jit(solution)/shard_map/ppermute | solution.py:352
  33.4 4.2 %collective-permute-start.13 = (f32[16,256]{1,0:T(8,128)S(1)}, f32[16,256]{1,0:T(8,128)S(1)}, u32[]{:S(2)}, u32[]{:S(2)}) collective-permute-start(f32[16,256]{1,0:T(8,128)S(1)} %get-tuple-element.84.sent), channel_id=1, source_target_pairs={{0,16},{1,2},{2,1},{3,4},{4,3},{5,6},{6,5},{7,8},{8,7},{9,10},{10,... | collective-permute-start | bytes 49160 | tf_op jit(solution)/shard_map/ppermute | solution.py:355
  33.5 4.1 %collective-permute-start.14 = (f32[24,256]{1,0:T(8,128)S(1)}, f32[24,256]{1,0:T(8,128)S(1)}, u32[]{:S(2)}, u32[]{:S(2)}) collective-permute-start(f32[24,256]{1,0:T(8,128)S(1)} %get-tuple-element.86), channel_id=1, source_target_pairs={{0,1},{1,0},{2,3},{3,2},{4,5},{5,4},{6,7},{7,6},{8,9},{9,8},{10,11... | collective-permute-start | bytes 73736 | tf_op jit(solution)/shard_map/ppermute | solution.py:356
  38.3 11.0 %collective-permute-start.16 = (f32[7,8,256]{2,1,0:T(8,128)S(1)}, f32[7,8,256]{2,1,0:T(8,128)S(1)}, u32[]{:S(2)}, u32[]{:S(2)}) collective-permute-start(f32[7,8,256]{2,1,0:T(8,128)S(1)} %get-tuple-element.91), channel_id=1, source_target_pairs={{0,1},{1,0},{2,3},{3,2},{4,5},{5,4},{6,7},{7,6},{8,9},{9,8},{10,11... | collective-permute-start | bytes 172040 | tf_op jit(solution)/shard_map/ppermute | solution.py:353
  38.4 10.9 %collective-permute-start.17 = (f32[6,8,256]{2,1,0:T(8,128)S(1)}, f32[6,8,256]{2,1,0:T(8,128)S(1)}, u32[]{:S(2)}, u32[]{:S(2)}) collective-permute-start(f32[6,8,256]{2,1,0:T(8,128)S(1)} %get-tuple-element.94), channel_id=1, source_target_pairs={{0,16},{1,17},{2,18},{3,19},{4,20},{5,21},{6,22},{7,23},{8,24},{9,... | collective-permute-start | bytes 147464 | tf_op jit(solution)/shard_map/ppermute | solution.py:354
  42.0 7.8 %collective-permute-start.15 = (f32[8,128]{1,0:T(8,128)S(1)}, f32[8,128]{1,0:T(8,128)S(1)}, u32[]{:S(2)}, u32[]{:S(2)}) collective-permute-start(f32[8,128]{1,0:T(8,128)S(1)} %get-tuple-element.90), channel_id=1, source_target_pairs={{0,240},{1,241},{2,242},{3,243},{4,244},{5,245},{6,246},{7,247},{8... | collective-permute-start | bytes 12296 | tf_op jit(solution)/shard_map/ppermute | solution.py:352
  45.2 4.2 %collective-permute-start.18 = (f32[16,256]{1,0:T(8,128)S(1)}, f32[16,256]{1,0:T(8,128)S(1)}, u32[]{:S(2)}, u32[]{:S(2)}) collective-permute-start(f32[16,256]{1,0:T(8,128)S(1)} %get-tuple-element.93.sent), channel_id=1, source_target_pairs={{0,16},{1,2},{2,1},{3,4},{4,3},{5,6},{6,5},{7,8},{8,7},{9,10},{10,... | collective-permute-start | bytes 49160 | tf_op jit(solution)/shard_map/ppermute | solution.py:355
  45.3 4.1 %collective-permute-start.19 = (f32[24,256]{1,0:T(8,128)S(1)}, f32[24,256]{1,0:T(8,128)S(1)}, u32[]{:S(2)}, u32[]{:S(2)}) collective-permute-start(f32[24,256]{1,0:T(8,128)S(1)} %get-tuple-element.95), channel_id=1, source_target_pairs={{0,1},{1,0},{2,3},{3,2},{4,5},{5,4},{6,7},{7,6},{8,9},{9,8},{10,11... | collective-permute-start | bytes 73736 | tf_op jit(solution)/shard_map/ppermute | solution.py:356
  50.1 8.9 %collective-permute-start.21 = (f32[7,8,256]{2,1,0:T(8,128)S(1)}, f32[7,8,256]{2,1,0:T(8,128)S(1)}, u32[]{:S(2)}, u32[]{:S(2)}) collective-permute-start(f32[7,8,256]{2,1,0:T(8,128)S(1)} %get-tuple-element.100), channel_id=1, source_target_pairs={{0,1},{1,0},{2,3},{3,2},{4,5},{5,4},{6,7},{7,6},{8,9},{9,8},{10,11... | collective-permute-start | bytes 172040 | tf_op jit(solution)/shard_map/ppermute | solution.py:353
  50.2 8.8 %collective-permute-start.22 = (f32[6,8,256]{2,1,0:T(8,128)S(1)}, f32[6,8,256]{2,1,0:T(8,128)S(1)}, u32[]{:S(2)}, u32[]{:S(2)}) collective-permute-start(f32[6,8,256]{2,1,0:T(8,128)S(1)} %get-tuple-element.103), channel_id=1, source_target_pairs={{0,16},{1,17},{2,18},{3,19},{4,20},{5,21},{6,22},{7,23},{8,24},{9,... | collective-permute-start | bytes 147464 | tf_op jit(solution)/shard_map/ppermute | solution.py:354
  51.6 7.8 %collective-permute-start.20 = (f32[8,128]{1,0:T(8,128)S(1)}, f32[8,128]{1,0:T(8,128)S(1)}, u32[]{:S(2)}, u32[]{:S(2)}) collective-permute-start(f32[8,128]{1,0:T(8,128)S(1)} %get-tuple-element.99), channel_id=1, source_target_pairs={{0,240},{1,241},{2,242},{3,243},{4,244},{5,245},{6,246},{7,247},{8... | collective-permute-start | bytes 12296 | tf_op jit(solution)/shard_map/ppermute | solution.py:352
  54.8 4.2 %collective-permute-start.23 = (f32[16,256]{1,0:T(8,128)S(1)}, f32[16,256]{1,0:T(8,128)S(1)}, u32[]{:S(2)}, u32[]{:S(2)}) collective-permute-start(f32[16,256]{1,0:T(8,128)S(1)} %get-tuple-element.102.sent), channel_id=1, source_target_pairs={{0,16},{1,2},{2,1},{3,4},{4,3},{5,6},{6,5},{7,8},{8,7},{9,10},{10,... | collective-permute-start | bytes 49160 | tf_op jit(solution)/shard_map/ppermute | solution.py:355
  54.9 4.1 %collective-permute-start.24 = (f32[24,256]{1,0:T(8,128)S(1)}, f32[24,256]{1,0:T(8,128)S(1)}, u32[]{:S(2)}, u32[]{:S(2)}) collective-permute-start(f32[24,256]{1,0:T(8,128)S(1)} %get-tuple-element.104), channel_id=1, source_target_pairs={{0,1},{1,0},{2,3},{3,2},{4,5},{5,4},{6,7},{7,6},{8,9},{9,8},{10,11... | collective-permute-start | bytes 73736 | tf_op jit(solution)/shard_map/ppermute | solution.py:356
  59.6 11.0 %collective-permute-start.26 = (f32[7,8,256]{2,1,0:T(8,128)S(1)}, f32[7,8,256]{2,1,0:T(8,128)S(1)}, u32[]{:S(2)}, u32[]{:S(2)}) collective-permute-start(f32[7,8,256]{2,1,0:T(8,128)S(1)} %get-tuple-element.109), channel_id=1, source_target_pairs={{0,1},{1,0},{2,3},{3,2},{4,5},{5,4},{6,7},{7,6},{8,9},{9,8},{10,11... | collective-permute-start | bytes 172040 | tf_op jit(solution)/shard_map/ppermute | solution.py:353
  59.7 10.9 %collective-permute-start.27 = (f32[6,8,256]{2,1,0:T(8,128)S(1)}, f32[6,8,256]{2,1,0:T(8,128)S(1)}, u32[]{:S(2)}, u32[]{:S(2)}) collective-permute-start(f32[6,8,256]{2,1,0:T(8,128)S(1)} %get-tuple-element.112), channel_id=1, source_target_pairs={{0,16},{1,17},{2,18},{3,19},{4,20},{5,21},{6,22},{7,23},{8,24},{9,... | collective-permute-start | bytes 147464 | tf_op jit(solution)/shard_map/ppermute | solution.py:354
  63.4 7.8 %collective-permute-start.25 = (f32[8,128]{1,0:T(8,128)S(1)}, f32[8,128]{1,0:T(8,128)S(1)}, u32[]{:S(2)}, u32[]{:S(2)}) collective-permute-start(f32[8,128]{1,0:T(8,128)S(1)} %get-tuple-element.108), channel_id=1, source_target_pairs={{0,240},{1,241},{2,242},{3,243},{4,244},{5,245},{6,246},{7,247},{8... | collective-permute-start | bytes 12296 | tf_op jit(solution)/shard_map/ppermute | solution.py:352
  66.5 4.2 %collective-permute-start.28 = (f32[16,256]{1,0:T(8,128)S(1)}, f32[16,256]{1,0:T(8,128)S(1)}, u32[]{:S(2)}, u32[]{:S(2)}) collective-permute-start(f32[16,256]{1,0:T(8,128)S(1)} %get-tuple-element.111.sent), channel_id=1, source_target_pairs={{0,16},{1,2},{2,1},{3,4},{4,3},{5,6},{6,5},{7,8},{8,7},{9,10},{10,... | collective-permute-start | bytes 49160 | tf_op jit(solution)/shard_map/ppermute | solution.py:355
  66.6 4.1 %collective-permute-start.29 = (f32[24,256]{1,0:T(8,128)S(1)}, f32[24,256]{1,0:T(8,128)S(1)}, u32[]{:S(2)}, u32[]{:S(2)}) collective-permute-start(f32[24,256]{1,0:T(8,128)S(1)} %get-tuple-element.113), channel_id=1, source_target_pairs={{0,1},{1,0},{2,3},{3,2},{4,5},{5,4},{6,7},{7,6},{8,9},{9,8},{10,11... | collective-permute-start | bytes 73736 | tf_op jit(solution)/shard_map/ppermute | solution.py:356
  (3 other events, 30.0 us)

commit v6 on v5

--- a/solution.py
+++ b/solution.py
@@ -251,7 +251,7 @@
     cut_ref[...] = row
     chord_odd_ref[6, :, 0:128] = row
     chord_odd_ref[0:6] = odd[...]
-    chord_even_ref[...] = even[...]
+    chord_even_ref[0:6] = even[...]
     up = product_rows(couplings, (1,), delta, 8, 128)
     down = product_rows(couplings, (0,), delta, 0, 128)
     even_chord = lax.axis_index("chord") % 2 == 0
@@ -298,7 +298,7 @@
 FIELD = (6, 16, 256)
 SLAB = (6, 8, 256)
 ROWS = (16, 256)
-FIRST = [(8, 128), (7, 8, 256), SLAB]
+FIRST = [(8, 128), (7, 8, 256), (8, 8, 256)]
 SECOND = [ROWS, (24, 256)]
 
 

time: 72.3 us -> 72.3 us (level)
  the two profiles are of different devices: /device:TPU:8 before, /device:TPU:14 now
where the time goes in v6:
time: 72.3 us; the launch traced here: 72.2 us
  starting transfers between devices  47.3 us (65%)
  waiting for transfers between devices  15.4 us (21%)
  Pallas kernels  8.28 us (11%)
  between operations  1.07 us (1%)
    ppermute x6, starting transfers between devices, exchange(): cut = lax.ppermute(cut, ('chord', 'span'), mirrors(chords, spans))  22.1 us
    ppermute x6, starting transfers between devices, exchange(): lax.ppermute(chord_odd, ('chord', 'span'), pairs(chords, spans, 'chord', 1))  16.6 us
    ppermute x6, waiting for transfers between devices, exchange(): lax.ppermute(span_odd, ('chord', 'span'), pairs(chords, spans, 'span', 1))  15.2 us
    pallas_call x24, Pallas kernels, call(): pl.pallas_call(kernel, name=name, out_shape=[space(s, F32) for s in shape...  6.74 us
    ppermute x6, starting transfers between devices, exchange(): lax.ppermute(span_even, ('chord', 'span'), pairs(chords, spans, 'span', 0))  6.7 us
    pallas_call x1, Pallas kernels, load(): pl.pallas_call(load_kernel, name='load', out_shape=[*held, *(pltpu.VMEM(s...  1.54 us
  transfers between devices with their start and end apart: 30, of which 7 were waited for; matrix products, arithmetic and copies ran while one was open for 0% of the time, Pallas kernels for 7%

profile of v6, /device:TPU:14, one launch (start us, length us, event | category | flops | bytes accessed | tf_op | source)
XLA Modules:
  0.0 72.2 jit_solution(1454302888020168958)
XLA Ops:
  0.7 1.5 %load.1 = (f32[6,16,256]{2,1,0:T(8,128)S(1)}, bf16[6,6,6,16,256]{4,3,2,1,0:T(8,128)(2,1)S(1)}, f32[8,128]{1,0:T(8,128)S(1)}, f32[7,8,256]{2,1,0:T(8,128)S(1)}, f32[8,8,256]{2,1,0:T(8,128)S(1)}) custom-call(bf16[6,6,6,16,256]{4,3,2,1,0:T(8,128)(2,1)} %bitcast.33, f32[6,16,256]{2,1,0:T(8,128)} %bitcast.34), custom_call_target="tpu_custom_call" | custom-call | flops 1000000 | tf_op jit(solution)/shard_map/load/pallas_call | solution.py:311
  2.2 0.9 %collective-permute-start.2 = (f32[8,8,256]{2,1,0:T(8,128)S(1)}, f32[8,8,256]{2,1,0:T(8,128)S(1)}, u32[]{:S(2)}, u32[]{:S(2)}) collective-permute-start(f32[8,8,256]{2,1,0:T(8,128)S(1)} %get-tuple-element.67), channel_id=1, source_target_pairs={{0,16},{1,17},{2,18},{3,19},{4,20},{5,21},{6,22},{7,23},{8,24},{9,... | collective-permute-start | bytes 196616 | tf_op jit(solution)/shard_map/ppermute | solution.py:354
  3.1 3.8 %collective-permute-start.1 = (f32[7,8,256]{2,1,0:T(8,128)S(1)}, f32[7,8,256]{2,1,0:T(8,128)S(1)}, u32[]{:S(2)}, u32[]{:S(2)}) collective-permute-start(f32[7,8,256]{2,1,0:T(8,128)S(1)} %get-tuple-element.61), channel_id=1, source_target_pairs={{0,1},{1,0},{2,3},{3,2},{4,5},{5,4},{6,7},{7,6},{8,9},{9,8},{10,11... | collective-permute-start | bytes 172040 | tf_op jit(solution)/shard_map/ppermute | solution.py:353
  7.0 6.0 %collective-permute-start = (f32[8,128]{1,0:T(8,128)S(1)}, f32[8,128]{1,0:T(8,128)S(1)}, u32[]{:S(2)}, u32[]{:S(2)}) collective-permute-start(f32[8,128]{1,0:T(8,128)S(1)} %get-tuple-element.60), channel_id=1, source_target_pairs={{0,240},{1,241},{2,242},{3,243},{4,244},{5,245},{6,246},{7,247},{8... | collective-permute-start | bytes 12296 | tf_op jit(solution)/shard_map/ppermute | solution.py:352
  13.2 1.1 %collective-permute-start.4 = (f32[24,256]{1,0:T(8,128)S(1)}, f32[24,256]{1,0:T(8,128)S(1)}, u32[]{:S(2)}, u32[]{:S(2)}) collective-permute-start(f32[24,256]{1,0:T(8,128)S(1)} %get-tuple-element.68), channel_id=1, source_target_pairs={{0,1},{1,0},{2,3},{3,2},{4,5},{5,4},{6,7},{7,6},{8,9},{9,8},{10,11... | collective-permute-start | bytes 73736 | tf_op jit(solution)/shard_map/ppermute | solution.py:356
  14.3 0.4 inside_masks.1
  14.7 2.5 %collective-permute-done.3.span_odd = f32[16,256]{1,0:T(8,128)S(1)} collective-permute-done((f32[16,256]{1,0:T(8,128)S(1)}, f32[16,256]{1,0:T(8,128)S(1)}, u32[]{:S(2)}, u32[]{:S(2)}) %collective-permute-start.3) | collective-permute-done | bytes 16416 | tf_op jit(solution)/shard_map/ppermute | solution.py:355
  17.9 2.1 %collective-permute-start.6 = (f32[7,8,256]{2,1,0:T(8,128)S(1)}, f32[7,8,256]{2,1,0:T(8,128)S(1)}, u32[]{:S(2)}, u32[]{:S(2)}) collective-permute-start(f32[7,8,256]{2,1,0:T(8,128)S(1)} %get-tuple-element.73), channel_id=1, source_target_pairs={{0,1},{1,0},{2,3},{3,2},{4,5},{5,4},{6,7},{7,6},{8,9},{9,8},{10,11... | collective-permute-start | bytes 172040 | tf_op jit(solution)/shard_map/ppermute | solution.py:353
  20.1 3.2 %collective-permute-start.5 = (f32[8,128]{1,0:T(8,128)S(1)}, f32[8,128]{1,0:T(8,128)S(1)}, u32[]{:S(2)}, u32[]{:S(2)}) collective-permute-start(f32[8,128]{1,0:T(8,128)S(1)} %get-tuple-element.72), channel_id=1, source_target_pairs={{0,240},{1,241},{2,242},{3,243},{4,244},{5,245},{6,246},{7,247},{8... | collective-permute-start | bytes 12296 | tf_op jit(solution)/shard_map/ppermute | solution.py:352
  23.5 1.1 %collective-permute-start.9 = (f32[24,256]{1,0:T(8,128)S(1)}, f32[24,256]{1,0:T(8,128)S(1)}, u32[]{:S(2)}, u32[]{:S(2)}) collective-permute-start(f32[24,256]{1,0:T(8,128)S(1)} %get-tuple-element.77), channel_id=1, source_target_pairs={{0,1},{1,0},{2,3},{3,2},{4,5},{5,4},{6,7},{7,6},{8,9},{9,8},{10,11... | collective-permute-start | bytes 73736 | tf_op jit(solution)/shard_map/ppermute | solution.py:356
  24.6 0.4 inside.5.part
  25.0 2.5 %collective-permute-done.8.span_odd = f32[16,256]{1,0:T(8,128)S(1)} collective-permute-done((f32[16,256]{1,0:T(8,128)S(1)}, f32[16,256]{1,0:T(8,128)S(1)}, u32[]{:S(2)}, u32[]{:S(2)}) %collective-permute-start.8) | collective-permute-done | bytes 16416 | tf_op jit(solution)/shard_map/ppermute | solution.py:355
  28.3 3.1 %collective-permute-start.11 = (f32[7,8,256]{2,1,0:T(8,128)S(1)}, f32[7,8,256]{2,1,0:T(8,128)S(1)}, u32[]{:S(2)}, u32[]{:S(2)}) collective-permute-start(f32[7,8,256]{2,1,0:T(8,128)S(1)} %get-tuple-element.82), channel_id=1, source_target_pairs={{0,1},{1,0},{2,3},{3,2},{4,5},{5,4},{6,7},{7,6},{8,9},{9,8},{10,11... | collective-permute-start | bytes 172040 | tf_op jit(solution)/shard_map/ppermute | solution.py:353
  31.3 3.2 %collective-permute-start.10 = (f32[8,128]{1,0:T(8,128)S(1)}, f32[8,128]{1,0:T(8,128)S(1)}, u32[]{:S(2)}, u32[]{:S(2)}) collective-permute-start(f32[8,128]{1,0:T(8,128)S(1)} %get-tuple-element.81), channel_id=1, source_target_pairs={{0,240},{1,241},{2,242},{3,243},{4,244},{5,245},{6,246},{7,247},{8... | collective-permute-start | bytes 12296 | tf_op jit(solution)/shard_map/ppermute | solution.py:352
  34.8 1.1 %collective-permute-start.14 = (f32[24,256]{1,0:T(8,128)S(1)}, f32[24,256]{1,0:T(8,128)S(1)}, u32[]{:S(2)}, u32[]{:S(2)}) collective-permute-start(f32[24,256]{1,0:T(8,128)S(1)} %get-tuple-element.86), channel_id=1, source_target_pairs={{0,1},{1,0},{2,3},{3,2},{4,5},{5,4},{6,7},{7,6},{8,9},{9,8},{10,11... | collective-permute-start | bytes 73736 | tf_op jit(solution)/shard_map/ppermute | solution.py:356
  35.9 0.4 inside.6.part
  36.3 2.5 %collective-permute-done.13.span_odd = f32[16,256]{1,0:T(8,128)S(1)} collective-permute-done((f32[16,256]{1,0:T(8,128)S(1)}, f32[16,256]{1,0:T(8,128)S(1)}, u32[]{:S(2)}, u32[]{:S(2)}) %collective-permute-start.13) | collective-permute-done | bytes 16416 | tf_op jit(solution)/shard_map/ppermute | solution.py:355
  39.5 2.3 %collective-permute-start.16 = (f32[7,8,256]{2,1,0:T(8,128)S(1)}, f32[7,8,256]{2,1,0:T(8,128)S(1)}, u32[]{:S(2)}, u32[]{:S(2)}) collective-permute-start(f32[7,8,256]{2,1,0:T(8,128)S(1)} %get-tuple-element.91), channel_id=1, source_target_pairs={{0,1},{1,0},{2,3},{3,2},{4,5},{5,4},{6,7},{7,6},{8,9},{9,8},{10,11... | collective-permute-start | bytes 172040 | tf_op jit(solution)/shard_map/ppermute | solution.py:353
  41.8 3.2 %collective-permute-start.15 = (f32[8,128]{1,0:T(8,128)S(1)}, f32[8,128]{1,0:T(8,128)S(1)}, u32[]{:S(2)}, u32[]{:S(2)}) collective-permute-start(f32[8,128]{1,0:T(8,128)S(1)} %get-tuple-element.90), channel_id=1, source_target_pairs={{0,240},{1,241},{2,242},{3,243},{4,244},{5,245},{6,246},{7,247},{8... | collective-permute-start | bytes 12296 | tf_op jit(solution)/shard_map/ppermute | solution.py:352
  45.2 1.1 %collective-permute-start.19 = (f32[24,256]{1,0:T(8,128)S(1)}, f32[24,256]{1,0:T(8,128)S(1)}, u32[]{:S(2)}, u32[]{:S(2)}) collective-permute-start(f32[24,256]{1,0:T(8,128)S(1)} %get-tuple-element.95), channel_id=1, source_target_pairs={{0,1},{1,0},{2,3},{3,2},{4,5},{5,4},{6,7},{7,6},{8,9},{9,8},{10,11... | collective-permute-start | bytes 73736 | tf_op jit(solution)/shard_map/ppermute | solution.py:356
  46.4 0.4 inside.7.part
  46.8 2.5 %collective-permute-done.18.span_odd = f32[16,256]{1,0:T(8,128)S(1)} collective-permute-done((f32[16,256]{1,0:T(8,128)S(1)}, f32[16,256]{1,0:T(8,128)S(1)}, u32[]{:S(2)}, u32[]{:S(2)}) %collective-permute-start.18) | collective-permute-done | bytes 16416 | tf_op jit(solution)/shard_map/ppermute | solution.py:355
  50.0 3.1 %collective-permute-start.21 = (f32[7,8,256]{2,1,0:T(8,128)S(1)}, f32[7,8,256]{2,1,0:T(8,128)S(1)}, u32[]{:S(2)}, u32[]{:S(2)}) collective-permute-start(f32[7,8,256]{2,1,0:T(8,128)S(1)} %get-tuple-element.100), channel_id=1, source_target_pairs={{0,1},{1,0},{2,3},{3,2},{4,5},{5,4},{6,7},{7,6},{8,9},{9,8},{10,11... | collective-permute-start | bytes 172040 | tf_op jit(solution)/shard_map/ppermute | solution.py:353
  53.1 3.2 %collective-permute-start.20 = (f32[8,128]{1,0:T(8,128)S(1)}, f32[8,128]{1,0:T(8,128)S(1)}, u32[]{:S(2)}, u32[]{:S(2)}) collective-permute-start(f32[8,128]{1,0:T(8,128)S(1)} %get-tuple-element.99), channel_id=1, source_target_pairs={{0,240},{1,241},{2,242},{3,243},{4,244},{5,245},{6,246},{7,247},{8... | collective-permute-start | bytes 12296 | tf_op jit(solution)/shard_map/ppermute | solution.py:352
  56.5 1.1 %collective-permute-start.24 = (f32[24,256]{1,0:T(8,128)S(1)}, f32[24,256]{1,0:T(8,128)S(1)}, u32[]{:S(2)}, u32[]{:S(2)}) collective-permute-start(f32[24,256]{1,0:T(8,128)S(1)} %get-tuple-element.104), channel_id=1, source_target_pairs={{0,1},{1,0},{2,3},{3,2},{4,5},{5,4},{6,7},{7,6},{8,9},{9,8},{10,11... | collective-permute-start | bytes 73736 | tf_op jit(solution)/shard_map/ppermute | solution.py:356
  57.6 0.4 inside.8.part
  58.0 2.5 %collective-permute-done.23.span_odd = f32[16,256]{1,0:T(8,128)S(1)} collective-permute-done((f32[16,256]{1,0:T(8,128)S(1)}, f32[16,256]{1,0:T(8,128)S(1)}, u32[]{:S(2)}, u32[]{:S(2)}) %collective-permute-start.23) | collective-permute-done | bytes 16416 | tf_op jit(solution)/shard_map/ppermute | solution.py:355
  61.2 2.1 %collective-permute-start.26 = (f32[7,8,256]{2,1,0:T(8,128)S(1)}, f32[7,8,256]{2,1,0:T(8,128)S(1)}, u32[]{:S(2)}, u32[]{:S(2)}) collective-permute-start(f32[7,8,256]{2,1,0:T(8,128)S(1)} %get-tuple-element.109), channel_id=1, source_target_pairs={{0,1},{1,0},{2,3},{3,2},{4,5},{5,4},{6,7},{7,6},{8,9},{9,8},{10,11... | collective-permute-start | bytes 172040 | tf_op jit(solution)/shard_map/ppermute | solution.py:353
  63.4 3.2 %collective-permute-start.25 = (f32[8,128]{1,0:T(8,128)S(1)}, f32[8,128]{1,0:T(8,128)S(1)}, u32[]{:S(2)}, u32[]{:S(2)}) collective-permute-start(f32[8,128]{1,0:T(8,128)S(1)} %get-tuple-element.108), channel_id=1, source_target_pairs={{0,240},{1,241},{2,242},{3,243},{4,244},{5,245},{6,246},{7,247},{8... | collective-permute-start | bytes 12296 | tf_op jit(solution)/shard_map/ppermute | solution.py:352
  66.8 1.1 %collective-permute-start.29 = (f32[24,256]{1,0:T(8,128)S(1)}, f32[24,256]{1,0:T(8,128)S(1)}, u32[]{:S(2)}, u32[]{:S(2)}) collective-permute-start(f32[24,256]{1,0:T(8,128)S(1)} %get-tuple-element.113), channel_id=1, source_target_pairs={{0,1},{1,0},{2,3},{3,2},{4,5},{5,4},{6,7},{7,6},{8,9},{9,8},{10,11... | collective-permute-start | bytes 73736 | tf_op jit(solution)/shard_map/ppermute | solution.py:356
  68.3 2.5 %collective-permute-done.28.span_odd = f32[16,256]{1,0:T(8,128)S(1)} collective-permute-done((f32[16,256]{1,0:T(8,128)S(1)}, f32[16,256]{1,0:T(8,128)S(1)}, u32[]{:S(2)}, u32[]{:S(2)}) %collective-permute-start.28) | collective-permute-done | bytes 16416 | tf_op jit(solution)/shard_map/ppermute | solution.py:355
  71.2 0.8 %last.1 = (f32[6,16,256]{2,1,0:T(8,128)}, f32[6,16,256]{2,1,0:T(8,128)}) custom-call(f32[8,128]{1,0:T(8,128)S(1)} %collective-permute-done.25.cut, f32[7,8,256]{2,1,0:T(8,128)S(1)} %collective-permute-done.26.chord_odd, f32[3,16,128]{2,1,0:T(8,128)S(1)} %get-tuple-element.65.masks, bf16[6,6,2,16,256]{4,3,2,1,0:T(8,128)(2,1)S(1)} %bitcast.19, ...), custom_call_target="tpu_custom_call" | custom-call | flops 1000 | tf_op jit(solution)/shard_map/last/pallas_call | solution.py:286
  (63 shorter events, 5.2 us)
Async XLA Ops:
  0.6 13.7 %copy-start.1 = (bf16[6,6,2,8,256]{4,3,2,1,0:T(8,128)(2,1)S(1)}, bf16[6,6,2,8,256]{4,3,2,1,0:T(8,128)(2,1)}, u32[]{:S(2)}) copy-start(bf16[6,6,2,8,256]{4,3,2,1,0:T(8,128)(2,1)} %param.9) | copy-start | bytes 884740
  0.6 13.7 %copy-start.2 = (f32[6,2,8,256]{3,2,1,0:T(8,128)S(1)}, f32[6,2,8,256]{3,2,1,0:T(8,128)}, u32[]{:S(2)}) copy-start(f32[6,2,8,256]{3,2,1,0:T(8,128)} %param.8) | copy-start | bytes 294916
  2.2 15.0 %collective-permute-start.2 = (f32[8,8,256]{2,1,0:T(8,128)S(1)}, f32[8,8,256]{2,1,0:T(8,128)S(1)}, u32[]{:S(2)}, u32[]{:S(2)}) collective-permute-start(f32[8,8,256]{2,1,0:T(8,128)S(1)} %get-tuple-element.67), channel_id=1, source_target_pairs={{0,16},{1,17},{2,18},{3,19},{4,20},{5,21},{6,22},{7,23},{8,24},{9,... | collective-permute-start | bytes 196616 | tf_op jit(solution)/shard_map/ppermute | solution.py:354
  3.1 14.1 %collective-permute-start.1 = (f32[7,8,256]{2,1,0:T(8,128)S(1)}, f32[7,8,256]{2,1,0:T(8,128)S(1)}, u32[]{:S(2)}, u32[]{:S(2)}) collective-permute-start(f32[7,8,256]{2,1,0:T(8,128)S(1)} %get-tuple-element.61), channel_id=1, source_target_pairs={{0,1},{1,0},{2,3},{3,2},{4,5},{5,4},{6,7},{7,6},{8,9},{9,8},{10,11... | collective-permute-start | bytes 172040 | tf_op jit(solution)/shard_map/ppermute | solution.py:353
  7.0 10.6 %collective-permute-start = (f32[8,128]{1,0:T(8,128)S(1)}, f32[8,128]{1,0:T(8,128)S(1)}, u32[]{:S(2)}, u32[]{:S(2)}) collective-permute-start(f32[8,128]{1,0:T(8,128)S(1)} %get-tuple-element.60), channel_id=1, source_target_pairs={{0,240},{1,241},{2,242},{3,243},{4,244},{5,245},{6,246},{7,247},{8... | collective-permute-start | bytes 12296 | tf_op jit(solution)/shard_map/ppermute | solution.py:352
  13.1 4.2 %collective-permute-start.3 = (f32[16,256]{1,0:T(8,128)S(1)}, f32[16,256]{1,0:T(8,128)S(1)}, u32[]{:S(2)}, u32[]{:S(2)}) collective-permute-start(f32[16,256]{1,0:T(8,128)S(1)} %get-tuple-element.64.sent), channel_id=1, source_target_pairs={{0,16},{1,2},{2,1},{3,4},{4,3},{5,6},{6,5},{7,8},{8,7},{9,10},{10,... | collective-permute-start | bytes 49160 | tf_op jit(solution)/shard_map/ppermute | solution.py:355
  13.2 4.1 %collective-permute-start.4 = (f32[24,256]{1,0:T(8,128)S(1)}, f32[24,256]{1,0:T(8,128)S(1)}, u32[]{:S(2)}, u32[]{:S(2)}) collective-permute-start(f32[24,256]{1,0:T(8,128)S(1)} %get-tuple-element.68), channel_id=1, source_target_pairs={{0,1},{1,0},{2,3},{3,2},{4,5},{5,4},{6,7},{7,6},{8,9},{9,8},{10,11... | collective-permute-start | bytes 73736 | tf_op jit(solution)/shard_map/ppermute | solution.py:356
  17.8 9.7 %collective-permute-start.7 = (f32[8,8,256]{2,1,0:T(8,128)S(1)}, f32[8,8,256]{2,1,0:T(8,128)S(1)}, u32[]{:S(2)}, u32[]{:S(2)}) collective-permute-start(f32[8,8,256]{2,1,0:T(8,128)S(1)} %get-tuple-element.76), channel_id=1, source_target_pairs={{0,16},{1,17},{2,18},{3,19},{4,20},{5,21},{6,22},{7,23},{8,24},{9,... | collective-permute-start | bytes 196616 | tf_op jit(solution)/shard_map/ppermute | solution.py:354
  17.9 9.6 %collective-permute-start.6 = (f32[7,8,256]{2,1,0:T(8,128)S(1)}, f32[7,8,256]{2,1,0:T(8,128)S(1)}, u32[]{:S(2)}, u32[]{:S(2)}) collective-permute-start(f32[7,8,256]{2,1,0:T(8,128)S(1)} %get-tuple-element.73), channel_id=1, source_target_pairs={{0,1},{1,0},{2,3},{3,2},{4,5},{5,4},{6,7},{7,6},{8,9},{9,8},{10,11... | collective-permute-start | bytes 172040 | tf_op jit(solution)/shard_map/ppermute | solution.py:353
  20.1 7.8 %collective-permute-start.5 = (f32[8,128]{1,0:T(8,128)S(1)}, f32[8,128]{1,0:T(8,128)S(1)}, u32[]{:S(2)}, u32[]{:S(2)}) collective-permute-start(f32[8,128]{1,0:T(8,128)S(1)} %get-tuple-element.72), channel_id=1, source_target_pairs={{0,240},{1,241},{2,242},{3,243},{4,244},{5,245},{6,246},{7,247},{8... | collective-permute-start | bytes 12296 | tf_op jit(solution)/shard_map/ppermute | solution.py:352
  23.4 4.2 %collective-permute-start.8 = (f32[16,256]{1,0:T(8,128)S(1)}, f32[16,256]{1,0:T(8,128)S(1)}, u32[]{:S(2)}, u32[]{:S(2)}) collective-permute-start(f32[16,256]{1,0:T(8,128)S(1)} %get-tuple-element.75.sent), channel_id=1, source_target_pairs={{0,16},{1,2},{2,1},{3,4},{4,3},{5,6},{6,5},{7,8},{8,7},{9,10},{10,... | collective-permute-start | bytes 49160 | tf_op jit(solution)/shard_map/ppermute | solution.py:355
  23.5 4.1 %collective-permute-start.9 = (f32[24,256]{1,0:T(8,128)S(1)}, f32[24,256]{1,0:T(8,128)S(1)}, u32[]{:S(2)}, u32[]{:S(2)}) collective-permute-start(f32[24,256]{1,0:T(8,128)S(1)} %get-tuple-element.77), channel_id=1, source_target_pairs={{0,1},{1,0},{2,3},{3,2},{4,5},{5,4},{6,7},{7,6},{8,9},{9,8},{10,11... | collective-permute-start | bytes 73736 | tf_op jit(solution)/shard_map/ppermute | solution.py:356
  28.2 10.7 %collective-permute-start.12 = (f32[8,8,256]{2,1,0:T(8,128)S(1)}, f32[8,8,256]{2,1,0:T(8,128)S(1)}, u32[]{:S(2)}, u32[]{:S(2)}) collective-permute-start(f32[8,8,256]{2,1,0:T(8,128)S(1)} %get-tuple-element.85), channel_id=1, source_target_pairs={{0,16},{1,17},{2,18},{3,19},{4,20},{5,21},{6,22},{7,23},{8,24},{9,... | collective-permute-start | bytes 196616 | tf_op jit(solution)/shard_map/ppermute | solution.py:354
  28.3 10.6 %collective-permute-start.11 = (f32[7,8,256]{2,1,0:T(8,128)S(1)}, f32[7,8,256]{2,1,0:T(8,128)S(1)}, u32[]{:S(2)}, u32[]{:S(2)}) collective-permute-start(f32[7,8,256]{2,1,0:T(8,128)S(1)} %get-tuple-element.82), channel_id=1, source_target_pairs={{0,1},{1,0},{2,3},{3,2},{4,5},{5,4},{6,7},{7,6},{8,9},{9,8},{10,11... | collective-permute-start | bytes 172040 | tf_op jit(solution)/shard_map/ppermute | solution.py:353
  31.3 7.8 %collective-permute-start.10 = (f32[8,128]{1,0:T(8,128)S(1)}, f32[8,128]{1,0:T(8,128)S(1)}, u32[]{:S(2)}, u32[]{:S(2)}) collective-permute-start(f32[8,128]{1,0:T(8,128)S(1)} %get-tuple-element.81), channel_id=1, source_target_pairs={{0,240},{1,241},{2,242},{3,243},{4,244},{5,245},{6,246},{7,247},{8... | collective-permute-start | bytes 12296 | tf_op jit(solution)/shard_map/ppermute | solution.py:352
  34.7 4.2 %collective-permute-start.13 = (f32[16,256]{1,0:T(8,128)S(1)}, f32[16,256]{1,0:T(8,128)S(1)}, u32[]{:S(2)}, u32[]{:S(2)}) collective-permute-start(f32[16,256]{1,0:T(8,128)S(1)} %get-tuple-element.84.sent), channel_id=1, source_target_pairs={{0,16},{1,2},{2,1},{3,4},{4,3},{5,6},{6,5},{7,8},{8,7},{9,10},{10,... | collective-permute-start | bytes 49160 | tf_op jit(solution)/shard_map/ppermute | solution.py:355
  34.8 4.1 %collective-permute-start.14 = (f32[24,256]{1,0:T(8,128)S(1)}, f32[24,256]{1,0:T(8,128)S(1)}, u32[]{:S(2)}, u32[]{:S(2)}) collective-permute-start(f32[24,256]{1,0:T(8,128)S(1)} %get-tuple-element.86), channel_id=1, source_target_pairs={{0,1},{1,0},{2,3},{3,2},{4,5},{5,4},{6,7},{7,6},{8,9},{9,8},{10,11... | collective-permute-start | bytes 73736 | tf_op jit(solution)/shard_map/ppermute | solution.py:356
  39.4 9.9 %collective-permute-start.17 = (f32[8,8,256]{2,1,0:T(8,128)S(1)}, f32[8,8,256]{2,1,0:T(8,128)S(1)}, u32[]{:S(2)}, u32[]{:S(2)}) collective-permute-start(f32[8,8,256]{2,1,0:T(8,128)S(1)} %get-tuple-element.94), channel_id=1, source_target_pairs={{0,16},{1,17},{2,18},{3,19},{4,20},{5,21},{6,22},{7,23},{8,24},{9,... | collective-permute-start | bytes 196616 | tf_op jit(solution)/shard_map/ppermute | solution.py:354
  39.5 9.8 %collective-permute-start.16 = (f32[7,8,256]{2,1,0:T(8,128)S(1)}, f32[7,8,256]{2,1,0:T(8,128)S(1)}, u32[]{:S(2)}, u32[]{:S(2)}) collective-permute-start(f32[7,8,256]{2,1,0:T(8,128)S(1)} %get-tuple-element.91), channel_id=1, source_target_pairs={{0,1},{1,0},{2,3},{3,2},{4,5},{5,4},{6,7},{7,6},{8,9},{9,8},{10,11... | collective-permute-start | bytes 172040 | tf_op jit(solution)/shard_map/ppermute | solution.py:353
  41.8 7.8 %collective-permute-start.15 = (f32[8,128]{1,0:T(8,128)S(1)}, f32[8,128]{1,0:T(8,128)S(1)}, u32[]{:S(2)}, u32[]{:S(2)}) collective-permute-start(f32[8,128]{1,0:T(8,128)S(1)} %get-tuple-element.90), channel_id=1, source_target_pairs={{0,240},{1,241},{2,242},{3,243},{4,244},{5,245},{6,246},{7,247},{8... | collective-permute-start | bytes 12296 | tf_op jit(solution)/shard_map/ppermute | solution.py:352
  45.1 4.2 %collective-permute-start.18 = (f32[16,256]{1,0:T(8,128)S(1)}, f32[16,256]{1,0:T(8,128)S(1)}, u32[]{:S(2)}, u32[]{:S(2)}) collective-permute-start(f32[16,256]{1,0:T(8,128)S(1)} %get-tuple-element.93.sent), channel_id=1, source_target_pairs={{0,16},{1,2},{2,1},{3,4},{4,3},{5,6},{6,5},{7,8},{8,7},{9,10},{10,... | collective-permute-start | bytes 49160 | tf_op jit(solution)/shard_map/ppermute | solution.py:355
  45.2 4.1 %collective-permute-start.19 = (f32[24,256]{1,0:T(8,128)S(1)}, f32[24,256]{1,0:T(8,128)S(1)}, u32[]{:S(2)}, u32[]{:S(2)}) collective-permute-start(f32[24,256]{1,0:T(8,128)S(1)} %get-tuple-element.95), channel_id=1, source_target_pairs={{0,1},{1,0},{2,3},{3,2},{4,5},{5,4},{6,7},{7,6},{8,9},{9,8},{10,11... | collective-permute-start | bytes 73736 | tf_op jit(solution)/shard_map/ppermute | solution.py:356
  49.9 10.7 %collective-permute-start.22 = (f32[8,8,256]{2,1,0:T(8,128)S(1)}, f32[8,8,256]{2,1,0:T(8,128)S(1)}, u32[]{:S(2)}, u32[]{:S(2)}) collective-permute-start(f32[8,8,256]{2,1,0:T(8,128)S(1)} %get-tuple-element.103), channel_id=1, source_target_pairs={{0,16},{1,17},{2,18},{3,19},{4,20},{5,21},{6,22},{7,23},{8,24},{9,... | collective-permute-start | bytes 196616 | tf_op jit(solution)/shard_map/ppermute | solution.py:354
  50.0 10.6 %collective-permute-start.21 = (f32[7,8,256]{2,1,0:T(8,128)S(1)}, f32[7,8,256]{2,1,0:T(8,128)S(1)}, u32[]{:S(2)}, u32[]{:S(2)}) collective-permute-start(f32[7,8,256]{2,1,0:T(8,128)S(1)} %get-tuple-element.100), channel_id=1, source_target_pairs={{0,1},{1,0},{2,3},{3,2},{4,5},{5,4},{6,7},{7,6},{8,9},{9,8},{10,11... | collective-permute-start | bytes 172040 | tf_op jit(solution)/shard_map/ppermute | solution.py:353
  53.1 7.8 %collective-permute-start.20 = (f32[8,128]{1,0:T(8,128)S(1)}, f32[8,128]{1,0:T(8,128)S(1)}, u32[]{:S(2)}, u32[]{:S(2)}) collective-permute-start(f32[8,128]{1,0:T(8,128)S(1)} %get-tuple-element.99), channel_id=1, source_target_pairs={{0,240},{1,241},{2,242},{3,243},{4,244},{5,245},{6,246},{7,247},{8... | collective-permute-start | bytes 12296 | tf_op jit(solution)/shard_map/ppermute | solution.py:352
  56.4 4.2 %collective-permute-start.23 = (f32[16,256]{1,0:T(8,128)S(1)}, f32[16,256]{1,0:T(8,128)S(1)}, u32[]{:S(2)}, u32[]{:S(2)}) collective-permute-start(f32[16,256]{1,0:T(8,128)S(1)} %get-tuple-element.102.sent), channel_id=1, source_target_pairs={{0,16},{1,2},{2,1},{3,4},{4,3},{5,6},{6,5},{7,8},{8,7},{9,10},{10,... | collective-permute-start | bytes 49160 | tf_op jit(solution)/shard_map/ppermute | solution.py:355
  56.5 4.1 %collective-permute-start.24 = (f32[24,256]{1,0:T(8,128)S(1)}, f32[24,256]{1,0:T(8,128)S(1)}, u32[]{:S(2)}, u32[]{:S(2)}) collective-permute-start(f32[24,256]{1,0:T(8,128)S(1)} %get-tuple-element.104), channel_id=1, source_target_pairs={{0,1},{1,0},{2,3},{3,2},{4,5},{5,4},{6,7},{7,6},{8,9},{9,8},{10,11... | collective-permute-start | bytes 73736 | tf_op jit(solution)/shard_map/ppermute | solution.py:356
  61.1 9.7 %collective-permute-start.27 = (f32[8,8,256]{2,1,0:T(8,128)S(1)}, f32[8,8,256]{2,1,0:T(8,128)S(1)}, u32[]{:S(2)}, u32[]{:S(2)}) collective-permute-start(f32[8,8,256]{2,1,0:T(8,128)S(1)} %get-tuple-element.112), channel_id=1, source_target_pairs={{0,16},{1,17},{2,18},{3,19},{4,20},{5,21},{6,22},{7,23},{8,24},{9,... | collective-permute-start | bytes 196616 | tf_op jit(solution)/shard_map/ppermute | solution.py:354
  61.2 9.6 %collective-permute-start.26 = (f32[7,8,256]{2,1,0:T(8,128)S(1)}, f32[7,8,256]{2,1,0:T(8,128)S(1)}, u32[]{:S(2)}, u32[]{:S(2)}) collective-permute-start(f32[7,8,256]{2,1,0:T(8,128)S(1)} %get-tuple-element.109), channel_id=1, source_target_pairs={{0,1},{1,0},{2,3},{3,2},{4,5},{5,4},{6,7},{7,6},{8,9},{9,8},{10,11... | collective-permute-start | bytes 172040 | tf_op jit(solution)/shard_map/ppermute | solution.py:353
  63.4 7.8 %collective-permute-start.25 = (f32[8,128]{1,0:T(8,128)S(1)}, f32[8,128]{1,0:T(8,128)S(1)}, u32[]{:S(2)}, u32[]{:S(2)}) collective-permute-start(f32[8,128]{1,0:T(8,128)S(1)} %get-tuple-element.108), channel_id=1, source_target_pairs={{0,240},{1,241},{2,242},{3,243},{4,244},{5,245},{6,246},{7,247},{8... | collective-permute-start | bytes 12296 | tf_op jit(solution)/shard_map/ppermute | solution.py:352
  66.7 4.2 %collective-permute-start.28 = (f32[16,256]{1,0:T(8,128)S(1)}, f32[16,256]{1,0:T(8,128)S(1)}, u32[]{:S(2)}, u32[]{:S(2)}) collective-permute-start(f32[16,256]{1,0:T(8,128)S(1)} %get-tuple-element.111.sent), channel_id=1, source_target_pairs={{0,16},{1,2},{2,1},{3,4},{4,3},{5,6},{6,5},{7,8},{8,7},{9,10},{10,... | collective-permute-start | bytes 49160 | tf_op jit(solution)/shard_map/ppermute | solution.py:355
  66.8 4.1 %collective-permute-start.29 = (f32[24,256]{1,0:T(8,128)S(1)}, f32[24,256]{1,0:T(8,128)S(1)}, u32[]{:S(2)}, u32[]{:S(2)}) collective-permute-start(f32[24,256]{1,0:T(8,128)S(1)} %get-tuple-element.113), channel_id=1, source_target_pairs={{0,1},{1,0},{2,3},{3,2},{4,5},{5,4},{6,7},{7,6},{8,9},{9,8},{10,11... | collective-permute-start | bytes 73736 | tf_op jit(solution)/shard_map/ppermute | solution.py:356
  (3 other events, 31.6 us)
